TPU v7x, 32 devices: a whole 2x2x4 slice. The times are simulated.
32 devices in a mesh: cd: 4 (over y, x), ab: 8 (over z, core).
Axes of the slice: x: 2, y: 2, z: 4, core: 2. Of those that a mesh axis runs over, the one named last changes fastest.
Arguments:
- amplitudes: float32 [2048, 16384], P('ab', 'cd'), may hold values from -6 to 6
- amp_tiles: int32 [16, 16], P('ab', 'cd'), may hold values 0 or 1
- integrals: float32 [16384, 16384], P('cd', 'ab'), may hold values from -0.046875 to 0.046875
- int_tiles: int32 [16, 16], P('cd', 'ab'), may hold values 0 or 1
- owner_tiles: int32 [16], replicated, may hold values from 0 to 15, each once
- other_terms: float32 [2048, 16384], P('cd', 'ab'), may hold values from -6 to 6
- denominators: float32 [2048, 16384], P('cd', 'ab'), may hold values from -4 to -0.5
Outputs:
- update: float32 [2048, 16384], P('cd', 'ab')
Inputs may be any that keep to these rules, and one draw needn't show every extreme that they name: owner_tiles is a permutation of the row tiles.
All inputs are finite; a program needn't handle non-finite values. No bound on the sum of `amp_tiles` or of `int_tiles` on one device may be relied on, other than what follows from the above.
Results may differ from a plain program's by a relative error of at most 0.00013.
Values sent between devices are 32-bit elements; how exact they have to be, the bound alone decides.
No kernel may reach another device: no remote copies, remote signals or barrier semaphores. Data moves between devices by JAX's collectives and lax.ppermute only.
A program may use at most 256 MiB of HBM per device.

v0:
```python
import jax
import jax.numpy as jnp
from jax import lax
from jax.sharding import PartitionSpec as P

TILE = 1024
TILE_ROWS = 128


def spread_tiles(tile_flags, row_span, col_span):
    tile_rows, tile_cols = tile_flags.shape
    values = tile_flags.astype(jnp.float32)
    return jnp.broadcast_to(
        values[:, None, :, None], (tile_rows, row_span, tile_cols, col_span)
    ).reshape(tile_rows * row_span, tile_cols * col_span)


def on_device(amplitudes, amp_tiles, integrals, int_tiles, owner_tiles, other_terms, denominators):
    masked_ints = integrals * spread_tiles(int_tiles, TILE, TILE)
    masked_amps = amplitudes * spread_tiles(amp_tiles, TILE_ROWS, TILE)
    tile_count = owner_tiles.shape[0]
    gathered = lax.all_gather(masked_amps, "ab", axis=0, tiled=True)
    partial_value = jnp.dot(
        gathered, masked_ints, precision=lax.Precision.HIGHEST, preferred_element_type=jnp.float32
    )
    col_width = partial_value.shape[1]
    partial_value = partial_value.reshape(tile_count, TILE_ROWS, col_width)[owner_tiles].reshape(
        tile_count * TILE_ROWS, col_width
    )
    owned = lax.psum_scatter(partial_value, "cd", scatter_dimension=0, tiled=True)
    return (owned + other_terms) / denominators


def solution(mesh):
    return jax.shard_map(
        on_device,
        mesh=mesh,
        in_specs=(
            P("ab", "cd"),
            P("ab", "cd"),
            P("cd", "ab"),
            P("cd", "ab"),
            P(),
            P("cd", "ab"),
            P("cd", "ab"),
        ),
        out_specs=P("cd", "ab"),
        check_vma=False,
    )
```

profile of v0, /device:TPU:0, one launch (start us, length us, event | category | flops | bytes accessed | tf_op | source)
XLA Modules:
  0.0 716.1 jit_solution(2114166275794045669)
XLA Ops:
  6.5 0.0 copy-start
  6.5 0.0 all-gather.2.cloned.1.call-start
  6.5 0.7 convert_element_type.6
  7.2 1.1 broadcast_in_dim.6
  8.3 3.8 copy.9
  12.1 4.8 mul.6
  16.9 0.0 all-gather.2.cloned.1.call-update
  16.9 0.0 reduce-scatter.2.cloned.1.call-start
  17.0 0.0 copy-done
  17.0 0.1 copy.8
  17.1 13.2 %broadcast_in_dim.7 = f32[4,1024,2,1024]{3,2,1,0:T(2,128)} broadcast(f32[4,2]{1,0:T(4,128)S(1)} %copy.8), dimensions={0,2} | broadcast | bytes 33554464 | tf_op jit(solution)/shard_map/broadcast_in_dim | solution.py:13
  30.3 0.0 copy-start.1
  30.3 31.3 %copy.10 = f32[512,8,2,1024]{3,1,2,0:T(8,128)} copy(f32[512,8,2,1024]{3,2,1,0:T(2,128)} %bitcast.10) | data formatting | bytes 67108864
  61.6 0.0 copy-done.1
  61.6 246.8 %all-gather.2.cloned.1.call-done = f32[2048,4096]{1,0:T(8,128)} async-done(((f32[256,4096]{1,0:T(8,128)}), f32[2048,4096]{1,0:T(8,128)}) %all-gather.2.cloned.1.call-update) | async-done | bytes 33554448 | tf_op jit(solution)/shard_map/all_gather | solution.py:22
  308.4 226.3 %fusion = f32[2048,2048]{1,0:T(8,128)} fusion(f32[2048,4096]{1,0:T(8,128)} %all-gather.2.cloned.1.call-done, f32[4096,2048]{1,0:T(8,128)} %param.9, f32[4096,2048]{1,0:T(8,128)} %bitcast.12), kind=kOutput, calls=%fused_computation.1 | convolution fusion | flops 206166818816 | bytes 117440512 | tf_op jit(solution)/shard_map/dot_general | solution.py:23
  534.8 13.8 %gather_fusion = f32[16,128,2048]{2,1,0:T(8,128)} fusion(f32[16,128,2048]{2,1,0:T(8,128)} %bitcast.14, s32[1024]{0:T(1024)S(1)} %pad_clamp_fusion), kind=kCustom, calls=%fused_computation | custom fusion | bytes 33554496 | tf_op jit(solution)/shard_map/gather | solution.py:27
  548.6 0.0 reduce-scatter.2.cloned.1.call-update
  548.6 152.2 %reduce-scatter.2.cloned.1.call-done = f32[512,2048]{1,0:T(8,128)} async-done(((f32[2048,2048]{1,0:T(8,128)}), f32[512,2048]{1,0:T(8,128)}) %reduce-scatter.2.cloned.1.call-update) | async-done | bytes 4194320 | tf_op jit(solution)/shard_map/reduce_scatter | solution.py:30
  700.8 8.4 %add_divide_fusion = f32[512,2048]{1,0:T(8,128)} fusion(f32[512,2048]{1,0:T(8,128)} %param.13, f32[512,2048]{1,0:T(8,128)} %reduce-scatter.2.cloned.1.call-done, f32[512,2048]{1,0:T(8,128)} %param.12), kind=kLoop, calls=%fused_computation.3 | loop fusion | flops 2097152 | bytes 16777216 | tf_op jit(solution)/shard_map/div | solution.py:31
  (3 shorter events, 0.0 us)
Async XLA Ops:
  6.5 10.5 %copy-start = (s32[4,2]{0,1:T(2,128)S(1)}, s32[4,2]{0,1:T(2,128)}, u32[]{:S(2)}) copy-start(s32[4,2]{0,1:T(2,128)} %param.10) | copy-start | bytes 100
  6.5 301.9 %all-gather.2.cloned.1.call-start = ((), (), s32[]{:S(2)}) async-start(), calls=%async_computation.1 | async-start | bytes 37748736 | tf_op jit(solution)/shard_map/all_gather | solution.py:22
  16.9 683.9 %reduce-scatter.2.cloned.1.call-start = ((), (), s32[]{:S(2)}) async-start(), calls=%async_computation.2 | async-start | bytes 20971520 | tf_op jit(solution)/shard_map/reduce_scatter | solution.py:30
  30.3 31.3 %copy-start.1 = (s32[16]{0:T(128)S(1)}, s32[16]{0:T(128)}, u32[]{:S(2)}) copy-start(s32[16]{0:T(128)} %param.11) | copy-start | bytes 196
Sparse Core Ops, SparseCore 0:
  17.1 291.3 all-gather.1
  548.8 152.0 reduce-scatter.1
where the time goes:
time: 716 us
  waiting for transfers between devices  399 us (56%)
  matrix products  226 us (32%)
  local copies, waits for them, and re-layouts  63.4 us (9%)
  other arithmetic  13.9 us (2%)
  between operations  13.4 us (2%)
    all_gather x1, waiting for transfers between devices, on_device(): gathered = lax.all_gather(masked_amps, 'ab', axis=0, tiled=True)  247 us
    dot_general x1, matrix products, on_device(): jnp.dot(gathered, masked_ints, precision=lax.Precision.HIGHEST, preferred...  226 us
    reduce_scatter x1, waiting for transfers between devices, on_device(): lax.psum_scatter(partial_value, 'cd', scatter_dimension=0, tiled=True)  152 us
    unnamed x6, local copies, waits for them, and re-layouts  35.1 us
  transfers between devices with their start and end apart: 2, of which 2 were waited for; matrix products, arithmetic and copies ran while one was open for 6% of the time, Pallas kernels for 0%

commit v1 on v0

--- a/solution.py
+++ b/solution.py
@@ -1,10 +1,17 @@
+import functools
+import itertools
+
 import jax
 import jax.numpy as jnp
 from jax import lax
+from jax.experimental import pallas as pl
+from jax.experimental.pallas import tpu as pltpu
 from jax.sharding import PartitionSpec as P
 
 TILE = 1024
 TILE_ROWS = 128
+CORES = 2
+VMEM_BYTES = 58 * 1024 * 1024
 
 
 def spread_tiles(tile_flags, row_span, col_span):
@@ -15,7 +22,7 @@
     ).reshape(tile_rows * row_span, tile_cols * col_span)
 
 
-def on_device(amplitudes, amp_tiles, integrals, int_tiles, owner_tiles, other_terms, denominators):
+def plain(amplitudes, amp_tiles, integrals, int_tiles, owner_tiles, other_terms, denominators):
     masked_ints = integrals * spread_tiles(int_tiles, TILE, TILE)
     masked_amps = amplitudes * spread_tiles(amp_tiles, TILE_ROWS, TILE)
     tile_count = owner_tiles.shape[0]
@@ -31,7 +38,261 @@
     return (owned + other_terms) / denominators
 
 
+def plan_kernel(chips, rounds, owner_ref, pick_ref, source_ref, slot_ref, place_ref):
+    for q in range(chips * rounds):
+        place_ref[owner_ref[q]] = q
+    owner = [[place_ref[z * rounds + k] // rounds for k in range(rounds)] for z in range(chips)]
+    left = [
+        [sum((owner[z][k] == c).astype(jnp.int32) for k in range(rounds)) for c in range(chips)]
+        for z in range(chips)
+    ]
+    used = [[jnp.int32(0)] * rounds for _ in range(chips)]
+    for r in range(rounds):
+        there = [[jnp.minimum(left[z][c], 1) for c in range(chips)] for z in range(chips)]
+        code = jnp.int32(0)
+        for order in itertools.permutations(range(chips)):
+            fits = there[0][order[0]]
+            for z in range(1, chips):
+                fits = fits * there[z][order[z]]
+            code = jnp.where(fits > 0, sum(c << (4 * z) for z, c in enumerate(order)), code)
+        for z in range(chips):
+            target = (code >> (4 * z)) & 15
+            for c in range(chips):
+                left[z][c] = left[z][c] - (target == c).astype(jnp.int32)
+            pick = jnp.int32(0)
+            for k in range(rounds):
+                free = (owner[z][k] == target).astype(jnp.int32) * (1 - used[z][k])
+                pick = jnp.where(free > 0, k, pick)
+            for k in range(rounds):
+                used[z][k] = jnp.maximum(used[z][k], (pick == k).astype(jnp.int32))
+            pick_ref[r * chips + z] = pick
+            source_ref[r * chips + target] = z
+            slot_ref[r * chips + target] = place_ref[z * rounds + pick] % rounds
+
+
+def plan(owner_tiles, chips, rounds):
+    count = jax.ShapeDtypeStruct((chips * rounds,), jnp.int32)
+    smem = pl.BlockSpec(memory_space=pltpu.SMEM)
+    return pl.pallas_call(
+        functools.partial(plan_kernel, chips, rounds),
+        out_shape=(count, count, count),
+        in_specs=[smem],
+        out_specs=(smem, smem, smem),
+        scratch_shapes=[pltpu.SMEM((chips * rounds,), jnp.int32)],
+    )(owner_tiles)
+
+
+def half_kernel(core_ref, flag_ref, amp_ref, out_ref):
+    tiles = flag_ref.shape[1] // CORES
+    flag = flag_ref[pl.program_id(0), (1 - core_ref[0]) * tiles + pl.program_id(1)]
+    out_ref[...] = amp_ref[...] * flag.astype(jnp.float32)
+
+
+def other_half(core, amp_tiles, amplitudes):
+    rows, depth = amplitudes.shape
+    tiles = depth // TILE // CORES
+    return pl.pallas_call(
+        half_kernel,
+        out_shape=jax.ShapeDtypeStruct((rows, depth // CORES), jnp.float32),
+        grid_spec=pltpu.PrefetchScalarGridSpec(
+            num_scalar_prefetch=2,
+            grid=(rows // TILE_ROWS, tiles),
+            in_specs=[
+                pl.BlockSpec((TILE_ROWS, TILE), lambda i, j, core, flags: (i, (1 - core[0]) * tiles + j))
+            ],
+            out_specs=pl.BlockSpec((TILE_ROWS, TILE), lambda i, j, core, flags: (i, j)),
+        ),
+    )(core, amp_tiles, amplitudes)
+
+
+def pack_kernel(core_ref, pick_ref, flag_ref, amp_ref, swapped_ref, out_ref):
+    tiles = flag_ref.shape[1] // CORES
+    per_core = flag_ref.shape[0]
+    core = core_ref[0]
+    pick = pick_ref[0]
+    mine = pick // per_core == core
+
+    @pl.when(mine)
+    def _():
+        for j in range(tiles):
+            flag = flag_ref[pick % per_core, core * tiles + j].astype(jnp.float32)
+            columns = pl.ds(j * TILE, TILE)
+            out_ref[:, columns] = amp_ref[:, columns] * flag
+
+    @pl.when(jnp.logical_not(mine))
+    def _():
+        out_ref[...] = swapped_ref[...]
+
+
+def pack(core, pick, amp_tiles, amplitudes, swapped):
+    per_core = amp_tiles.shape[0]
+    half = swapped.shape[1]
+    return pl.pallas_call(
+        pack_kernel,
+        out_shape=jax.ShapeDtypeStruct((TILE_ROWS, half), jnp.float32),
+        grid_spec=pltpu.PrefetchScalarGridSpec(
+            num_scalar_prefetch=3,
+            grid=(1,),
+            in_specs=[
+                pl.BlockSpec((TILE_ROWS, half), lambda i, core, pick, flags: (pick[0] % per_core, core[0])),
+                pl.BlockSpec((TILE_ROWS, half), lambda i, core, pick, flags: (pick[0] % per_core, 0)),
+            ],
+            out_specs=pl.BlockSpec((TILE_ROWS, half), lambda i, core, pick, flags: (0, 0)),
+        ),
+    )(core, pick, amp_tiles, amplitudes, swapped)
+
+
+def split_kernel(value_ref, high_ref, low_ref):
+    value = value_ref[...]
+    high = value.astype(jnp.bfloat16)
+    high_ref[...] = high
+    low_ref[...] = (value - high.astype(jnp.float32)).astype(jnp.bfloat16)
+
+
+def split(integrals):
+    depth, width = integrals.shape
+    rows = TILE // 2
+    block = pl.BlockSpec((rows, width), lambda i: (i, 0))
+    half = jax.ShapeDtypeStruct((depth, width), jnp.bfloat16)
+    return pl.pallas_call(
+        split_kernel,
+        out_shape=(half, half),
+        grid=(depth // rows,),
+        in_specs=[block],
+        out_specs=(block, block),
+        compiler_params=pltpu.CompilerParams(vmem_limit_bytes=VMEM_BYTES),
+        cost_estimate=pl.CostEstimate(flops=0, bytes_accessed=8 * depth * width, transcendentals=0),
+    )(integrals)
+
+
+def product_kernel(ranks, source_ref, flag_ref, amp_ref, high_ref, low_ref, *rest):
+    out_refs, (pair_ref, total_ref) = rest[:ranks], rest[ranks:]
+    rows = ranks * TILE_ROWS
+    half = amp_ref.shape[2]
+    width = high_ref.shape[1]
+    step = pl.program_id(0)
+
+    @pl.when(step == 0)
+    def _():
+        for i in range(ranks):
+            at = pl.ds(i * TILE_ROWS, TILE_ROWS)
+            low_at = pl.ds(rows + i * TILE_ROWS, TILE_ROWS)
+            for core in range(CORES):
+                value = amp_ref[source_ref[i] * CORES + core]
+                high = value.astype(jnp.bfloat16)
+                columns = pl.ds(core * half, half)
+                pair_ref[at, columns] = high
+                pair_ref[low_at, columns] = (value - high.astype(jnp.float32)).astype(jnp.bfloat16)
+
+    total_ref[...] = jnp.zeros_like(total_ref)
+    for k in range(high_ref.shape[0] // TILE):
+        @pl.when(flag_ref[k, step * width // TILE] != 0)
+        def _():
+            deep = pl.ds(k * TILE, TILE)
+            both = jnp.dot(pair_ref[:, deep], high_ref[deep, :], preferred_element_type=jnp.float32)
+            cross = jnp.dot(pair_ref[:rows, deep], low_ref[deep, :], preferred_element_type=jnp.float32)
+            total_ref[...] += both[:rows] + (both[rows:] + cross)
+    for i in range(ranks):
+        out_refs[i][...] = total_ref[pl.ds(i * TILE_ROWS, TILE_ROWS), :]
+
+
+def product(source, int_tiles, gathered, high, low):
+    ranks = source.shape[0]
+    depth, width = high.shape
+    rows = ranks * TILE_ROWS
+    columns = TILE // 2
+    return pl.pallas_call(
+        functools.partial(product_kernel, ranks),
+        out_shape=[jax.ShapeDtypeStruct((TILE_ROWS, width), jnp.float32)] * ranks,
+        grid_spec=pltpu.PrefetchScalarGridSpec(
+            num_scalar_prefetch=2,
+            grid=(width // columns,),
+            in_specs=[
+                pl.BlockSpec(gathered.shape, lambda i, *_: (0, 0, 0), pipeline_mode=pl.Buffered(1)),
+                pl.BlockSpec((depth, columns), lambda i, *_: (0, i)),
+                pl.BlockSpec((depth, columns), lambda i, *_: (0, i)),
+            ],
+            out_specs=[pl.BlockSpec((TILE_ROWS, columns), lambda i, *_: (0, i))] * ranks,
+            scratch_shapes=[
+                pltpu.VMEM((2 * rows, depth), jnp.bfloat16),
+                pltpu.VMEM((rows, columns), jnp.float32),
+            ],
+        ),
+        compiler_params=pltpu.CompilerParams(vmem_limit_bytes=VMEM_BYTES),
+        cost_estimate=pl.CostEstimate(
+            flops=6 * rows * depth * width, bytes_accessed=4 * depth * width, transcendentals=0
+        ),
+    )(source, int_tiles, gathered, high, low)
+
+
+def finish_kernel(ranks, slot_ref, *refs):
+    parts, (term_ref, denominator_ref) = refs[:ranks], refs[ranks : ranks + 2]
+    total = parts[0][...]
+    for part in parts[1:]:
+        total = total + part[...]
+    refs[-1][...] = (total + term_ref[...]) / denominator_ref[...]
+
+
+def finish(slot, parts, other_terms, denominators, update):
+    ranks = len(parts)
+    width = other_terms.shape[1]
+    columns = TILE
+    part = pl.BlockSpec((TILE_ROWS, columns), lambda i, slot: (0, i))
+    owned = pl.BlockSpec((TILE_ROWS, columns), lambda i, slot: (slot[0], i))
+    before = [] if update is None else [update]
+    return pl.pallas_call(
+        functools.partial(finish_kernel, ranks),
+        out_shape=jax.ShapeDtypeStruct(other_terms.shape, jnp.float32),
+        grid_spec=pltpu.PrefetchScalarGridSpec(
+            num_scalar_prefetch=1,
+            grid=(width // columns,),
+            in_specs=[part] * ranks + [owned, owned] + [pl.BlockSpec(memory_space=pl.ANY)] * len(before),
+            out_specs=owned,
+        ),
+        input_output_aliases={ranks + 3: 0} if before else {},
+        cost_estimate=pl.CostEstimate(
+            flops=0, bytes_accessed=4 * (ranks + 3) * TILE_ROWS * width, transcendentals=0
+        ),
+    )(slot, *parts, other_terms, denominators, *before)
+
+
+def in_rounds(chips, rounds, amplitudes, amp_tiles, integrals, int_tiles, owner_tiles, other_terms, denominators):
+    rank = lax.axis_index("cd")
+    place = lax.axis_index("ab")
+    core = (place % CORES).astype(jnp.int32).reshape(1)
+    chip = place // CORES
+    swapped = lax.ppermute(
+        other_half(core, amp_tiles, amplitudes), "ab", [(i, i ^ 1) for i in range(chips * CORES)]
+    )
+    pick, source, slot = plan(owner_tiles, chips, rounds)
+    high, low = split(integrals)
+    peers = rank ^ jnp.arange(chips, dtype=jnp.int32)
+    update = None
+    for r in range(rounds):
+        mine = lax.dynamic_slice(pick, (r * chips + chip,), (1,))
+        gathered = lax.all_gather(pack(core, mine, amp_tiles, amplitudes, swapped), "ab", axis=0)
+        parts = product(source[r * chips + peers], int_tiles, gathered, high, low)
+        parts = [parts[0]] + [
+            lax.ppermute(parts[d], "cd", [(c, c ^ d) for c in range(chips)]) for d in range(1, chips)
+        ]
+        here = lax.dynamic_slice(slot, (r * chips + rank,), (1,))
+        update = finish(here, parts, other_terms, denominators, update)
+    return update
+
+
 def solution(mesh):
+    ranks, places = mesh.shape["cd"], mesh.shape["ab"]
+
+    def on_device(amplitudes, amp_tiles, integrals, int_tiles, owner_tiles, other_terms, denominators):
+        args = (amplitudes, amp_tiles, integrals, int_tiles, owner_tiles, other_terms, denominators)
+        tiles = owner_tiles.shape[0]
+        chips = places // CORES
+        rounds = tiles // chips
+        whole = places % CORES == 0 and tiles == chips * rounds and amplitudes.shape[1] % (CORES * TILE) == 0
+        if whole and chips == ranks and ranks in (2, 4):
+            return in_rounds(chips, rounds, *args)
+        return plain(*args)
+
     return jax.shard_map(
         on_device,
         mesh=mesh,

time: 716 us -> 488 us (0.68)
  matrix products: 226 us -> 0 us
  Pallas kernels: 0 us -> 180 us
  waiting for transfers between devices: 399 us -> 235 us
  local copies, waits for them, and re-layouts: 63.4 us -> 9.7 us
  starting transfers between devices: 0.04 us -> 47 us
  other arithmetic: 13.9 us -> 0.04 us
    dot_general x1 -> x0, matrix products: 226 us -> none  [on_device(): jnp.dot(gathered, masked_ints, precision=lax.Precision.HIGHEST, preferred...]
    pallas_call x0 -> x15, Pallas kernels: none -> 180 us  [the longest x4 118 us: product(): pl.pallas_call(functools.partial(product_kernel, ranks), out_shape=[jax.S...]
    reduce_scatter x1 -> x0, waiting for transfers between devices: 152 us -> none  [on_device(): lax.psum_scatter(partial_value, 'cd', scatter_dimension=0, tiled=True)]
    all_gather x1 -> x4, waiting for transfers between devices: 247 us -> 171 us  [in_rounds(): lax.all_gather(pack(core, mine, amp_tiles, amplitudes, swapped), 'ab', ax...]
    ppermute x0 -> x13, waiting for transfers between devices: none -> 63.6 us  [the longest x12 62.9 us: in_rounds(): lax.ppermute(parts[d], 'cd', [(c, c ^ d) for c in range(chips)])]
    ppermute x0 -> x13, starting transfers between devices: none -> 46.9 us  [the longest x12 46.4 us: in_rounds(): lax.ppermute(parts[d], 'cd', [(c, c ^ d) for c in range(chips)])]
    unnamed x6 -> x19, local copies, waits for them, and re-layouts: 35.1 us -> 3.01 us
    broadcast_in_dim x2 -> x0, local copies, waits for them, and re-layouts: 14.3 us -> none  [spread_tiles(): jnp.broadcast_to(values[:, None, :, None], (tile_rows, row_span, tile_col...]
  transfers between devices with their start and end apart: 2 -> 17, of which waited for: 2 -> 8; matrix products, arithmetic and copies ran while one was open for 6% -> 2% of each run, Pallas kernels for 0% -> 35%
where the time goes in v1:
time: 488 us; the launch traced here: 485 us
  waiting for transfers between devices  235 us (48%)
  Pallas kernels  180 us (37%)
  starting transfers between devices  47 us (10%)
  between operations  13.3 us (3%)
  local copies, waits for them, and re-layouts  9.7 us (2%)
    all_gather x4, waiting for transfers between devices, in_rounds(): lax.all_gather(pack(core, mine, amp_tiles, amplitudes, swapped), 'ab', ax...  171 us
    pallas_call x4, Pallas kernels, product(): pl.pallas_call(functools.partial(product_kernel, ranks), out_shape=[jax.S...  118 us
    ppermute x12, waiting for transfers between devices, in_rounds(): lax.ppermute(parts[d], 'cd', [(c, c ^ d) for c in range(chips)])  62.9 us
    ppermute x12, starting transfers between devices, in_rounds(): lax.ppermute(parts[d], 'cd', [(c, c ^ d) for c in range(chips)])  46.4 us
    pallas_call x1, Pallas kernels, split(): pl.pallas_call(split_kernel, out_shape=(half, half), grid=(depth // rows,...  22.8 us
    pallas_call x4, Pallas kernels, finish(): pl.pallas_call(functools.partial(finish_kernel, ranks), out_shape=jax.Sha...  17.4 us
    pallas_call x4, Pallas kernels, pack(): pl.pallas_call(pack_kernel, out_shape=jax.ShapeDtypeStruct((TILE_ROWS, ha...  15.9 us
  transfers between devices with their start and end apart: 17, of which 8 were waited for; matrix products, arithmetic and copies ran while one was open for 2% of the time, Pallas kernels for 35%

profile of v1, /device:TPU:0, one launch (start us, length us, event | category | flops | bytes accessed | tf_op | source)
XLA Modules:
  0.0 485.1 jit_solution(14307808669822935929)
XLA Ops:
  6.5 4.5 shard_map.74
  11.0 0.5 collective-permute-start
  11.5 1.8 shard_map.73
  13.4 1.4 fusion.4
  14.8 0.7 collective-permute-done.swapped_ref
  15.5 1.3 copy-done.1
  16.8 3.9 shard_map.82
  20.7 0.0 all-gather.15.cloned.1.call-update
  20.8 0.0 all-gather.13.cloned.1.call-start
  20.8 3.9 shard_map.80
  24.7 0.0 all-gather.13.cloned.1.call-update
  24.7 0.0 all-gather.11.cloned.1.call-start
  24.8 4.0 shard_map.78
  28.7 0.0 all-gather.11.cloned.1.call-update
  28.8 0.0 all-gather.9.cloned.1.call-start
  28.8 4.1 shard_map.75
  33.0 22.8 %shard_map.76 = (bf16[4096,2048]{1,0:T(8,128)(2,1)}, bf16[4096,2048]{1,0:T(8,128)(2,1)}) custom-call(f32[4096,2048]{1,0:T(8,128)} %value_ref.1), custom_call_target="tpu_custom_call" | custom-call | bytes 67108864 | tf_op jit(solution)/shard_map/pallas_call | solution.py:157
  55.8 0.7 copy.15.flag_ref
  56.5 1.1 gather_fusion.3
  57.6 1.1 gather_fusion.2
  58.8 1.2 gather_fusion.1
  60.0 1.2 gather_fusion
  61.1 44.5 %all-gather.15.cloned.1.call-done = f32[1024,2048]{1,0:T(8,128)} async-done(((f32[128,2048]{1,0:T(8,128)}), f32[1024,2048]{1,0:T(8,128)}) %all-gather.15.cloned.1.call-update) | async-done | bytes 8388624 | tf_op jit(solution)/shard_map/all_gather | solution.py:273
  105.6 29.4 %shard_map.83 = (f32[128,2048]{1,0:T(8,128)}, f32[128,2048]{1,0:T(8,128)}, f32[128,2048]{1,0:T(8,128)}, f32[128,2048]{1,0:T(8,128)}) custom-call(s32[4]{0:T(128)} %gather_fusion.3, s32[4,2]{1,0:T(4,128)} %copy.15.flag_ref, f32[8,128,2048]{2,1,0:T(8,128)} %bitcast.16, bf16[4096,2048]{1,0:T(8,128)(2,1)} %get-tuple-element.29.high_ref, ...), custom_call_target="tpu_custom_call" | custom-call | flops 25769803776 | bytes 33554432 | tf_op jit(solution)/shard_map/pallas_call | solution.py:204
  135.0 9.9 %collective-permute-start.10 = (f32[128,2048]{1,0:T(8,128)}, f32[128,2048]{1,0:T(8,128)S(1)}, u32[]{:S(2)}, u32[]{:S(2)}) collective-permute-start(f32[128,2048]{1,0:T(8,128)} %get-tuple-element.44), channel_id=1, source_target_pairs={{0,8},{8,0},{16,24},{24,16},{1,9},{9,1},{17,25},{25,17},{2,10},{10... | collective-permute-start | bytes 3145736 | tf_op jit(solution)/shard_map/ppermute | solution.py:276
  144.9 1.5 collective-permute-start.12
  146.5 41.4 %all-gather.13.cloned.1.call-done = f32[1024,2048]{1,0:T(8,128)} async-done(((f32[128,2048]{1,0:T(8,128)}), f32[1024,2048]{1,0:T(8,128)}) %all-gather.13.cloned.1.call-update) | async-done | bytes 8388624 | tf_op jit(solution)/shard_map/all_gather | solution.py:273
  187.8 29.4 %shard_map.81 = (f32[128,2048]{1,0:T(8,128)}, f32[128,2048]{1,0:T(8,128)}, f32[128,2048]{1,0:T(8,128)}, f32[128,2048]{1,0:T(8,128)}) custom-call(s32[4]{0:T(128)} %gather_fusion.2, s32[4,2]{1,0:T(4,128)} %copy.15.flag_ref, f32[8,128,2048]{2,1,0:T(8,128)} %bitcast.15, bf16[4096,2048]{1,0:T(8,128)(2,1)} %get-tuple-element.29.high_ref, ...), custom_call_target="tpu_custom_call" | custom-call | flops 25769803776 | bytes 33554432 | tf_op jit(solution)/shard_map/pallas_call | solution.py:204
  217.2 9.9 %collective-permute-start.7 = (f32[128,2048]{1,0:T(8,128)}, f32[128,2048]{1,0:T(8,128)}, u32[]{:S(2)}, u32[]{:S(2)}) collective-permute-start(f32[128,2048]{1,0:T(8,128)} %get-tuple-element.40), channel_id=1, source_target_pairs={{0,8},{8,0},{16,24},{24,16},{1,9},{9,1},{17,25},{25,17},{2,10},{10... | collective-permute-start | bytes 3145736 | tf_op jit(solution)/shard_map/ppermute | solution.py:276
  227.1 42.9 %all-gather.11.cloned.1.call-done = f32[1024,2048]{1,0:T(8,128)} async-done(((f32[128,2048]{1,0:T(8,128)}), f32[1024,2048]{1,0:T(8,128)}) %all-gather.11.cloned.1.call-update) | async-done | bytes 8388624 | tf_op jit(solution)/shard_map/all_gather | solution.py:273
  270.0 29.6 %shard_map.79 = (f32[128,2048]{1,0:T(8,128)}, f32[128,2048]{1,0:T(8,128)}, f32[128,2048]{1,0:T(8,128)}, f32[128,2048]{1,0:T(8,128)}) custom-call(s32[4]{0:T(128)} %gather_fusion.1, s32[4,2]{1,0:T(4,128)} %copy.15.flag_ref, f32[8,128,2048]{2,1,0:T(8,128)} %bitcast.14, bf16[4096,2048]{1,0:T(8,128)(2,1)} %get-tuple-element.29.high_ref, ...), custom_call_target="tpu_custom_call" | custom-call | flops 25769803776 | bytes 33554432 | tf_op jit(solution)/shard_map/pallas_call | solution.py:204
  299.7 0.3 collective-permute-start.9
  300.0 9.7 %collective-permute-start.4 = (f32[128,2048]{1,0:T(8,128)}, f32[128,2048]{1,0:T(8,128)}, u32[]{:S(2)}, u32[]{:S(2)}) collective-permute-start(f32[128,2048]{1,0:T(8,128)} %get-tuple-element.36), channel_id=1, source_target_pairs={{0,8},{8,0},{16,24},{24,16},{1,9},{9,1},{17,25},{25,17},{2,10},{10... | collective-permute-start | bytes 3145736 | tf_op jit(solution)/shard_map/ppermute | solution.py:276
  309.7 42.4 %all-gather.9.cloned.1.call-done = f32[1024,2048]{1,0:T(8,128)} async-done(((f32[128,2048]{1,0:T(8,128)}), f32[1024,2048]{1,0:T(8,128)}) %all-gather.9.cloned.1.call-update) | async-done | bytes 8388624 | tf_op jit(solution)/shard_map/all_gather | solution.py:273
  352.1 29.5 %shard_map.77 = (f32[128,2048]{1,0:T(8,128)}, f32[128,2048]{1,0:T(8,128)}, f32[128,2048]{1,0:T(8,128)}, f32[128,2048]{1,0:T(8,128)}) custom-call(s32[4]{0:T(128)} %gather_fusion, s32[4,2]{1,0:T(4,128)} %copy.15.flag_ref, f32[8,128,2048]{2,1,0:T(8,128)} %bitcast.13, bf16[4096,2048]{1,0:T(8,128)(2,1)} %get-tuple-element.29.high_ref, ...), custom_call_target="tpu_custom_call" | custom-call | flops 25769803776 | bytes 33554432 | tf_op jit(solution)/shard_map/pallas_call | solution.py:204
  381.7 3.0 collective-permute-start.5
  384.6 8.5 %collective-permute-start.6 = (f32[128,2048]{1,0:T(8,128)}, f32[128,2048]{1,0:T(8,128)}, u32[]{:S(2)}, u32[]{:S(2)}) collective-permute-start(f32[128,2048]{1,0:T(8,128)} %get-tuple-element.38), channel_id=1, source_target_pairs={{0,24},{8,16},{16,8},{24,0},{1,25},{9,17},{17,9},{25,1},{2,26},{10... | collective-permute-start | bytes 3145736 | tf_op jit(solution)/shard_map/ppermute | solution.py:276
  393.2 0.6 collective-permute-start.2
  393.8 2.9 collective-permute-start.3
  396.7 0.7 fusion.5
  397.3 4.4 shard_map.84.refs_6_
  401.7 4.3 shard_map.85.refs_6_
  406.1 23.3 %collective-permute-done.5.refs_2_ = f32[128,2048]{1,0:T(8,128)S(1)} collective-permute-done((f32[128,2048]{1,0:T(8,128)}, f32[128,2048]{1,0:T(8,128)S(1)}, u32[]{:S(2)}, u32[]{:S(2)}) %collective-permute-start.5) | collective-permute-done | bytes 1048608 | tf_op jit(solution)/shard_map/ppermute | solution.py:276
  429.4 1.0 copy-done.6
  430.4 4.4 shard_map.86.refs_6_
  434.8 4.8 collective-permute-done.1.refs_1_
  439.6 34.7 %collective-permute-done.2.refs_2_ = f32[128,2048]{1,0:T(8,128)} collective-permute-done((f32[128,2048]{1,0:T(8,128)}, f32[128,2048]{1,0:T(8,128)}, u32[]{:S(2)}, u32[]{:S(2)}) %collective-permute-start.2) | collective-permute-done | bytes 1048608 | tf_op jit(solution)/shard_map/ppermute | solution.py:276
  474.3 4.3 shard_map.87
  (36 shorter events, 0.1 us)
Async XLA Ops:
  6.5 99.1 %all-gather.15.cloned.1.call-start = ((), (), s32[]{:S(2)}) async-start(), calls=%async_computation.3 | async-start | bytes 9437184 | tf_op jit(solution)/shard_map/all_gather | solution.py:273
  11.0 4.5 collective-permute-start
  15.5 1.3 copy-start.1
  20.8 167.1 %all-gather.13.cloned.1.call-start = ((), (), s32[]{:S(2)}) async-start(), calls=%async_computation.2 | async-start | bytes 9437184 | tf_op jit(solution)/shard_map/all_gather | solution.py:273
  24.7 245.3 %all-gather.11.cloned.1.call-start = ((), (), s32[]{:S(2)}) async-start(), calls=%async_computation.1 | async-start | bytes 9437184 | tf_op jit(solution)/shard_map/all_gather | solution.py:273
  28.8 323.3 %all-gather.9.cloned.1.call-start = ((), (), s32[]{:S(2)}) async-start(), calls=%async_computation | async-start | bytes 9437184 | tf_op jit(solution)/shard_map/all_gather | solution.py:273
  32.9 22.9 %copy-start.8 = (s32[4,2]{0,1:T(2,128)S(1)}, s32[4,2]{0,1:T(2,128)}, u32[]{:S(2)}) copy-start(s32[4,2]{0,1:T(2,128)} %param.10) | copy-start | bytes 100
  33.0 23.6 %copy-start = (s32[16]{0:T(128)S(1)}, s32[16]{0:T(128)}, u32[]{:S(2)}) copy-start(s32[16]{0:T(128)} %get-tuple-element.27) | copy-start | bytes 196
  135.0 164.7 %collective-permute-start.10 = (f32[128,2048]{1,0:T(8,128)}, f32[128,2048]{1,0:T(8,128)S(1)}, u32[]{:S(2)}, u32[]{:S(2)}) collective-permute-start(f32[128,2048]{1,0:T(8,128)} %get-tuple-element.44), channel_id=1, source_target_pairs={{0,8},{8,0},{16,24},{24,16},{1,9},{9,1},{17,25},{25,17},{2,10},{10... | collective-permute-start | bytes 3145736 | tf_op jit(solution)/shard_map/ppermute | solution.py:276
  144.9 155.0 %collective-permute-start.11 = (f32[128,2048]{1,0:T(8,128)}, f32[128,2048]{1,0:T(8,128)S(1)}, u32[]{:S(2)}, u32[]{:S(2)}) collective-permute-start(f32[128,2048]{1,0:T(8,128)} %get-tuple-element.45), channel_id=1, source_target_pairs={{0,16},{8,24},{16,0},{24,8},{1,17},{9,25},{17,1},{25,9},{2,18},{10... | collective-permute-start | bytes 3145736 | tf_op jit(solution)/shard_map/ppermute | solution.py:276
  144.9 236.7 %collective-permute-start.12 = (f32[128,2048]{1,0:T(8,128)}, f32[128,2048]{1,0:T(8,128)S(1)}, u32[]{:S(2)}, u32[]{:S(2)}) collective-permute-start(f32[128,2048]{1,0:T(8,128)} %get-tuple-element.46), channel_id=1, source_target_pairs={{0,24},{8,16},{16,8},{24,0},{1,25},{9,17},{17,9},{25,1},{2,26},{10... | collective-permute-start | bytes 3145736 | tf_op jit(solution)/shard_map/ppermute | solution.py:276
  217.2 167.5 %collective-permute-start.7 = (f32[128,2048]{1,0:T(8,128)}, f32[128,2048]{1,0:T(8,128)}, u32[]{:S(2)}, u32[]{:S(2)}) collective-permute-start(f32[128,2048]{1,0:T(8,128)} %get-tuple-element.40), channel_id=1, source_target_pairs={{0,8},{8,0},{16,24},{24,16},{1,9},{9,1},{17,25},{25,17},{2,10},{10... | collective-permute-start | bytes 3145736 | tf_op jit(solution)/shard_map/ppermute | solution.py:276
  227.1 166.1 %collective-permute-start.8 = (f32[128,2048]{1,0:T(8,128)}, f32[128,2048]{1,0:T(8,128)}, u32[]{:S(2)}, u32[]{:S(2)}) collective-permute-start(f32[128,2048]{1,0:T(8,128)} %get-tuple-element.41), channel_id=1, source_target_pairs={{0,16},{8,24},{16,0},{24,8},{1,17},{9,25},{17,1},{25,9},{2,18},{10... | collective-permute-start | bytes 3145736 | tf_op jit(solution)/shard_map/ppermute | solution.py:276
  299.6 82.0 %copy-start.2 = (f32[128,2048]{1,0:T(8,128)}, f32[128,2048]{1,0:T(8,128)S(1)}, u32[]{:S(2)}) copy-start(f32[128,2048]{1,0:T(8,128)S(1)} %collective-permute-done.10.refs_1_) | copy-start | bytes 3145732
  299.7 93.5 %collective-permute-start.9 = (f32[128,2048]{1,0:T(8,128)}, f32[128,2048]{1,0:T(8,128)}, u32[]{:S(2)}, u32[]{:S(2)}) collective-permute-start(f32[128,2048]{1,0:T(8,128)} %get-tuple-element.42), channel_id=1, source_target_pairs={{0,24},{8,16},{16,8},{24,0},{1,25},{9,17},{17,9},{25,1},{2,26},{10... | collective-permute-start | bytes 3145736 | tf_op jit(solution)/shard_map/ppermute | solution.py:276
  299.9 81.7 %copy-start.3 = (f32[128,2048]{1,0:T(8,128)}, f32[128,2048]{1,0:T(8,128)S(1)}, u32[]{:S(2)}) copy-start(f32[128,2048]{1,0:T(8,128)S(1)} %collective-permute-done.11.refs_2_) | copy-start | bytes 3145732
  300.0 93.8 %collective-permute-start.4 = (f32[128,2048]{1,0:T(8,128)}, f32[128,2048]{1,0:T(8,128)}, u32[]{:S(2)}, u32[]{:S(2)}) collective-permute-start(f32[128,2048]{1,0:T(8,128)} %get-tuple-element.36), channel_id=1, source_target_pairs={{0,8},{8,0},{16,24},{24,16},{1,9},{9,1},{17,25},{25,17},{2,10},{10... | collective-permute-start | bytes 3145736 | tf_op jit(solution)/shard_map/ppermute | solution.py:276
  352.1 44.5 %copy-start.7 = (s32[16]{0:T(128)S(1)}, s32[16]{0:T(128)}, u32[]{:S(2)}) copy-start(s32[16]{0:T(128)} %get-tuple-element.26) | copy-start | bytes 196
  381.6 15.7 %copy-start.4 = (f32[128,2048]{1,0:T(8,128)}, f32[128,2048]{1,0:T(8,128)S(1)}, u32[]{:S(2)}) copy-start(f32[128,2048]{1,0:T(8,128)S(1)} %collective-permute-done.12.refs_3_) | copy-start | bytes 3145732
  381.7 47.7 %collective-permute-start.5 = (f32[128,2048]{1,0:T(8,128)}, f32[128,2048]{1,0:T(8,128)S(1)}, u32[]{:S(2)}, u32[]{:S(2)}) collective-permute-start(f32[128,2048]{1,0:T(8,128)} %get-tuple-element.37), channel_id=1, source_target_pairs={{0,16},{8,24},{16,0},{24,8},{1,17},{9,25},{17,1},{25,9},{2,18},{10... | collective-permute-start | bytes 3145736 | tf_op jit(solution)/shard_map/ppermute | solution.py:276
  384.6 44.7 %collective-permute-start.6 = (f32[128,2048]{1,0:T(8,128)}, f32[128,2048]{1,0:T(8,128)}, u32[]{:S(2)}, u32[]{:S(2)}) collective-permute-start(f32[128,2048]{1,0:T(8,128)} %get-tuple-element.38), channel_id=1, source_target_pairs={{0,24},{8,16},{16,8},{24,0},{1,25},{9,17},{17,9},{25,1},{2,26},{10... | collective-permute-start | bytes 3145736 | tf_op jit(solution)/shard_map/ppermute | solution.py:276
  393.2 46.4 %collective-permute-start.1 = (f32[128,2048]{1,0:T(8,128)}, f32[128,2048]{1,0:T(8,128)S(1)}, u32[]{:S(2)}, u32[]{:S(2)}) collective-permute-start(f32[128,2048]{1,0:T(8,128)} %get-tuple-element.32), channel_id=1, source_target_pairs={{0,8},{8,0},{16,24},{24,16},{1,9},{9,1},{17,25},{25,17},{2,10},{10... | collective-permute-start | bytes 3145736 | tf_op jit(solution)/shard_map/ppermute | solution.py:276
  393.2 81.1 %collective-permute-start.2 = (f32[128,2048]{1,0:T(8,128)}, f32[128,2048]{1,0:T(8,128)}, u32[]{:S(2)}, u32[]{:S(2)}) collective-permute-start(f32[128,2048]{1,0:T(8,128)} %get-tuple-element.33), channel_id=1, source_target_pairs={{0,16},{8,24},{16,0},{24,8},{1,17},{9,25},{17,1},{25,9},{2,18},{10... | collective-permute-start | bytes 3145736 | tf_op jit(solution)/shard_map/ppermute | solution.py:276
  393.8 80.5 %collective-permute-start.3 = (f32[128,2048]{1,0:T(8,128)}, f32[128,2048]{1,0:T(8,128)}, u32[]{:S(2)}, u32[]{:S(2)}) collective-permute-start(f32[128,2048]{1,0:T(8,128)} %get-tuple-element.34), channel_id=1, source_target_pairs={{0,24},{8,16},{16,8},{24,0},{1,25},{9,17},{17,9},{25,1},{2,26},{10... | collective-permute-start | bytes 3145736 | tf_op jit(solution)/shard_map/ppermute | solution.py:276
  429.4 1.0 copy-start.6
  439.6 34.8 %copy-start.5 = (f32[128,2048]{1,0:T(8,128)}, f32[128,2048]{1,0:T(8,128)S(1)}, u32[]{:S(2)}) copy-start(f32[128,2048]{1,0:T(8,128)S(1)} %collective-permute-done.1.refs_1_) | copy-start | bytes 3145732
Sparse Core Ops, SparseCore 0:
  20.9 84.6 all-gather.14
  107.2 80.5 all-gather.12
  189.4 80.5 all-gather.10
  271.5 80.5 all-gather.8

commit v2 on v1

v2 whole, which is shorter than its diff:
```python
import functools
import itertools

import jax
import jax.numpy as jnp
from jax import lax
from jax.experimental import pallas as pl
from jax.experimental.pallas import tpu as pltpu
from jax.sharding import PartitionSpec as P

TILE = 1024
TILE_ROWS = 128
CORES = 2
VMEM_BYTES = 58 * 1024 * 1024
CHAINS = 2
RANKS = (((0, 2), (1, 3)), ((0, 1), (2, 3)))


def spread_tiles(tile_flags, row_span, col_span):
    tile_rows, tile_cols = tile_flags.shape
    values = tile_flags.astype(jnp.float32)
    return jnp.broadcast_to(
        values[:, None, :, None], (tile_rows, row_span, tile_cols, col_span)
    ).reshape(tile_rows * row_span, tile_cols * col_span)


def plain(amplitudes, amp_tiles, integrals, int_tiles, owner_tiles, other_terms, denominators):
    masked_ints = integrals * spread_tiles(int_tiles, TILE, TILE)
    masked_amps = amplitudes * spread_tiles(amp_tiles, TILE_ROWS, TILE)
    tile_count = owner_tiles.shape[0]
    gathered = lax.all_gather(masked_amps, "ab", axis=0, tiled=True)
    partial_value = jnp.dot(
        gathered, masked_ints, precision=lax.Precision.HIGHEST, preferred_element_type=jnp.float32
    )
    col_width = partial_value.shape[1]
    partial_value = partial_value.reshape(tile_count, TILE_ROWS, col_width)[owner_tiles].reshape(
        tile_count * TILE_ROWS, col_width
    )
    owned = lax.psum_scatter(partial_value, "cd", scatter_dimension=0, tiled=True)
    return (owned + other_terms) / denominators


def plan_kernel(chips, rounds, owner_ref, here_ref, pick_ref, place_ref, slot_ref, inverse_ref):
    rank, chip = here_ref[0], here_ref[1]
    for q in range(chips * rounds):
        inverse_ref[owner_ref[q]] = q
    owner = [[inverse_ref[z * rounds + k] // rounds for k in range(rounds)] for z in range(chips)]
    left = [
        [sum((owner[z][k] == c).astype(jnp.int32) for k in range(rounds)) for c in range(chips)]
        for z in range(chips)
    ]
    used = [[jnp.int32(0)] * rounds for _ in range(chips)]
    for r in range(rounds):
        there = [[jnp.minimum(left[z][c], 1) for c in range(chips)] for z in range(chips)]
        code = jnp.int32(0)
        for order in itertools.permutations(range(chips)):
            fits = there[0][order[0]]
            for z in range(1, chips):
                fits = fits * there[z][order[z]]
            code = jnp.where(fits > 0, sum(c << (4 * z) for z, c in enumerate(order)), code)
        my_pick = jnp.int32(0)
        slot = jnp.int32(0)
        for z in range(chips):
            target = (code >> (4 * z)) & 15
            for c in range(chips):
                left[z][c] = left[z][c] - (target == c).astype(jnp.int32)
            pick = jnp.int32(0)
            for k in range(rounds):
                free = (owner[z][k] == target).astype(jnp.int32) * (1 - used[z][k])
                pick = jnp.where(free > 0, k, pick)
            for k in range(rounds):
                used[z][k] = jnp.maximum(used[z][k], (pick == k).astype(jnp.int32))
            my_pick = jnp.where(chip == z, pick, my_pick)
            slot = jnp.where(target == rank, inverse_ref[z * rounds + pick] % rounds, slot)
            place_ref[r * chips + z] = target ^ rank
        pick_ref[r] = my_pick
        slot_ref[r] = slot


def plan(owner_tiles, here, chips, rounds):
    each = jax.ShapeDtypeStruct((rounds,), jnp.int32)
    smem = pl.BlockSpec(memory_space=pltpu.SMEM)
    return pl.pallas_call(
        functools.partial(plan_kernel, chips, rounds),
        out_shape=(each, jax.ShapeDtypeStruct((rounds * chips,), jnp.int32), each),
        in_specs=[smem, smem],
        out_specs=(smem, smem, smem),
        scratch_shapes=[pltpu.SMEM((chips * rounds,), jnp.int32)],
    )(owner_tiles, here)


def half_kernel(core_ref, flag_ref, amp_ref, out_ref):
    tiles = flag_ref.shape[1] // CORES
    flag = flag_ref[pl.program_id(0), (1 - core_ref[0]) * tiles + pl.program_id(1)]
    out_ref[...] = amp_ref[...] * flag.astype(jnp.float32)


def other_half(core, amp_tiles, amplitudes):
    rows, depth = amplitudes.shape
    tiles = depth // TILE // CORES
    return pl.pallas_call(
        half_kernel,
        out_shape=jax.ShapeDtypeStruct((rows, depth // CORES), jnp.float32),
        grid_spec=pltpu.PrefetchScalarGridSpec(
            num_scalar_prefetch=2,
            grid=(rows // TILE_ROWS, tiles),
            in_specs=[
                pl.BlockSpec((TILE_ROWS, TILE), lambda i, j, core, flags: (i, (1 - core[0]) * tiles + j))
            ],
            out_specs=pl.BlockSpec((TILE_ROWS, TILE), lambda i, j, core, flags: (i, j)),
        ),
    )(core, amp_tiles, amplitudes)


def pack_kernel(r, core_ref, pick_ref, flag_ref, amp_ref, swapped_ref, out_ref):
    tiles = flag_ref.shape[1] // CORES
    per_core = flag_ref.shape[0]
    core = core_ref[0]
    pick = pick_ref[r]
    mine = pick // per_core == core

    @pl.when(mine)
    def _():
        for j in range(tiles):
            flag = flag_ref[pick % per_core, core * tiles + j].astype(jnp.float32)
            columns = pl.ds(j * TILE, TILE)
            out_ref[:, columns] = amp_ref[:, columns] * flag

    @pl.when(jnp.logical_not(mine))
    def _():
        out_ref[...] = swapped_ref[...]


def pack(r, core, pick, amp_tiles, amplitudes, swapped):
    per_core = amp_tiles.shape[0]
    half = swapped.shape[1]
    return pl.pallas_call(
        functools.partial(pack_kernel, r),
        out_shape=jax.ShapeDtypeStruct((TILE_ROWS, half), jnp.float32),
        grid_spec=pltpu.PrefetchScalarGridSpec(
            num_scalar_prefetch=3,
            grid=(1,),
            in_specs=[
                pl.BlockSpec((TILE_ROWS, half), lambda i, core, pick, flags: (pick[r] % per_core, core[0])),
                pl.BlockSpec((TILE_ROWS, half), lambda i, core, pick, flags: (pick[r] % per_core, 0)),
            ],
            out_specs=pl.BlockSpec((TILE_ROWS, half), lambda i, core, pick, flags: (0, 0)),
        ),
    )(core, pick, amp_tiles, amplitudes, swapped)


def split_kernel(value_ref, high_ref, low_ref):
    value = value_ref[...]
    high = value.astype(jnp.bfloat16)
    high_ref[...] = high
    low_ref[...] = (value - high.astype(jnp.float32)).astype(jnp.bfloat16)


def split(integrals):
    depth, width = integrals.shape
    rows = TILE // 2
    block = pl.BlockSpec((rows, width), lambda i: (i, 0))
    half = jax.ShapeDtypeStruct((depth, width), jnp.bfloat16)
    return pl.pallas_call(
        split_kernel,
        out_shape=(half, half),
        grid=(depth // rows,),
        in_specs=[block],
        out_specs=(block, block),
        compiler_params=pltpu.CompilerParams(vmem_limit_bytes=VMEM_BYTES),
        cost_estimate=pl.CostEstimate(flops=0, bytes_accessed=8 * depth * width, transcendentals=0),
    )(integrals)


def product_kernel(r, first, ranks, core_ref, place_ref, flag_ref, mine_ref, other_ref, high_ref, low_ref, *refs):
    out_refs, (pair_ref, total_ref) = refs[: 2 * CHAINS], refs[2 * CHAINS :]
    rows = ranks * TILE_ROWS
    half = mine_ref.shape[2]
    width = high_ref.shape[1]
    step = pl.program_id(0)

    @pl.when(step == 0)
    def _():
        for z in range(ranks):
            at = pl.multiple_of(place_ref[r * ranks + z] * TILE_ROWS, TILE_ROWS)
            for away, amp_ref in enumerate((mine_ref, other_ref)):
                value = amp_ref[z]
                high = value.astype(jnp.bfloat16)
                columns = pl.ds(pl.multiple_of((core_ref[0] ^ away) * half, half), half)
                pair_ref[pl.ds(at, TILE_ROWS), columns] = high
                pair_ref[pl.ds(rows + at, TILE_ROWS), columns] = (value - high.astype(jnp.float32)).astype(
                    jnp.bfloat16
                )

    total_ref[...] = jnp.zeros_like(total_ref)
    for k in range(high_ref.shape[0] // TILE):
        @pl.when(flag_ref[k, (first + step) * width // TILE] != 0)
        def _():
            deep = pl.ds(k * TILE, TILE)
            both = jnp.dot(pair_ref[:, deep], high_ref[deep, :], preferred_element_type=jnp.float32)
            cross = jnp.dot(pair_ref[:rows, deep], low_ref[deep, :], preferred_element_type=jnp.float32)
            total_ref[...] += both[:rows] + (both[rows:] + cross)
    share = width // CHAINS
    for chain, (kept, sent) in enumerate(RANKS):
        columns = pl.ds(chain * share, share)
        for ref, peers in ((out_refs[2 * chain], kept), (out_refs[2 * chain + 1], sent)):
            for i, peer in enumerate(peers):
                ref[i] = total_ref[pl.ds(peer * TILE_ROWS, TILE_ROWS), columns]


def product(r, piece, pieces, core, place, int_tiles, mine, other, high, low):
    ranks = mine.shape[0]
    depth, width = high.shape
    rows = ranks * TILE_ROWS
    columns = TILE // 2
    share = columns // CHAINS
    steps = width // columns // pieces
    amp = pl.BlockSpec(mine.shape, lambda i, *_: (0, 0, 0), pipeline_mode=pl.Buffered(1))
    integral = pl.BlockSpec((depth, columns), lambda i, *_: (0, piece * steps + i))
    return pl.pallas_call(
        functools.partial(product_kernel, r, piece * steps, ranks),
        out_shape=[jax.ShapeDtypeStruct((2, TILE_ROWS, share * steps), jnp.float32)] * (2 * CHAINS),
        grid_spec=pltpu.PrefetchScalarGridSpec(
            num_scalar_prefetch=3,
            grid=(steps,),
            in_specs=[amp, amp, integral, integral],
            out_specs=[pl.BlockSpec((2, TILE_ROWS, share), lambda i, *_: (0, 0, i))] * (2 * CHAINS),
            scratch_shapes=[
                pltpu.VMEM((2 * rows, depth), jnp.bfloat16),
                pltpu.VMEM((rows, columns), jnp.float32),
            ],
        ),
        compiler_params=pltpu.CompilerParams(vmem_limit_bytes=VMEM_BYTES),
        cost_estimate=pl.CostEstimate(
            flops=6 * rows * depth * width // pieces, bytes_accessed=4 * depth * width // pieces, transcendentals=0
        ),
    )(core, place, int_tiles, mine, other, high, low)


def relay_kernel(*refs):
    for chain in range(CHAINS):
        refs[2 * CHAINS + chain][...] = refs[2 * chain][0] + refs[2 * chain + 1][0]


def relay(kept, heard):
    _, rows, width = kept[0].shape
    passed = pl.BlockSpec((1, rows, width), lambda i: (1, 0, 0))
    out = jax.ShapeDtypeStruct((rows, width), jnp.float32)
    return pl.pallas_call(
        relay_kernel,
        out_shape=[out] * CHAINS,
        grid=(1,),
        in_specs=[passed] * (2 * CHAINS),
        out_specs=[pl.BlockSpec((rows, width), lambda i: (0, 0))] * CHAINS,
    )(*[array for pair in zip(kept, heard) for array in pair])


def finish_kernel(columns, *refs):
    refs = refs[1:]
    parts, (term_ref, denominator_ref), out_ref = refs[: 3 * CHAINS], refs[3 * CHAINS : 3 * CHAINS + 2], refs[-1]
    share = columns // CHAINS
    for block in range(term_ref.shape[1] // columns):
        for chain in range(CHAINS):
            kept, heard, relayed = parts[3 * chain : 3 * chain + 3]
            source = pl.ds(block * share, share)
            target = pl.ds(block * columns + chain * share, share)
            total = kept[0, :, source] + heard[0, :, source] + relayed[:, source]
            out_ref[:, target] = (total + term_ref[:, target]) / denominator_ref[:, target]


def finish(r, piece, slot, kept, heard, relayed, other_terms, denominators, update):
    share = kept[0].shape[2]
    width = share * CHAINS
    first = pl.BlockSpec((1, TILE_ROWS, share), lambda i, slot: (0, 0, 0))
    whole = pl.BlockSpec((TILE_ROWS, share), lambda i, slot: (0, 0))
    owned = pl.BlockSpec((TILE_ROWS, width), lambda i, slot: (slot[r], piece))
    before = [] if update is None else [update]
    return pl.pallas_call(
        functools.partial(finish_kernel, TILE // 2),
        out_shape=jax.ShapeDtypeStruct(other_terms.shape, jnp.float32),
        grid_spec=pltpu.PrefetchScalarGridSpec(
            num_scalar_prefetch=1,
            grid=(1,),
            in_specs=[first, first, whole] * CHAINS
            + [owned, owned]
            + [pl.BlockSpec(memory_space=pl.ANY)] * len(before),
            out_specs=owned,
        ),
        input_output_aliases={3 * CHAINS + 3: 0} if before else {},
        cost_estimate=pl.CostEstimate(flops=0, bytes_accessed=24 * TILE_ROWS * width, transcendentals=0),
    )(
        slot,
        *[array for chain in zip(kept, heard, relayed) for array in chain],
        other_terms,
        denominators,
        *before,
    )


def in_rounds(chips, rounds, amplitudes, amp_tiles, integrals, int_tiles, owner_tiles, other_terms, denominators):
    rank = lax.axis_index("cd").astype(jnp.int32)
    spot = lax.axis_index("ab").astype(jnp.int32)
    core = (spot % CORES).reshape(1)
    spots = chips * CORES
    siblings = [(i, i ^ 1) for i in range(spots)]
    same_core = [list(range(i, spots, CORES)) for i in range(CORES)]
    swapped = lax.ppermute(other_half(core, amp_tiles, amplitudes), "ab", siblings)
    pick, place, slot = plan(owner_tiles, jnp.stack([rank, spot // CORES]), chips, rounds)
    high, low = split(integrals)
    owns = [pack(r, core, pick, amp_tiles, amplitudes, swapped) for r in range(rounds)]
    gathered = [lax.all_gather(own, "ab", axis=0, axis_index_groups=same_core) for own in owns]
    def swap(sent, peers):
        return [lax.ppermute(array, "cd", [(c, c ^ peer) for c in range(chips)]) for array, peer in zip(sent, peers)]

    terms = (other_terms, denominators)
    update = waiting = None
    for r in range(rounds):
        if r == 0:
            mine, high, low, *_ = lax.optimization_barrier((gathered[r], high, low, *owns))
        else:
            mine, onward, update = lax.optimization_barrier((gathered[r], onward, update))
        other = lax.ppermute(mine, "ab", siblings)
        pieces = 2 if r == rounds - 1 else 1
        sums = []
        for piece in range(pieces):
            parts = product(r, piece, pieces, core, place, int_tiles, mine, other, high, low)
            if waiting is not None:
                parts, relayed = lax.optimization_barrier((parts, waiting[-1]))
                update = finish(*waiting[:-1], relayed, *terms, update)
                waiting = None
            if piece > 0:
                parts, heard = lax.optimization_barrier((parts, sums[-1][1]))
                sums[-1] = (sums[-1][0], heard)
            sums.append((parts[0::2], swap(parts[1::2], (1, 2))))
        for piece, (kept, heard) in enumerate(sums):
            if piece > 0:
                heard, update = lax.optimization_barrier((heard, update))
            onward = relay(kept, heard)
            relayed = swap(onward, (2, 1))
            if piece < pieces - 1 or r == rounds - 1:
                sums[piece] = (r, piece, slot, kept, heard, relayed)
            else:
                waiting = (r, piece, slot, kept, heard, relayed)
    for ready in sums:
        update = finish(*ready, *terms, update)
    return update


def solution(mesh):
    ranks, places = mesh.shape["cd"], mesh.shape["ab"]

    def on_device(amplitudes, amp_tiles, integrals, int_tiles, owner_tiles, other_terms, denominators):
        args = (amplitudes, amp_tiles, integrals, int_tiles, owner_tiles, other_terms, denominators)
        tiles = owner_tiles.shape[0]
        chips = places // CORES
        rounds = tiles // chips
        whole = places % CORES == 0 and tiles == chips * rounds and amplitudes.shape[1] % (CORES * TILE) == 0
        if whole and chips == ranks and ranks == 4:
            return in_rounds(chips, rounds, *args)
        return plain(*args)

    return jax.shard_map(
        on_device,
        mesh=mesh,
        in_specs=(
            P("ab", "cd"),
            P("ab", "cd"),
            P("cd", "ab"),
            P("cd", "ab"),
            P(),
            P("cd", "ab"),
            P("cd", "ab"),
        ),
        out_specs=P("cd", "ab"),
        check_vma=False,
    )
```

time: 488 us -> 439 us (0.90)
  waiting for transfers between devices: 235 us -> 168 us
  starting transfers between devices: 47 us -> 74.6 us
  Pallas kernels: 180 us -> 172 us
    all_gather x4, waiting for transfers between devices: 171 us -> 80.5 us  [in_rounds(): lax.all_gather(own, 'ab', axis=0, axis_index_groups=same_core)]
    ppermute x13 -> x25, starting transfers between devices: 46.9 us -> 74.3 us  [the longest x20 73.8 us: swap(): lax.ppermute(array, 'cd', [(c, c ^ peer) for c in range(chips)])]
    ppermute x13 -> x25, waiting for transfers between devices: 63.6 us -> 87.7 us  [the longest x20 66.4 us: swap(): lax.ppermute(array, 'cd', [(c, c ^ peer) for c in range(chips)])]
    pallas_call x12 -> x19, Pallas kernels: 151 us -> 143 us  [the longest x5 97.7 us: product(): pl.pallas_call(functools.partial(product_kernel, r, piece * steps, ranks)...]
    unnamed x19 -> x47, local copies, waits for them, and re-layouts: 3.01 us -> 9.97 us
  transfers between devices with their start and end apart: 17 -> 29, of which waited for: 8 -> 18; matrix products, arithmetic and copies ran while one was open for 2% -> 0% of each run, Pallas kernels for 35% -> 37%
where the time goes in v2:
time: 439 us; the launch traced here: 438 us
  Pallas kernels  172 us (39%)
  waiting for transfers between devices  168 us (38%)
  starting transfers between devices  74.6 us (17%)
  between operations  13.3 us (3%)
  local copies, waits for them, and re-layouts  9.97 us (2%)
    pallas_call x5, Pallas kernels, product(): pl.pallas_call(functools.partial(product_kernel, r, piece * steps, ranks)...  97.7 us
    all_gather x4, waiting for transfers between devices, in_rounds(): lax.all_gather(own, 'ab', axis=0, axis_index_groups=same_core)  80.5 us
    ppermute x20, starting transfers between devices, swap(): lax.ppermute(array, 'cd', [(c, c ^ peer) for c in range(chips)])  73.8 us
    ppermute x20, waiting for transfers between devices, swap(): lax.ppermute(array, 'cd', [(c, c ^ peer) for c in range(chips)])  66.4 us
    pallas_call x1, Pallas kernels, split(): pl.pallas_call(split_kernel, out_shape=(half, half), grid=(depth // rows,...  22.8 us
    pallas_call x5, Pallas kernels, finish(): pl.pallas_call(functools.partial(finish_kernel, TILE // 2), out_shape=jax...  19.8 us
    ppermute x4, waiting for transfers between devices, in_rounds(): other = lax.ppermute(mine, 'ab', siblings)  19.8 us
    pallas_call x4, Pallas kernels, pack(): pl.pallas_call(functools.partial(pack_kernel, r), out_shape=jax.ShapeDtyp...  13.4 us
  transfers between devices with their start and end apart: 29, of which 18 were waited for; matrix products, arithmetic and copies ran while one was open for 0% of the time, Pallas kernels for 37%

profile of v2, /device:TPU:0, one launch (start us, length us, event | category | flops | bytes accessed | tf_op | source)
XLA Modules:
  0.0 438.5 jit_solution(3236147580342479714)
XLA Ops:
  6.5 4.5 %shard_map.74 = f32[256,2048]{1,0:T(8,128)} custom-call(s32[1]{0:T(128)} %bitcast.2.core_ref, s32[2,4]{1,0:T(2,128)} %flag_ref.14, f32[256,4096]{1,0:T(8,128)} %amp_ref.9), custom_call_target="tpu_custom_call" | custom-call | tf_op jit(solution)/shard_map/pallas_call | solution.py:101
  16.8 3.3 shard_map.78
  20.2 22.8 %shard_map.79 = (bf16[4096,2048]{1,0:T(8,128)(2,1)}, bf16[4096,2048]{1,0:T(8,128)(2,1)}) custom-call(f32[4096,2048]{1,0:T(8,128)} %value_ref.1), custom_call_target="tpu_custom_call" | custom-call | bytes 67108864 | tf_op jit(solution)/shard_map/pallas_call | solution.py:164
  43.0 3.3 shard_map.76
  46.3 3.3 shard_map.77
  49.6 3.5 shard_map.75
  53.1 50.6 %all-gather.15.cloned.1.call-done = f32[512,2048]{1,0:T(8,128)} async-done(((f32[128,2048]{1,0:T(8,128)}), f32[512,2048]{1,0:T(8,128)}) %all-gather.15.cloned.1.call-update) | async-done | bytes 4194320 | tf_op jit(solution)/shard_map/all_gather | solution.py:311
  104.4 6.8 %collective-permute-done.1.other_ref = f32[4,128,2048]{2,1,0:T(8,128)} collective-permute-done((f32[4,128,2048]{2,1,0:T(8,128)}, f32[4,128,2048]{2,1,0:T(8,128)}, u32[]{:S(2)}, u32[]{:S(2)}) %collective-permute-start.1) | collective-permute-done | bytes 4194336 | tf_op jit(solution)/shard_map/ppermute | solution.py:322
  111.2 22.8 %shard_map.80 = (f32[2,128,1024]{2,1,0:T(8,128)}, f32[2,128,1024]{2,1,0:T(8,128)}, f32[2,128,1024]{2,1,0:T(8,128)}, f32[2,128,1024]{2,1,0:T(8,128)}) custom-call(s32[1]{0:T(128)} %bitcast.2.core_ref, s32[16]{0:T(128)} %get-tuple-element.76.place_ref, s32[4,2]{1,0:T(4,128)} %copy.15.flag_ref, f32[4,128,2048]{2,1,0:T(8,128)} %bitcast.15, ...), custom_call_target="tpu_custom_call" | custom-call | flops 25769803776 | bytes 33554432 | tf_op jit(solution)/shard_map/pallas_call | solution.py:220
  134.0 6.4 %collective-permute-start.2 = (f32[2,128,1024]{2,1,0:T(8,128)}, f32[2,128,1024]{2,1,0:T(8,128)S(1)}, u32[]{:S(2)}, u32[]{:S(2)}) collective-permute-start(f32[2,128,1024]{2,1,0:T(8,128)} %get-tuple-element.84), channel_id=1, source_target_pairs={{0,8},{8,0},{16,24},{24,16},{1,9},{9,1},{17,25},{25,17},{2,10},{10... | collective-permute-start | bytes 3145736 | tf_op jit(solution)/shard_map/ppermute | solution.py:313
  140.4 7.1 %collective-permute-start.3 = (f32[2,128,1024]{2,1,0:T(8,128)}, f32[2,128,1024]{2,1,0:T(8,128)S(1)}, u32[]{:S(2)}, u32[]{:S(2)}) collective-permute-start(f32[2,128,1024]{2,1,0:T(8,128)} %get-tuple-element.86), channel_id=1, source_target_pairs={{0,16},{8,24},{16,0},{24,8},{1,17},{9,25},{17,1},{25,9},{2,18},{10... | collective-permute-start | bytes 3145736 | tf_op jit(solution)/shard_map/ppermute | solution.py:313
  147.5 10.6 %collective-permute-done.2.refs_1_.refs_2_ = f32[2,128,1024]{2,1,0:T(8,128)S(1)} collective-permute-done((f32[2,128,1024]{2,1,0:T(8,128)}, f32[2,128,1024]{2,1,0:T(8,128)S(1)}, u32[]{:S(2)}, u32[]{:S(2)}) %collective-permute-start.2) | collective-permute-done | bytes 1048608 | tf_op jit(solution)/shard_map/ppermute | solution.py:313
  158.1 12.8 %collective-permute-done.3.refs_3_.refs_5_ = f32[2,128,1024]{2,1,0:T(8,128)S(1)} collective-permute-done((f32[2,128,1024]{2,1,0:T(8,128)}, f32[2,128,1024]{2,1,0:T(8,128)S(1)}, u32[]{:S(2)}, u32[]{:S(2)}) %collective-permute-start.3) | collective-permute-done | bytes 1048608 | tf_op jit(solution)/shard_map/ppermute | solution.py:313
  171.9 2.6 shard_map.81
  174.4 10.1 %all-gather.13.cloned.1.call-done = f32[512,2048]{1,0:T(8,128)} async-done(((f32[128,2048]{1,0:T(8,128)}), f32[512,2048]{1,0:T(8,128)}) %all-gather.13.cloned.1.call-update) | async-done | bytes 4194320 | tf_op jit(solution)/shard_map/all_gather | solution.py:311
  187.9 4.2 collective-permute-done.4.other_ref
  192.1 22.8 %shard_map.82 = (f32[2,128,1024]{2,1,0:T(8,128)}, f32[2,128,1024]{2,1,0:T(8,128)}, f32[2,128,1024]{2,1,0:T(8,128)}, f32[2,128,1024]{2,1,0:T(8,128)}) custom-call(s32[1]{0:T(128)} %bitcast.2.core_ref, s32[16]{0:T(128)} %get-tuple-element.76.place_ref, s32[4,2]{1,0:T(4,128)} %copy.15.flag_ref, f32[4,128,2048]{2,1,0:T(8,128)} %bitcast.13, ...), custom_call_target="tpu_custom_call" | custom-call | flops 25769803776 | bytes 33554432 | tf_op jit(solution)/shard_map/pallas_call | solution.py:220
  214.9 6.5 %collective-permute-start.7 = (f32[2,128,1024]{2,1,0:T(8,128)}, f32[2,128,1024]{2,1,0:T(8,128)S(1)}, u32[]{:S(2)}, u32[]{:S(2)}) collective-permute-start(f32[2,128,1024]{2,1,0:T(8,128)} %get-tuple-element.95), channel_id=1, source_target_pairs={{0,8},{8,0},{16,24},{24,16},{1,9},{9,1},{17,25},{25,17},{2,10},{10... | collective-permute-start | bytes 3145736 | tf_op jit(solution)/shard_map/ppermute | solution.py:313
  221.4 7.1 %collective-permute-start.8 = (f32[2,128,1024]{2,1,0:T(8,128)}, f32[2,128,1024]{2,1,0:T(8,128)S(1)}, u32[]{:S(2)}, u32[]{:S(2)}) collective-permute-start(f32[2,128,1024]{2,1,0:T(8,128)} %get-tuple-element.97), channel_id=1, source_target_pairs={{0,16},{8,24},{16,0},{24,8},{1,17},{9,25},{17,1},{25,9},{2,18},{10... | collective-permute-start | bytes 3145736 | tf_op jit(solution)/shard_map/ppermute | solution.py:313
  228.5 4.4 %shard_map.84.refs_9_ = f32[512,2048]{1,0:T(8,128)} custom-call(s32[4]{0:T(128)} %get-tuple-element.75.refs_0_, f32[2,128,1024]{2,1,0:T(8,128)} %get-tuple-element.83.refs_0_.refs_1_, f32[2,128,1024]{2,1,0:T(8,128)} %copy-done.5, f32[128,1024]{1,0:T(8,128)} %copy-done.13, f32[2,128,1024]{2,1,0:T(8,128)} %get-tuple-element.85.refs_2_.refs_4_, ...), custom_call_target="tpu_custom_call" | custom-call | bytes 6291456 | tf_op jit(solution)/shard_map/pallas_call | solution.py:278
  232.9 6.1 %collective-permute-done.7.refs_1_.refs_2_ = f32[2,128,1024]{2,1,0:T(8,128)S(1)} collective-permute-done((f32[2,128,1024]{2,1,0:T(8,128)}, f32[2,128,1024]{2,1,0:T(8,128)S(1)}, u32[]{:S(2)}, u32[]{:S(2)}) %collective-permute-start.7) | collective-permute-done | bytes 1048608 | tf_op jit(solution)/shard_map/ppermute | solution.py:313
  239.1 12.8 %collective-permute-done.8.refs_3_.refs_5_ = f32[2,128,1024]{2,1,0:T(8,128)S(1)} collective-permute-done((f32[2,128,1024]{2,1,0:T(8,128)}, f32[2,128,1024]{2,1,0:T(8,128)S(1)}, u32[]{:S(2)}, u32[]{:S(2)}) %collective-permute-start.8) | collective-permute-done | bytes 1048608 | tf_op jit(solution)/shard_map/ppermute | solution.py:313
  253.0 2.6 shard_map.83
  255.5 9.9 %all-gather.11.cloned.1.call-done = f32[512,2048]{1,0:T(8,128)} async-done(((f32[128,2048]{1,0:T(8,128)}), f32[512,2048]{1,0:T(8,128)}) %all-gather.11.cloned.1.call-update) | async-done | bytes 4194320 | tf_op jit(solution)/shard_map/all_gather | solution.py:311
  268.5 4.4 %collective-permute-done.9.other_ref = f32[4,128,2048]{2,1,0:T(8,128)} collective-permute-done((f32[4,128,2048]{2,1,0:T(8,128)}, f32[4,128,2048]{2,1,0:T(8,128)}, u32[]{:S(2)}, u32[]{:S(2)}) %collective-permute-start.9) | collective-permute-done | bytes 4194336 | tf_op jit(solution)/shard_map/ppermute | solution.py:322
  273.0 22.8 %shard_map.85 = (f32[2,128,1024]{2,1,0:T(8,128)}, f32[2,128,1024]{2,1,0:T(8,128)}, f32[2,128,1024]{2,1,0:T(8,128)}, f32[2,128,1024]{2,1,0:T(8,128)}) custom-call(s32[1]{0:T(128)} %bitcast.2.core_ref, s32[16]{0:T(128)} %get-tuple-element.76.place_ref, s32[4,2]{1,0:T(4,128)} %copy.15.flag_ref, f32[4,128,2048]{2,1,0:T(8,128)} %bitcast.11, ...), custom_call_target="tpu_custom_call" | custom-call | flops 25769803776 | bytes 33554432 | tf_op jit(solution)/shard_map/pallas_call | solution.py:220
  295.8 6.5 %collective-permute-start.12 = (f32[2,128,1024]{2,1,0:T(8,128)}, f32[2,128,1024]{2,1,0:T(8,128)S(1)}, u32[]{:S(2)}, u32[]{:S(2)}) collective-permute-start(f32[2,128,1024]{2,1,0:T(8,128)} %get-tuple-element.108), channel_id=1, source_target_pairs={{0,8},{8,0},{16,24},{24,16},{1,9},{9,1},{17,25},{25,17},{2,10},{10... | collective-permute-start | bytes 3145736 | tf_op jit(solution)/shard_map/ppermute | solution.py:313
  302.3 7.1 %collective-permute-start.13 = (f32[2,128,1024]{2,1,0:T(8,128)}, f32[2,128,1024]{2,1,0:T(8,128)S(1)}, u32[]{:S(2)}, u32[]{:S(2)}) collective-permute-start(f32[2,128,1024]{2,1,0:T(8,128)} %get-tuple-element.110), channel_id=1, source_target_pairs={{0,16},{8,24},{16,0},{24,8},{1,17},{9,25},{17,1},{25,9},{2,18},{10... | collective-permute-start | bytes 3145736 | tf_op jit(solution)/shard_map/ppermute | solution.py:313
  309.4 4.4 %shard_map.87.refs_9_ = f32[512,2048]{1,0:T(8,128)} custom-call(s32[4]{0:T(128)} %get-tuple-element.75.refs_0_, f32[2,128,1024]{2,1,0:T(8,128)} %get-tuple-element.94.refs_0_.refs_1_, f32[2,128,1024]{2,1,0:T(8,128)} %copy-done.3, f32[128,1024]{1,0:T(8,128)} %copy-done.14, ...), custom_call_target="tpu_custom_call", output_to_operand_aliasing={{}: (9, {})} | custom-call | bytes 6291456 | tf_op jit(solution)/shard_map/pallas_call | solution.py:278
  313.8 6.2 %collective-permute-done.12.refs_1_.refs_2_ = f32[2,128,1024]{2,1,0:T(8,128)S(1)} collective-permute-done((f32[2,128,1024]{2,1,0:T(8,128)}, f32[2,128,1024]{2,1,0:T(8,128)S(1)}, u32[]{:S(2)}, u32[]{:S(2)}) %collective-permute-start.12) | collective-permute-done | bytes 1048608 | tf_op jit(solution)/shard_map/ppermute | solution.py:313
  320.0 12.8 %collective-permute-done.13.refs_3_.refs_5_ = f32[2,128,1024]{2,1,0:T(8,128)S(1)} collective-permute-done((f32[2,128,1024]{2,1,0:T(8,128)}, f32[2,128,1024]{2,1,0:T(8,128)S(1)}, u32[]{:S(2)}, u32[]{:S(2)}) %collective-permute-start.13) | collective-permute-done | bytes 1048608 | tf_op jit(solution)/shard_map/ppermute | solution.py:313
  333.8 2.5 shard_map.86
  336.4 9.9 %all-gather.9.cloned.1.call-done = f32[512,2048]{1,0:T(8,128)} async-done(((f32[128,2048]{1,0:T(8,128)}), f32[512,2048]{1,0:T(8,128)}) %all-gather.9.cloned.1.call-update) | async-done | bytes 4194320 | tf_op jit(solution)/shard_map/all_gather | solution.py:311
  349.2 4.4 collective-permute-done.14.other_ref
  353.6 2.0 copy-done.22
  355.5 13.0 %shard_map.89 = (f32[2,128,512]{2,1,0:T(8,128)}, f32[2,128,512]{2,1,0:T(8,128)}, f32[2,128,512]{2,1,0:T(8,128)}, f32[2,128,512]{2,1,0:T(8,128)}) custom-call(s32[1]{0:T(128)} %bitcast.2.core_ref, s32[16]{0:T(128)} %get-tuple-element.76.place_ref, s32[4,2]{1,0:T(4,128)} %copy.15.flag_ref, f32[4,128,2048]{2,1,0:T(8,128)} %bitcast.8, ...), custom_call_target="tpu_custom_call" | custom-call | flops 12884901888 | bytes 16777216 | tf_op jit(solution)/shard_map/pallas_call | solution.py:220
  368.5 8.6 %collective-permute-start.17 = (f32[2,128,512]{2,1,0:T(8,128)}, f32[2,128,512]{2,1,0:T(8,128)S(1)}, u32[]{:S(2)}, u32[]{:S(2)}) collective-permute-start(f32[2,128,512]{2,1,0:T(8,128)} %get-tuple-element.125), channel_id=1, source_target_pairs={{0,8},{8,0},{16,24},{24,16},{1,9},{9,1},{17,25},{25,17},{2,10},{10... | collective-permute-start | bytes 1572872 | tf_op jit(solution)/shard_map/ppermute | solution.py:313
  377.2 16.3 %shard_map.88 = (f32[2,128,512]{2,1,0:T(8,128)}, f32[2,128,512]{2,1,0:T(8,128)}, f32[2,128,512]{2,1,0:T(8,128)}, f32[2,128,512]{2,1,0:T(8,128)}) custom-call(s32[1]{0:T(128)} %bitcast.2.core_ref, s32[16]{0:T(128)} %get-tuple-element.76.place_ref, s32[4,2]{1,0:T(4,128)} %copy.15.flag_ref, f32[4,128,2048]{2,1,0:T(8,128)} %bitcast.9, ...), custom_call_target="tpu_custom_call" | custom-call | flops 12884901888 | bytes 16777216 | tf_op jit(solution)/shard_map/pallas_call | solution.py:220
  393.6 2.0 collective-permute-start.19
  395.6 7.1 %collective-permute-start.20 = (f32[2,128,512]{2,1,0:T(8,128)}, f32[2,128,512]{2,1,0:T(8,128)S(1)}, u32[]{:S(2)}, u32[]{:S(2)}) collective-permute-start(f32[2,128,512]{2,1,0:T(8,128)} %get-tuple-element.129), channel_id=1, source_target_pairs={{0,16},{8,24},{16,0},{24,8},{1,17},{9,25},{17,1},{25,9},{2,18},{10... | collective-permute-start | bytes 1572872 | tf_op jit(solution)/shard_map/ppermute | solution.py:313
  402.7 4.4 %shard_map.90.refs_9_ = f32[512,2048]{1,0:T(8,128)} custom-call(s32[4]{0:T(128)} %get-tuple-element.75.refs_0_, f32[2,128,1024]{2,1,0:T(8,128)} %get-tuple-element.107.refs_0_.refs_1_, f32[2,128,1024]{2,1,0:T(8,128)} %copy-done.1, f32[128,1024]{1,0:T(8,128)} %copy-done.11, ...), custom_call_target="tpu_custom_call", output_to_operand_aliasing={{}: (9, {})} | custom-call | bytes 6291456 | tf_op jit(solution)/shard_map/pallas_call | solution.py:278
  407.1 2.0 shard_map.92
  409.1 1.9 collective-permute-start.24
  411.0 4.4 collective-permute-done.20.refs_3_.refs_5_
  416.2 2.0 shard_map.91
  418.2 3.0 collective-permute-start.21
  423.9 3.3 shard_map.93.refs_9_
  428.7 3.3 shard_map.94
  (84 shorter events, 24.0 us)
Async XLA Ops:
  6.5 97.1 %all-gather.15.cloned.1.call-start = ((), (), s32[]{:S(2)}) async-start(), calls=%async_computation.3 | async-start | bytes 5242880 | tf_op jit(solution)/shard_map/all_gather | solution.py:311
  11.0 4.5 %collective-permute-start = (f32[256,2048]{1,0:T(8,128)}, f32[256,2048]{1,0:T(8,128)S(1)}, u32[]{:S(2)}, u32[]{:S(2)}) collective-permute-start(f32[256,2048]{1,0:T(8,128)} %shard_map.74), channel_id=1, source_target_pairs={{0,1},{1,0},{2,3},{3,2},{4,5},{5,4},{6,7},{7,6},{8,9},{9,8},{10,11... | collective-permute-start | bytes 6291464 | tf_op jit(solution)/shard_map/ppermute | solution.py:307
  15.5 1.3 copy-start
  20.1 164.4 %all-gather.13.cloned.1.call-start = ((), (), s32[]{:S(2)}) async-start(), calls=%async_computation.2 | async-start | bytes 5242880 | tf_op jit(solution)/shard_map/all_gather | solution.py:311
  49.6 54.1 %copy-start.21 = (s32[4,2]{0,1:T(2,128)S(1)}, s32[4,2]{0,1:T(2,128)}, u32[]{:S(2)}) copy-start(s32[4,2]{0,1:T(2,128)} %param.10) | copy-start | bytes 100
  103.7 7.5 %collective-permute-start.1 = (f32[4,128,2048]{2,1,0:T(8,128)}, f32[4,128,2048]{2,1,0:T(8,128)}, u32[]{:S(2)}, u32[]{:S(2)}) collective-permute-start(f32[4,128,2048]{2,1,0:T(8,128)} %bitcast.14), channel_id=1, source_target_pairs={{0,1},{1,0},{2,3},{3,2},{4,5},{5,4},{6,7},{7,6},{8,9},{9,8},{10,11... | collective-permute-start | bytes 12582920 | tf_op jit(solution)/shard_map/ppermute | solution.py:322
  103.7 161.8 %all-gather.11.cloned.1.call-start = ((), (), s32[]{:S(2)}) async-start(), calls=%async_computation.1 | async-start | bytes 5242880 | tf_op jit(solution)/shard_map/all_gather | solution.py:311
  134.0 24.1 %collective-permute-start.2 = (f32[2,128,1024]{2,1,0:T(8,128)}, f32[2,128,1024]{2,1,0:T(8,128)S(1)}, u32[]{:S(2)}, u32[]{:S(2)}) collective-permute-start(f32[2,128,1024]{2,1,0:T(8,128)} %get-tuple-element.84), channel_id=1, source_target_pairs={{0,8},{8,0},{16,24},{24,16},{1,9},{9,1},{17,25},{25,17},{2,10},{10... | collective-permute-start | bytes 3145736 | tf_op jit(solution)/shard_map/ppermute | solution.py:313
  140.4 30.5 %collective-permute-start.3 = (f32[2,128,1024]{2,1,0:T(8,128)}, f32[2,128,1024]{2,1,0:T(8,128)S(1)}, u32[]{:S(2)}, u32[]{:S(2)}) collective-permute-start(f32[2,128,1024]{2,1,0:T(8,128)} %get-tuple-element.86), channel_id=1, source_target_pairs={{0,16},{8,24},{16,0},{24,8},{1,17},{9,25},{17,1},{25,9},{2,18},{10... | collective-permute-start | bytes 3145736 | tf_op jit(solution)/shard_map/ppermute | solution.py:313
  158.1 12.8 %copy-start.5 = (f32[2,128,1024]{2,1,0:T(8,128)}, f32[2,128,1024]{2,1,0:T(8,128)S(1)}, u32[]{:S(2)}) copy-start(f32[2,128,1024]{2,1,0:T(8,128)S(1)} %collective-permute-done.2.refs_1_.refs_2_) | copy-start | bytes 3145732
  170.9 1.0 copy-start.6
  184.6 7.5 %collective-permute-start.4 = (f32[4,128,2048]{2,1,0:T(8,128)}, f32[4,128,2048]{2,1,0:T(8,128)}, u32[]{:S(2)}, u32[]{:S(2)}) collective-permute-start(f32[4,128,2048]{2,1,0:T(8,128)} %bitcast.12), channel_id=1, source_target_pairs={{0,1},{1,0},{2,3},{3,2},{4,5},{5,4},{6,7},{7,6},{8,9},{9,8},{10,11... | collective-permute-start | bytes 12582920 | tf_op jit(solution)/shard_map/ppermute | solution.py:322
  184.6 161.6 %all-gather.9.cloned.1.call-start = ((), (), s32[]{:S(2)}) async-start(), calls=%async_computation | async-start | bytes 5242880 | tf_op jit(solution)/shard_map/all_gather | solution.py:311
  184.8 30.1 %collective-permute-start.5 = (f32[128,1024]{1,0:T(8,128)}, f32[128,1024]{1,0:T(8,128)S(1)}, u32[]{:S(2)}, u32[]{:S(2)}) collective-permute-start(f32[128,1024]{1,0:T(8,128)} %get-tuple-element.87), channel_id=1, source_target_pairs={{0,16},{8,24},{16,0},{24,8},{1,17},{9,25},{17,1},{25,9},{2,18},{10... | collective-permute-start | bytes 1572872 | tf_op jit(solution)/shard_map/ppermute | solution.py:313
  186.4 28.5 %collective-permute-start.6 = (f32[128,1024]{1,0:T(8,128)}, f32[128,1024]{1,0:T(8,128)S(1)}, u32[]{:S(2)}, u32[]{:S(2)}) collective-permute-start(f32[128,1024]{1,0:T(8,128)} %get-tuple-element.88), channel_id=1, source_target_pairs={{0,8},{8,0},{16,24},{24,16},{1,9},{9,1},{17,25},{25,17},{2,10},{10... | collective-permute-start | bytes 1572872 | tf_op jit(solution)/shard_map/ppermute | solution.py:313
  214.9 13.6 %copy-start.13 = (f32[128,1024]{1,0:T(8,128)}, f32[128,1024]{1,0:T(8,128)S(1)}, u32[]{:S(2)}) copy-start(f32[128,1024]{1,0:T(8,128)S(1)} %collective-permute-done.5.refs_3_) | copy-start | bytes 1572868
  214.9 13.6 %copy-start.15 = (f32[128,1024]{1,0:T(8,128)}, f32[128,1024]{1,0:T(8,128)S(1)}, u32[]{:S(2)}) copy-start(f32[128,1024]{1,0:T(8,128)S(1)} %collective-permute-done.6.refs_6_) | copy-start | bytes 1572868
  214.9 24.2 %collective-permute-start.7 = (f32[2,128,1024]{2,1,0:T(8,128)}, f32[2,128,1024]{2,1,0:T(8,128)S(1)}, u32[]{:S(2)}, u32[]{:S(2)}) collective-permute-start(f32[2,128,1024]{2,1,0:T(8,128)} %get-tuple-element.95), channel_id=1, source_target_pairs={{0,8},{8,0},{16,24},{24,16},{1,9},{9,1},{17,25},{25,17},{2,10},{10... | collective-permute-start | bytes 3145736 | tf_op jit(solution)/shard_map/ppermute | solution.py:313
  221.4 30.5 %collective-permute-start.8 = (f32[2,128,1024]{2,1,0:T(8,128)}, f32[2,128,1024]{2,1,0:T(8,128)S(1)}, u32[]{:S(2)}, u32[]{:S(2)}) collective-permute-start(f32[2,128,1024]{2,1,0:T(8,128)} %get-tuple-element.97), channel_id=1, source_target_pairs={{0,16},{8,24},{16,0},{24,8},{1,17},{9,25},{17,1},{25,9},{2,18},{10... | collective-permute-start | bytes 3145736 | tf_op jit(solution)/shard_map/ppermute | solution.py:313
  239.1 12.8 %copy-start.3 = (f32[2,128,1024]{2,1,0:T(8,128)}, f32[2,128,1024]{2,1,0:T(8,128)S(1)}, u32[]{:S(2)}) copy-start(f32[2,128,1024]{2,1,0:T(8,128)S(1)} %collective-permute-done.7.refs_1_.refs_2_) | copy-start | bytes 3145732
  251.9 1.0 copy-start.4
  265.5 7.5 %collective-permute-start.9 = (f32[4,128,2048]{2,1,0:T(8,128)}, f32[4,128,2048]{2,1,0:T(8,128)}, u32[]{:S(2)}, u32[]{:S(2)}) collective-permute-start(f32[4,128,2048]{2,1,0:T(8,128)} %bitcast.10), channel_id=1, source_target_pairs={{0,1},{1,0},{2,3},{3,2},{4,5},{5,4},{6,7},{7,6},{8,9},{9,8},{10,11... | collective-permute-start | bytes 12582920 | tf_op jit(solution)/shard_map/ppermute | solution.py:322
  265.5 30.3 %collective-permute-start.10 = (f32[128,1024]{1,0:T(8,128)}, f32[128,1024]{1,0:T(8,128)S(1)}, u32[]{:S(2)}, u32[]{:S(2)}) collective-permute-start(f32[128,1024]{1,0:T(8,128)} %get-tuple-element.98), channel_id=1, source_target_pairs={{0,16},{8,24},{16,0},{24,8},{1,17},{9,25},{17,1},{25,9},{2,18},{10... | collective-permute-start | bytes 1572872 | tf_op jit(solution)/shard_map/ppermute | solution.py:313
  267.1 28.8 %collective-permute-start.11 = (f32[128,1024]{1,0:T(8,128)}, f32[128,1024]{1,0:T(8,128)S(1)}, u32[]{:S(2)}, u32[]{:S(2)}) collective-permute-start(f32[128,1024]{1,0:T(8,128)} %get-tuple-element.99), channel_id=1, source_target_pairs={{0,8},{8,0},{16,24},{24,16},{1,9},{9,1},{17,25},{25,17},{2,10},{10... | collective-permute-start | bytes 1572872 | tf_op jit(solution)/shard_map/ppermute | solution.py:313
  295.8 13.6 %copy-start.14 = (f32[128,1024]{1,0:T(8,128)}, f32[128,1024]{1,0:T(8,128)S(1)}, u32[]{:S(2)}) copy-start(f32[128,1024]{1,0:T(8,128)S(1)} %collective-permute-done.10.refs_3_) | copy-start | bytes 1572868
  295.8 13.6 %copy-start.16 = (f32[128,1024]{1,0:T(8,128)}, f32[128,1024]{1,0:T(8,128)S(1)}, u32[]{:S(2)}) copy-start(f32[128,1024]{1,0:T(8,128)S(1)} %collective-permute-done.11.refs_6_) | copy-start | bytes 1572868
  295.8 24.2 %collective-permute-start.12 = (f32[2,128,1024]{2,1,0:T(8,128)}, f32[2,128,1024]{2,1,0:T(8,128)S(1)}, u32[]{:S(2)}, u32[]{:S(2)}) collective-permute-start(f32[2,128,1024]{2,1,0:T(8,128)} %get-tuple-element.108), channel_id=1, source_target_pairs={{0,8},{8,0},{16,24},{24,16},{1,9},{9,1},{17,25},{25,17},{2,10},{10... | collective-permute-start | bytes 3145736 | tf_op jit(solution)/shard_map/ppermute | solution.py:313
  302.3 30.5 %collective-permute-start.13 = (f32[2,128,1024]{2,1,0:T(8,128)}, f32[2,128,1024]{2,1,0:T(8,128)S(1)}, u32[]{:S(2)}, u32[]{:S(2)}) collective-permute-start(f32[2,128,1024]{2,1,0:T(8,128)} %get-tuple-element.110), channel_id=1, source_target_pairs={{0,16},{8,24},{16,0},{24,8},{1,17},{9,25},{17,1},{25,9},{2,18},{10... | collective-permute-start | bytes 3145736 | tf_op jit(solution)/shard_map/ppermute | solution.py:313
  320.0 12.8 %copy-start.1 = (f32[2,128,1024]{2,1,0:T(8,128)}, f32[2,128,1024]{2,1,0:T(8,128)S(1)}, u32[]{:S(2)}) copy-start(f32[2,128,1024]{2,1,0:T(8,128)S(1)} %collective-permute-done.12.refs_1_.refs_2_) | copy-start | bytes 3145732
  332.8 1.0 copy-start.2
  346.2 7.4 %collective-permute-start.14 = (f32[4,128,2048]{2,1,0:T(8,128)}, f32[4,128,2048]{2,1,0:T(8,128)S(1)}, u32[]{:S(2)}, u32[]{:S(2)}) collective-permute-start(f32[4,128,2048]{2,1,0:T(8,128)} %bitcast.7), channel_id=1, source_target_pairs={{0,1},{1,0},{2,3},{3,2},{4,5},{5,4},{6,7},{7,6},{8,9},{9,8},{10,11... | collective-permute-start | bytes 12582920 | tf_op jit(solution)/shard_map/ppermute | solution.py:322
  346.2 22.3 %collective-permute-start.15 = (f32[128,1024]{1,0:T(8,128)}, f32[128,1024]{1,0:T(8,128)S(1)}, u32[]{:S(2)}, u32[]{:S(2)}) collective-permute-start(f32[128,1024]{1,0:T(8,128)} %get-tuple-element.111), channel_id=1, source_target_pairs={{0,16},{8,24},{16,0},{24,8},{1,17},{9,25},{17,1},{25,9},{2,18},{10... | collective-permute-start | bytes 1572872 | tf_op jit(solution)/shard_map/ppermute | solution.py:313
  347.7 20.8 %collective-permute-start.16 = (f32[128,1024]{1,0:T(8,128)}, f32[128,1024]{1,0:T(8,128)S(1)}, u32[]{:S(2)}, u32[]{:S(2)}) collective-permute-start(f32[128,1024]{1,0:T(8,128)} %get-tuple-element.112), channel_id=1, source_target_pairs={{0,8},{8,0},{16,24},{24,16},{1,9},{9,1},{17,25},{25,17},{2,10},{10... | collective-permute-start | bytes 1572872 | tf_op jit(solution)/shard_map/ppermute | solution.py:313
  353.6 2.0 copy-start.22
  368.5 25.0 %copy-start.11 = (f32[128,1024]{1,0:T(8,128)}, f32[128,1024]{1,0:T(8,128)S(1)}, u32[]{:S(2)}) copy-start(f32[128,1024]{1,0:T(8,128)S(1)} %collective-permute-done.15.refs_3_) | copy-start | bytes 1572868
  368.5 25.0 %copy-start.12 = (f32[128,1024]{1,0:T(8,128)}, f32[128,1024]{1,0:T(8,128)S(1)}, u32[]{:S(2)}) copy-start(f32[128,1024]{1,0:T(8,128)S(1)} %collective-permute-done.16.refs_6_) | copy-start | bytes 1572868
  368.5 25.0 %collective-permute-start.17 = (f32[2,128,512]{2,1,0:T(8,128)}, f32[2,128,512]{2,1,0:T(8,128)S(1)}, u32[]{:S(2)}, u32[]{:S(2)}) collective-permute-start(f32[2,128,512]{2,1,0:T(8,128)} %get-tuple-element.125), channel_id=1, source_target_pairs={{0,8},{8,0},{16,24},{24,16},{1,9},{9,1},{17,25},{25,17},{2,10},{10... | collective-permute-start | bytes 1572872 | tf_op jit(solution)/shard_map/ppermute | solution.py:313
  377.2 16.4 %collective-permute-start.18 = (f32[2,128,512]{2,1,0:T(8,128)}, f32[2,128,512]{2,1,0:T(8,128)S(1)}, u32[]{:S(2)}, u32[]{:S(2)}) collective-permute-start(f32[2,128,512]{2,1,0:T(8,128)} %get-tuple-element.126), channel_id=1, source_target_pairs={{0,16},{8,24},{16,0},{24,8},{1,17},{9,25},{17,1},{25,9},{2,18},{10... | collective-permute-start | bytes 1572872 | tf_op jit(solution)/shard_map/ppermute | solution.py:313
  393.5 13.6 %copy-start.7 = (f32[2,128,512]{2,1,0:T(8,128)}, f32[2,128,512]{2,1,0:T(8,128)S(1)}, u32[]{:S(2)}) copy-start(f32[2,128,512]{2,1,0:T(8,128)S(1)} %collective-permute-done.17.refs_1_.refs_2_) | copy-start | bytes 1572868
  393.5 13.5 %copy-start.8 = (f32[2,128,512]{2,1,0:T(8,128)}, f32[2,128,512]{2,1,0:T(8,128)S(1)}, u32[]{:S(2)}) copy-start(f32[2,128,512]{2,1,0:T(8,128)S(1)} %collective-permute-done.18.refs_3_.refs_5_) | copy-start | bytes 1572868
  393.6 17.5 %collective-permute-start.19 = (f32[2,128,512]{2,1,0:T(8,128)}, f32[2,128,512]{2,1,0:T(8,128)S(1)}, u32[]{:S(2)}, u32[]{:S(2)}) collective-permute-start(f32[2,128,512]{2,1,0:T(8,128)} %get-tuple-element.128), channel_id=1, source_target_pairs={{0,8},{8,0},{16,24},{24,16},{1,9},{9,1},{17,25},{25,17},{2,10},{10... | collective-permute-start | bytes 1572872 | tf_op jit(solution)/shard_map/ppermute | solution.py:313
  395.6 19.8 %collective-permute-start.20 = (f32[2,128,512]{2,1,0:T(8,128)}, f32[2,128,512]{2,1,0:T(8,128)S(1)}, u32[]{:S(2)}, u32[]{:S(2)}) collective-permute-start(f32[2,128,512]{2,1,0:T(8,128)} %get-tuple-element.129), channel_id=1, source_target_pairs={{0,16},{8,24},{16,0},{24,8},{1,17},{9,25},{17,1},{25,9},{2,18},{10... | collective-permute-start | bytes 1572872 | tf_op jit(solution)/shard_map/ppermute | solution.py:313
  409.1 13.4 %collective-permute-start.23 = (f32[128,512]{1,0:T(8,128)}, f32[128,512]{1,0:T(8,128)S(1)}, u32[]{:S(2)}, u32[]{:S(2)}) collective-permute-start(f32[128,512]{1,0:T(8,128)} %get-tuple-element.142), channel_id=1, source_target_pairs={{0,16},{8,24},{16,0},{24,8},{1,17},{9,25},{17,1},{25,9},{2,18},{10... | collective-permute-start | bytes 786440 | tf_op jit(solution)/shard_map/ppermute | solution.py:313
  409.1 13.4 %collective-permute-start.24 = (f32[128,512]{1,0:T(8,128)}, f32[128,512]{1,0:T(8,128)S(1)}, u32[]{:S(2)}, u32[]{:S(2)}) collective-permute-start(f32[128,512]{1,0:T(8,128)} %get-tuple-element.143), channel_id=1, source_target_pairs={{0,8},{8,0},{16,24},{24,16},{1,9},{9,1},{17,25},{25,17},{2,10},{10... | collective-permute-start | bytes 786440 | tf_op jit(solution)/shard_map/ppermute | solution.py:313
  411.0 4.4 copy-start.9
  415.4 0.8 copy-start.10
  418.2 9.0 %collective-permute-start.21 = (f32[128,512]{1,0:T(8,128)}, f32[128,512]{1,0:T(8,128)S(1)}, u32[]{:S(2)}, u32[]{:S(2)}) collective-permute-start(f32[128,512]{1,0:T(8,128)} %get-tuple-element.136), channel_id=1, source_target_pairs={{0,16},{8,24},{16,0},{24,8},{1,17},{9,25},{17,1},{25,9},{2,18},{10... | collective-permute-start | bytes 786440 | tf_op jit(solution)/shard_map/ppermute | solution.py:313
  421.3 6.6 %collective-permute-start.22 = (f32[128,512]{1,0:T(8,128)}, f32[128,512]{1,0:T(8,128)S(1)}, u32[]{:S(2)}, u32[]{:S(2)}) collective-permute-start(f32[128,512]{1,0:T(8,128)} %get-tuple-element.137), channel_id=1, source_target_pairs={{0,8},{8,0},{16,24},{24,16},{1,9},{9,1},{17,25},{25,17},{2,10},{10... | collective-permute-start | bytes 786440 | tf_op jit(solution)/shard_map/ppermute | solution.py:313
  (4 other events, 2.8 us)
Sparse Core Ops, SparseCore 0:
  20.3 83.3 all-gather.14
  105.2 79.2 all-gather.12
  186.1 79.2 all-gather.10
  266.9 79.2 all-gather.8

commit v3 on v2

--- a/solution.py
+++ b/solution.py
@@ -11,7 +11,9 @@
 TILE = 1024
 TILE_ROWS = 128
 CORES = 2
-VMEM_BYTES = 58 * 1024 * 1024
+VMEM_BYTES = 40 * 1024 * 1024
+COLUMNS = 256
+SMALL = pl.CostEstimate(flops=1, bytes_accessed=1, transcendentals=0)
 CHAINS = 2
 RANKS = (((0, 2), (1, 3)), ((0, 1), (2, 3)))
 
@@ -72,7 +74,8 @@
                 used[z][k] = jnp.maximum(used[z][k], (pick == k).astype(jnp.int32))
             my_pick = jnp.where(chip == z, pick, my_pick)
             slot = jnp.where(target == rank, inverse_ref[z * rounds + pick] % rounds, slot)
-            place_ref[r * chips + z] = target ^ rank
+            distance = (chip + (chips - z)) % chips
+            place_ref[r * chips + distance] = target ^ rank if r == rounds - 1 else target
         pick_ref[r] = my_pick
         slot_ref[r] = slot
 
@@ -146,6 +149,7 @@
             ],
             out_specs=pl.BlockSpec((TILE_ROWS, half), lambda i, core, pick, flags: (0, 0)),
         ),
+        cost_estimate=SMALL,
     )(core, pick, amp_tiles, amplitudes, swapped)
 
 
@@ -168,25 +172,26 @@
         in_specs=[block],
         out_specs=(block, block),
         compiler_params=pltpu.CompilerParams(vmem_limit_bytes=VMEM_BYTES),
-        cost_estimate=pl.CostEstimate(flops=0, bytes_accessed=8 * depth * width, transcendentals=0),
+        cost_estimate=pl.CostEstimate(flops=0, bytes_accessed=16 * depth * width, transcendentals=0),
     )(integrals)
 
 
-def product_kernel(r, first, ranks, core_ref, place_ref, flag_ref, mine_ref, other_ref, high_ref, low_ref, *refs):
-    out_refs, (pair_ref, total_ref) = refs[: 2 * CHAINS], refs[2 * CHAINS :]
+def product_kernel(r, first, ranks, chained, core_ref, place_ref, flag_ref, *refs):
+    amp_refs, (high_ref, low_ref), refs = refs[: CORES * ranks], refs[CORES * ranks :][:2], refs[CORES * ranks + 2 :]
+    out_refs, (pair_ref, total_ref) = refs[:-2], refs[-2:]
     rows = ranks * TILE_ROWS
-    half = mine_ref.shape[2]
+    half = amp_refs[0].shape[1]
     width = high_ref.shape[1]
     step = pl.program_id(0)
 
     @pl.when(step == 0)
     def _():
-        for z in range(ranks):
-            at = pl.multiple_of(place_ref[r * ranks + z] * TILE_ROWS, TILE_ROWS)
-            for away, amp_ref in enumerate((mine_ref, other_ref)):
-                value = amp_ref[z]
+        for away in range(CORES):
+            columns = pl.ds(pl.multiple_of((core_ref[0] ^ away) * half, half), half)
+            for d in range(ranks):
+                at = pl.multiple_of(place_ref[r * ranks + d] * TILE_ROWS, TILE_ROWS)
+                value = amp_refs[away * ranks + d][...]
                 high = value.astype(jnp.bfloat16)
-                columns = pl.ds(pl.multiple_of((core_ref[0] ^ away) * half, half), half)
                 pair_ref[pl.ds(at, TILE_ROWS), columns] = high
                 pair_ref[pl.ds(rows + at, TILE_ROWS), columns] = (value - high.astype(jnp.float32)).astype(
                     jnp.bfloat16
@@ -200,6 +205,9 @@
             both = jnp.dot(pair_ref[:, deep], high_ref[deep, :], preferred_element_type=jnp.float32)
             cross = jnp.dot(pair_ref[:rows, deep], low_ref[deep, :], preferred_element_type=jnp.float32)
             total_ref[...] += both[:rows] + (both[rows:] + cross)
+    if not chained:
+        out_refs[0][...] = total_ref[...]
+        return
     share = width // CHAINS
     for chain, (kept, sent) in enumerate(RANKS):
         columns = pl.ds(chain * share, share)
@@ -208,23 +216,29 @@
                 ref[i] = total_ref[pl.ds(peer * TILE_ROWS, TILE_ROWS), columns]
 
 
-def product(r, piece, pieces, core, place, int_tiles, mine, other, high, low):
-    ranks = mine.shape[0]
+def product(r, piece, pieces, chained, core, place, int_tiles, mine, other, high, low):
+    ranks = len(mine)
     depth, width = high.shape
     rows = ranks * TILE_ROWS
-    columns = TILE // 2
+    columns = COLUMNS
     share = columns // CHAINS
     steps = width // columns // pieces
-    amp = pl.BlockSpec(mine.shape, lambda i, *_: (0, 0, 0), pipeline_mode=pl.Buffered(1))
+    amp = pl.BlockSpec(mine[0].shape, lambda i, *_: (0, 0), pipeline_mode=pl.Buffered(1))
     integral = pl.BlockSpec((depth, columns), lambda i, *_: (0, piece * steps + i))
-    return pl.pallas_call(
-        functools.partial(product_kernel, r, piece * steps, ranks),
-        out_shape=[jax.ShapeDtypeStruct((2, TILE_ROWS, share * steps), jnp.float32)] * (2 * CHAINS),
+    if chained:
+        out_shape = [jax.ShapeDtypeStruct((2, TILE_ROWS, share * steps), jnp.float32)] * (2 * CHAINS)
+        out_specs = [pl.BlockSpec((2, TILE_ROWS, share), lambda i, *_: (0, 0, i))] * (2 * CHAINS)
+    else:
+        out_shape = [jax.ShapeDtypeStruct((rows, columns * steps), jnp.float32)]
+        out_specs = [pl.BlockSpec((rows, columns), lambda i, *_: (0, i))]
+    return pl.pallas_call(
+        functools.partial(product_kernel, r, piece * steps, ranks, chained),
+        out_shape=out_shape,
         grid_spec=pltpu.PrefetchScalarGridSpec(
             num_scalar_prefetch=3,
             grid=(steps,),
-            in_specs=[amp, amp, integral, integral],
-            out_specs=[pl.BlockSpec((2, TILE_ROWS, share), lambda i, *_: (0, 0, i))] * (2 * CHAINS),
+            in_specs=[amp] * (CORES * ranks) + [integral, integral],
+            out_specs=out_specs,
             scratch_shapes=[
                 pltpu.VMEM((2 * rows, depth), jnp.bfloat16),
                 pltpu.VMEM((rows, columns), jnp.float32),
@@ -232,9 +246,9 @@
         ),
         compiler_params=pltpu.CompilerParams(vmem_limit_bytes=VMEM_BYTES),
         cost_estimate=pl.CostEstimate(
-            flops=6 * rows * depth * width // pieces, bytes_accessed=4 * depth * width // pieces, transcendentals=0
-        ),
-    )(core, place, int_tiles, mine, other, high, low)
+            flops=6 * rows * depth * width, bytes_accessed=4 * depth * width, transcendentals=0
+        ),
+    )(core, place, int_tiles, *mine, *other, high, low)
 
 
 def relay_kernel(*refs):
@@ -276,7 +290,7 @@
     owned = pl.BlockSpec((TILE_ROWS, width), lambda i, slot: (slot[r], piece))
     before = [] if update is None else [update]
     return pl.pallas_call(
-        functools.partial(finish_kernel, TILE // 2),
+        functools.partial(finish_kernel, COLUMNS),
         out_shape=jax.ShapeDtypeStruct(other_terms.shape, jnp.float32),
         grid_spec=pltpu.PrefetchScalarGridSpec(
             num_scalar_prefetch=1,
@@ -287,7 +301,7 @@
             out_specs=owned,
         ),
         input_output_aliases={3 * CHAINS + 3: 0} if before else {},
-        cost_estimate=pl.CostEstimate(flops=0, bytes_accessed=24 * TILE_ROWS * width, transcendentals=0),
+        cost_estimate=SMALL,
     )(
         slot,
         *[array for chain in zip(kept, heard, relayed) for array in chain],
@@ -297,50 +311,87 @@
     )
 
 
+def settle_kernel(slot_ref, owned_ref, term_ref, denominator_ref, *refs):
+    refs[-1][...] = (owned_ref[...] + term_ref[...]) / denominator_ref[...]
+
+
+def settle(r, slot, owned, other_terms, denominators, update):
+    width = owned.shape[1]
+    columns = min(TILE, width)
+    here = pl.BlockSpec((TILE_ROWS, columns), lambda i, slot: (slot[r], i))
+    before = [] if update is None else [update]
+    return pl.pallas_call(
+        settle_kernel,
+        out_shape=jax.ShapeDtypeStruct(other_terms.shape, jnp.float32),
+        grid_spec=pltpu.PrefetchScalarGridSpec(
+            num_scalar_prefetch=1,
+            grid=(width // columns,),
+            in_specs=[pl.BlockSpec((TILE_ROWS, columns), lambda i, slot: (0, i)), here, here]
+            + [pl.BlockSpec(memory_space=pl.ANY)] * len(before),
+            out_specs=here,
+        ),
+        input_output_aliases={4: 0} if before else {},
+        cost_estimate=SMALL,
+    )(slot, owned, other_terms, denominators, *before)
+
+
 def in_rounds(chips, rounds, amplitudes, amp_tiles, integrals, int_tiles, owner_tiles, other_terms, denominators):
     rank = lax.axis_index("cd").astype(jnp.int32)
     spot = lax.axis_index("ab").astype(jnp.int32)
     core = (spot % CORES).reshape(1)
     spots = chips * CORES
-    siblings = [(i, i ^ 1) for i in range(spots)]
-    same_core = [list(range(i, spots, CORES)) for i in range(CORES)]
-    swapped = lax.ppermute(other_half(core, amp_tiles, amplitudes), "ab", siblings)
+
+    def across(array):
+        return lax.ppermute(array, "ab", [(i, i ^ 1) for i in range(spots)])
+
+    def shifts(array):
+        return [
+            lax.ppermute(array, "ab", [(i, (i + CORES * d) % spots) for i in range(spots)]) for d in range(1, chips)
+        ]
+
+    def swap(sent, peers):
+        return [lax.ppermute(array, "cd", [(c, c ^ peer) for c in range(chips)]) for array, peer in zip(sent, peers)]
+
+    swapped = across(other_half(core, amp_tiles, amplitudes))
     pick, place, slot = plan(owner_tiles, jnp.stack([rank, spot // CORES]), chips, rounds)
     high, low = split(integrals)
-    owns = [pack(r, core, pick, amp_tiles, amplitudes, swapped) for r in range(rounds)]
-    gathered = [lax.all_gather(own, "ab", axis=0, axis_index_groups=same_core) for own in owns]
-    def swap(sent, peers):
-        return [lax.ppermute(array, "cd", [(c, c ^ peer) for c in range(chips)]) for array, peer in zip(sent, peers)]
-
+    owns = [pack(0, core, pick, amp_tiles, amplitudes, swapped)]
+    pick, high, low = lax.optimization_barrier((pick, high, low))
+    owns += [pack(r, core, pick, amp_tiles, amplitudes, swapped) for r in range(1, rounds)]
     terms = (other_terms, denominators)
-    update = waiting = None
+    last = rounds - 1
+    update = owned = None
+    arrived = shifts(owns[0])
     for r in range(rounds):
         if r == 0:
-            mine, high, low, *_ = lax.optimization_barrier((gathered[r], high, low, *owns))
+            arrived, owns, high, low = lax.optimization_barrier((arrived, owns, high, low))
         else:
-            mine, onward, update = lax.optimization_barrier((gathered[r], onward, update))
-        other = lax.ppermute(mine, "ab", siblings)
-        pieces = 2 if r == rounds - 1 else 1
+            arrived, parts, update = lax.optimization_barrier((arrived, parts, update))
+        mine = [owns[r], *arrived]
+        if r < last:
+            begin, arrived = lax.optimization_barrier((owns[r + 1], arrived))
+            following = shifts(begin)
+        other = [*map(across, mine)]
+        pieces = 1 if r < last else 2
         sums = []
         for piece in range(pieces):
-            parts = product(r, piece, pieces, core, place, int_tiles, mine, other, high, low)
-            if waiting is not None:
-                parts, relayed = lax.optimization_barrier((parts, waiting[-1]))
-                update = finish(*waiting[:-1], relayed, *terms, update)
-                waiting = None
+            parts = product(r, piece, pieces, r == last, core, place, int_tiles, mine, other, high, low)
             if piece > 0:
                 parts, heard = lax.optimization_barrier((parts, sums[-1][1]))
                 sums[-1] = (sums[-1][0], heard)
-            sums.append((parts[0::2], swap(parts[1::2], (1, 2))))
-        for piece, (kept, heard) in enumerate(sums):
-            if piece > 0:
-                heard, update = lax.optimization_barrier((heard, update))
-            onward = relay(kept, heard)
-            relayed = swap(onward, (2, 1))
-            if piece < pieces - 1 or r == rounds - 1:
-                sums[piece] = (r, piece, slot, kept, heard, relayed)
-            else:
-                waiting = (r, piece, slot, kept, heard, relayed)
+            elif r > 0:
+                parts, owned = lax.optimization_barrier((parts, owned))
+                update = settle(r - 1, slot, owned, *terms, update)
+            if r == last:
+                sums.append((parts[0::2], swap(parts[1::2], (1, 2))))
+        if r < last:
+            owned = lax.psum_scatter(parts[0], "cd", scatter_dimension=0, tiled=True)
+            arrived = following
+    for piece, (kept, heard) in enumerate(sums):
+        if piece > 0:
+            heard, update = lax.optimization_barrier((heard, update))
+        onward = relay(kept, heard)
+        sums[piece] = (last, piece, slot, kept, heard, swap(onward, (2, 1)))
     for ready in sums:
         update = finish(*ready, *terms, update)
     return update

time: 439 us -> 600 us (1.37)
  the two profiles are of different devices: /device:TPU:0 before, /device:TPU:24 now
where the time goes in v3:
time: 600 us; the launch traced here: 594 us
  waiting for transfers between devices  297 us (50%)
  Pallas kernels  171 us (28%)
  starting transfers between devices  85.2 us (14%)
  local copies, waits for them, and re-layouts  25.9 us (4%)
  between operations  13.3 us (2%)
    ppermute x12, waiting for transfers between devices, shifts(): lax.ppermute(array, 'ab', [(i, (i + CORES * d) % spots) for i in range(sp...  271 us
    pallas_call x5, Pallas kernels, product(): pl.pallas_call(functools.partial(product_kernel, r, piece * steps, ranks,...  108 us
    ppermute x17, starting transfers between devices, across(): return lax.ppermute(array, 'ab', [(i, i ^ 1) for i in range(spots)])  56.1 us
    unnamed x57, local copies, waits for them, and re-layouts  25.9 us
    ppermute x17, waiting for transfers between devices, across(): return lax.ppermute(array, 'ab', [(i, i ^ 1) for i in range(spots)])  22.8 us
    pallas_call x1, Pallas kernels, split(): pl.pallas_call(split_kernel, out_shape=(half, half), grid=(depth // rows,...  22.5 us
    ppermute x8, starting transfers between devices, swap(): lax.ppermute(array, 'cd', [(c, c ^ peer) for c in range(chips)])  15.3 us
    ppermute x12, starting transfers between devices, shifts(): lax.ppermute(array, 'ab', [(i, (i + CORES * d) % spots) for i in range(sp...  13.7 us
  transfers between devices with their start and end apart: 40, of which 23 were waited for; matrix products, arithmetic and copies ran while one was open for 0% of the time, Pallas kernels for 23%

profile of v3, /device:TPU:24, one launch (start us, length us, event | category | flops | bytes accessed | tf_op | source)
XLA Modules:
  0.0 593.6 jit_solution(1566228174170123534)
XLA Ops:
  6.5 4.5 shard_map.74
  11.6 1.9 shard_map.73
  13.5 1.9 collective-permute-done.swapped_ref
  16.7 3.3 shard_map.75.refs_0_
  20.0 1.9 collective-permute-start.2
  22.4 22.5 %shard_map.76 = (bf16[4096,2048]{1,0:T(8,128)(2,1)}, bf16[4096,2048]{1,0:T(8,128)(2,1)}) custom-call(f32[4096,2048]{1,0:T(8,128)} %value_ref.1), custom_call_target="tpu_custom_call" | custom-call | bytes 134217728 | tf_op jit(solution)/shard_map/pallas_call | solution.py:168
  44.9 3.3 shard_map.79.refs_0_
  48.2 3.3 shard_map.78.refs_0_
  51.5 3.4 shard_map.77.refs_0_
  54.9 57.8 %collective-permute-done.2.refs_2_ = f32[128,2048]{1,0:T(8,128)S(1)} collective-permute-done((f32[128,2048]{1,0:T(8,128)}, f32[128,2048]{1,0:T(8,128)S(1)}, u32[]{:S(2)}, u32[]{:S(2)}) %collective-permute-start.2) | collective-permute-done | bytes 1048608 | tf_op jit(solution)/shard_map/ppermute | solution.py:349
  113.9 2.6 collective-permute-done.10.refs_7_
  120.0 26.4 %shard_map.80 = f32[512,2048]{1,0:T(8,128)S(1)} custom-call(s32[1]{0:T(128)} %bitcast.2.core_ref, s32[16]{0:T(128)S(1)} %copy-done.19, s32[4,2]{1,0:T(4,128)S(1)} %copy.15.flag_ref, f32[128,2048]{1,0:T(8,128)S(1)} %copy-done.10, f32[128,2048]{1,0:T(8,128)S(1)} %collective-permute-done.1.refs_1_, f32[128,2048]{1,0:T(8,128)S(1)} %collective-permute-done.2.refs_2_, ...), custom_call_target="tpu_custom_call" | custom-call | flops 25769803776 | bytes 33554432 | tf_op jit(solution)/shard_map/pallas_call | solution.py:234
  146.5 2.0 copy-done.1
  149.7 4.7 collective-permute-start.5
  154.4 9.4 %collective-permute-start.14 = (f32[128,2048]{1,0:T(8,128)S(1)}, f32[128,2048]{1,0:T(8,128)S(1)}, u32[]{:S(2)}, u32[]{:S(2)}) collective-permute-start(f32[128,2048]{1,0:T(8,128)S(1)} %copy-done.9), channel_id=1, source_target_pairs={{0,1},{1,0},{2,3},{3,2},{4,5},{5,4},{6,7},{7,6},{8,9},{9,8},{10,11... | collective-permute-start | bytes 3145736 | tf_op jit(solution)/shard_map/ppermute | solution.py:345
  163.8 11.4 %collective-permute-done.4.refs_1_ = f32[128,2048]{1,0:T(8,128)S(1)} collective-permute-done((f32[128,2048]{1,0:T(8,128)S(1)}, f32[128,2048]{1,0:T(8,128)S(1)}, u32[]{:S(2)}, u32[]{:S(2)}) %collective-permute-start.4) | collective-permute-done | bytes 1048608 | tf_op jit(solution)/shard_map/ppermute | solution.py:349
  175.2 62.9 %collective-permute-done.5.refs_2_ = f32[128,2048]{1,0:T(8,128)S(1)} collective-permute-done((f32[128,2048]{1,0:T(8,128)S(1)}, f32[128,2048]{1,0:T(8,128)S(1)}, u32[]{:S(2)}, u32[]{:S(2)}) %collective-permute-start.5) | collective-permute-done | bytes 1048608 | tf_op jit(solution)/shard_map/ppermute | solution.py:349
  238.1 7.5 %collective-permute-start.15 = (f32[128,2048]{1,0:T(8,128)S(1)}, f32[128,2048]{1,0:T(8,128)S(1)}, u32[]{:S(2)}, u32[]{:S(2)}) collective-permute-start(f32[128,2048]{1,0:T(8,128)S(1)} %collective-permute-done.4.refs_1_), channel_id=1, source_target_pairs={{0,1},{1,0},{2,3},{3,2},{4,5},{5,4},{6,7},{7,6},{8,9},{9,8},{10,11... | collective-permute-start | bytes 3145736 | tf_op jit(solution)/shard_map/ppermute | solution.py:345
  250.9 24.9 %shard_map.81 = f32[512,2048]{1,0:T(8,128)S(1)} custom-call(s32[1]{0:T(128)} %bitcast.2.core_ref, s32[16]{0:T(128)S(1)} %copy-done.19, s32[4,2]{1,0:T(4,128)S(1)} %copy.15.flag_ref, f32[128,2048]{1,0:T(8,128)S(1)} %copy-done.9, f32[128,2048]{1,0:T(8,128)S(1)} %collective-permute-done.4.refs_1_, f32[128,2048]{1,0:T(8,128)S(1)} %collective-permute-done.5.refs_2_, ...), custom_call_target="tpu_custom_call" | custom-call | flops 25769803776 | bytes 33554432 | tf_op jit(solution)/shard_map/pallas_call | solution.py:234
  275.8 2.0 copy-done
  278.9 2.0 collective-permute-start.12
  281.0 10.7 %collective-permute-start.21 = (f32[128,2048]{1,0:T(8,128)S(1)}, f32[128,2048]{1,0:T(8,128)}, u32[]{:S(2)}, u32[]{:S(2)}) collective-permute-start(f32[128,2048]{1,0:T(8,128)S(1)} %copy-done.8), channel_id=1, source_target_pairs={{0,1},{1,0},{2,3},{3,2},{4,5},{5,4},{6,7},{7,6},{8,9},{9,8},{10,11... | collective-permute-start | bytes 3145736 | tf_op jit(solution)/shard_map/ppermute | solution.py:345
  291.7 3.7 shard_map.82.refs_0_
  295.4 7.7 %collective-permute-done.11.refs_1_ = f32[128,2048]{1,0:T(8,128)S(1)} collective-permute-done((f32[128,2048]{1,0:T(8,128)S(1)}, f32[128,2048]{1,0:T(8,128)S(1)}, u32[]{:S(2)}, u32[]{:S(2)}) %collective-permute-start.11) | collective-permute-done | bytes 1048608 | tf_op jit(solution)/shard_map/ppermute | solution.py:349
  303.1 60.3 %collective-permute-done.12.refs_2_ = f32[128,2048]{1,0:T(8,128)S(1)} collective-permute-done((f32[128,2048]{1,0:T(8,128)S(1)}, f32[128,2048]{1,0:T(8,128)S(1)}, u32[]{:S(2)}, u32[]{:S(2)}) %collective-permute-start.12) | collective-permute-done | bytes 1048608 | tf_op jit(solution)/shard_map/ppermute | solution.py:349
  363.4 8.8 %collective-permute-start.22 = (f32[128,2048]{1,0:T(8,128)S(1)}, f32[128,2048]{1,0:T(8,128)S(1)}, u32[]{:S(2)}, u32[]{:S(2)}) collective-permute-start(f32[128,2048]{1,0:T(8,128)S(1)} %collective-permute-done.11.refs_1_), channel_id=1, source_target_pairs={{0,1},{1,0},{2,3},{3,2},{4,5},{5,4},{6,7},{7,6},{8,9},{9,8},{10,11... | collective-permute-start | bytes 3145736 | tf_op jit(solution)/shard_map/ppermute | solution.py:345
  372.7 1.8 collective-permute-done.22.refs_5_
  374.4 3.0 collective-permute-done.23.refs_6_
  377.6 25.5 %shard_map.83 = f32[512,2048]{1,0:T(8,128)S(1)} custom-call(s32[1]{0:T(128)} %bitcast.2.core_ref, s32[16]{0:T(128)S(1)} %copy-done.19, s32[4,2]{1,0:T(4,128)S(1)} %copy.15.flag_ref, f32[128,2048]{1,0:T(8,128)S(1)} %copy-done.8, f32[128,2048]{1,0:T(8,128)S(1)} %collective-permute-done.11.refs_1_, f32[128,2048]{1,0:T(8,128)S(1)} %collective-permute-done.12.refs_2_, ...), custom_call_target="tpu_custom_call" | custom-call | flops 25769803776 | bytes 33554432 | tf_op jit(solution)/shard_map/pallas_call | solution.py:234
  403.1 2.0 copy-done.2
  406.4 4.7 collective-permute-start.19
  411.1 9.5 %collective-permute-start.25 = (f32[128,2048]{1,0:T(8,128)S(1)}, f32[128,2048]{1,0:T(8,128)}, u32[]{:S(2)}, u32[]{:S(2)}) collective-permute-start(f32[128,2048]{1,0:T(8,128)S(1)} %copy-done.7), channel_id=1, source_target_pairs={{0,1},{1,0},{2,3},{3,2},{4,5},{5,4},{6,7},{7,6},{8,9},{9,8},{10,11... | collective-permute-start | bytes 3145736 | tf_op jit(solution)/shard_map/ppermute | solution.py:345
  420.6 3.7 shard_map.84.refs_0_
  424.3 7.4 %collective-permute-done.18.refs_1_ = f32[128,2048]{1,0:T(8,128)S(1)} collective-permute-done((f32[128,2048]{1,0:T(8,128)S(1)}, f32[128,2048]{1,0:T(8,128)S(1)}, u32[]{:S(2)}, u32[]{:S(2)}) %collective-permute-start.18) | collective-permute-done | bytes 1048608 | tf_op jit(solution)/shard_map/ppermute | solution.py:349
  431.8 63.0 %collective-permute-done.19.refs_2_ = f32[128,2048]{1,0:T(8,128)S(1)} collective-permute-done((f32[128,2048]{1,0:T(8,128)S(1)}, f32[128,2048]{1,0:T(8,128)S(1)}, u32[]{:S(2)}, u32[]{:S(2)}) %collective-permute-start.19) | collective-permute-done | bytes 1048608 | tf_op jit(solution)/shard_map/ppermute | solution.py:349
  494.8 7.6 %collective-permute-start.26 = (f32[128,2048]{1,0:T(8,128)S(1)}, f32[128,2048]{1,0:T(8,128)S(1)}, u32[]{:S(2)}, u32[]{:S(2)}) collective-permute-start(f32[128,2048]{1,0:T(8,128)S(1)} %collective-permute-done.18.refs_1_), channel_id=1, source_target_pairs={{0,1},{1,0},{2,3},{3,2},{4,5},{5,4},{6,7},{7,6},{8,9},{9,8},{10,11... | collective-permute-start | bytes 3145736 | tf_op jit(solution)/shard_map/ppermute | solution.py:345
  504.6 3.0 collective-permute-done.27.refs_6_
  507.8 17.0 %shard_map.86 = (f32[2,128,512]{2,1,0:T(8,128)S(1)}, f32[2,128,512]{2,1,0:T(8,128)S(1)}, f32[2,128,512]{2,1,0:T(8,128)S(1)}, f32[2,128,512]{2,1,0:T(8,128)S(1)}) custom-call(s32[1]{0:T(128)} %bitcast.2.core_ref, s32[16]{0:T(128)S(1)} %copy-done.19, s32[4,2]{1,0:T(4,128)S(1)} %copy.15.flag_ref, f32[128,2048]{1,0:T(8,128)S(1)} %copy-done.7, ...), custom_call_target="tpu_custom_call" | custom-call | flops 25769803776 | bytes 33554432 | tf_op jit(solution)/shard_map/pallas_call | solution.py:234
  536.1 14.0 %shard_map.85 = (f32[2,128,512]{2,1,0:T(8,128)S(1)}, f32[2,128,512]{2,1,0:T(8,128)}, f32[2,128,512]{2,1,0:T(8,128)S(1)}, f32[2,128,512]{2,1,0:T(8,128)}) custom-call(s32[1]{0:T(128)} %bitcast.2.core_ref, s32[16]{0:T(128)S(1)} %copy-done.19, s32[4,2]{1,0:T(4,128)S(1)} %copy.15.flag_ref, f32[128,2048]{1,0:T(8,128)S(1)} %copy-done.7, ...), custom_call_target="tpu_custom_call" | custom-call | flops 25769803776 | bytes 33554432 | tf_op jit(solution)/shard_map/pallas_call | solution.py:234
  551.7 4.2 collective-permute-start.31
  555.9 5.9 collective-permute-start.32
  561.8 3.4 shard_map.87.refs_9_
  565.2 2.0 shard_map.89
  568.8 2.3 collective-permute-done.32.refs_3_.refs_5_
  572.0 2.0 shard_map.88
  575.6 2.0 collective-permute-start.34
  579.0 3.3 shard_map.90.refs_9_
  583.7 3.3 shard_map.91
  (112 shorter events, 38.9 us)
Async XLA Ops:
  6.5 271.2 %reduce-scatter.4.cloned.1.call-start = ((), (), s32[]{:S(2)}) async-start(), calls=%async_computation.3 | async-start | bytes 5242880 | tf_op jit(solution)/shard_map/reduce_scatter | solution.py:388
  11.0 4.4 collective-permute-start
  15.4 1.3 copy-start.20
  20.0 34.9 %collective-permute-start.1 = (f32[128,2048]{1,0:T(8,128)}, f32[128,2048]{1,0:T(8,128)S(1)}, u32[]{:S(2)}, u32[]{:S(2)}) collective-permute-start(f32[128,2048]{1,0:T(8,128)} %shard_map.75.refs_0_), channel_id=1, source_target_pairs={{0,2},{1,3},{2,4},{3,5},{4,6},{5,7},{6,0},{7,1},{8,10},{9,11},{10,... | collective-permute-start | bytes 3145736 | tf_op jit(solution)/shard_map/ppermute | solution.py:349
  20.0 92.7 %collective-permute-start.2 = (f32[128,2048]{1,0:T(8,128)}, f32[128,2048]{1,0:T(8,128)S(1)}, u32[]{:S(2)}, u32[]{:S(2)}) collective-permute-start(f32[128,2048]{1,0:T(8,128)} %shard_map.75.refs_0_), channel_id=1, source_target_pairs={{0,4},{1,5},{2,6},{3,7},{4,0},{5,1},{6,2},{7,3},{8,12},{9,13},{10,... | collective-permute-start | bytes 3145736 | tf_op jit(solution)/shard_map/ppermute | solution.py:349
  21.9 90.8 %collective-permute-start.3 = (f32[128,2048]{1,0:T(8,128)}, f32[128,2048]{1,0:T(8,128)}, u32[]{:S(2)}, u32[]{:S(2)}) collective-permute-start(f32[128,2048]{1,0:T(8,128)} %shard_map.75.refs_0_), channel_id=1, source_target_pairs={{0,6},{1,7},{2,0},{3,1},{4,2},{5,3},{6,4},{7,5},{8,14},{9,15},{10,... | collective-permute-start | bytes 3145736 | tf_op jit(solution)/shard_map/ppermute | solution.py:349
  51.5 61.2 %copy-start.10 = (f32[128,2048]{1,0:T(8,128)S(1)}, f32[128,2048]{1,0:T(8,128)}, u32[]{:S(2)}) copy-start(f32[128,2048]{1,0:T(8,128)} %shard_map.75.refs_0_) | copy-start | bytes 3145732
  51.5 62.2 %copy-start.27 = (s32[4,2]{0,1:T(2,128)S(1)}, s32[4,2]{0,1:T(2,128)}, u32[]{:S(2)}) copy-start(s32[4,2]{0,1:T(2,128)} %param.10) | copy-start | bytes 100
  51.5 68.5 %copy-start.19 = (s32[16]{0:T(128)S(1)}, s32[16]{0:T(128)}, u32[]{:S(2)}) copy-start(s32[16]{0:T(128)} %get-tuple-element.67.place_ref) | copy-start | bytes 196
  112.7 3.8 collective-permute-start.10
  112.7 4.3 collective-permute-start.7
  113.2 5.3 collective-permute-start.8
  113.3 6.7 %collective-permute-start.9 = (f32[128,2048]{1,0:T(8,128)S(1)}, f32[128,2048]{1,0:T(8,128)}, u32[]{:S(2)}, u32[]{:S(2)}) collective-permute-start(f32[128,2048]{1,0:T(8,128)S(1)} %collective-permute-done.2.refs_2_), channel_id=1, source_target_pairs={{0,1},{1,0},{2,3},{3,2},{4,5},{5,4},{6,7},{7,6},{8,9},{9,8},{10,11... | collective-permute-start | bytes 3145736 | tf_op jit(solution)/shard_map/ppermute | solution.py:345
  146.4 2.0 copy-start.1
  148.5 256.7 %reduce-scatter.6.cloned.1.call-start = ((), (), s32[]{:S(2)}) async-start(), calls=%async_computation.4 | async-start | bytes 5242880 | tf_op jit(solution)/shard_map/reduce_scatter | solution.py:388
  149.7 25.6 %collective-permute-start.4 = (f32[128,2048]{1,0:T(8,128)S(1)}, f32[128,2048]{1,0:T(8,128)S(1)}, u32[]{:S(2)}, u32[]{:S(2)}) collective-permute-start(f32[128,2048]{1,0:T(8,128)S(1)} %copy-done.9), channel_id=1, source_target_pairs={{0,2},{1,3},{2,4},{3,5},{4,6},{5,7},{6,0},{7,1},{8,10},{9,11},{10,... | collective-permute-start | bytes 3145736 | tf_op jit(solution)/shard_map/ppermute | solution.py:349
  149.7 88.4 %collective-permute-start.5 = (f32[128,2048]{1,0:T(8,128)S(1)}, f32[128,2048]{1,0:T(8,128)S(1)}, u32[]{:S(2)}, u32[]{:S(2)}) collective-permute-start(f32[128,2048]{1,0:T(8,128)S(1)} %copy-done.9), channel_id=1, source_target_pairs={{0,4},{1,5},{2,6},{3,7},{4,0},{5,1},{6,2},{7,3},{8,12},{9,13},{10,... | collective-permute-start | bytes 3145736 | tf_op jit(solution)/shard_map/ppermute | solution.py:349
  154.3 83.8 %collective-permute-start.6 = (f32[128,2048]{1,0:T(8,128)S(1)}, f32[128,2048]{1,0:T(8,128)S(1)}, u32[]{:S(2)}, u32[]{:S(2)}) collective-permute-start(f32[128,2048]{1,0:T(8,128)S(1)} %copy-done.9), channel_id=1, source_target_pairs={{0,6},{1,7},{2,0},{3,1},{4,2},{5,3},{6,4},{7,5},{8,14},{9,15},{10,... | collective-permute-start | bytes 3145736 | tf_op jit(solution)/shard_map/ppermute | solution.py:349
  154.4 91.8 %collective-permute-start.14 = (f32[128,2048]{1,0:T(8,128)S(1)}, f32[128,2048]{1,0:T(8,128)S(1)}, u32[]{:S(2)}, u32[]{:S(2)}) collective-permute-start(f32[128,2048]{1,0:T(8,128)S(1)} %copy-done.9), channel_id=1, source_target_pairs={{0,1},{1,0},{2,3},{3,2},{4,5},{5,4},{6,7},{7,6},{8,9},{9,8},{10,11... | collective-permute-start | bytes 3145736 | tf_op jit(solution)/shard_map/ppermute | solution.py:345
  238.1 9.8 %collective-permute-start.15 = (f32[128,2048]{1,0:T(8,128)S(1)}, f32[128,2048]{1,0:T(8,128)S(1)}, u32[]{:S(2)}, u32[]{:S(2)}) collective-permute-start(f32[128,2048]{1,0:T(8,128)S(1)} %collective-permute-done.4.refs_1_), channel_id=1, source_target_pairs={{0,1},{1,0},{2,3},{3,2},{4,5},{5,4},{6,7},{7,6},{8,9},{9,8},{10,11... | collective-permute-start | bytes 3145736 | tf_op jit(solution)/shard_map/ppermute | solution.py:345
  245.6 3.8 collective-permute-start.16
  245.6 5.3 collective-permute-start.17
  275.7 2.0 copy-start
  277.7 253.2 %reduce-scatter.8.cloned.1.call-start = ((), (), s32[]{:S(2)}) async-start(), calls=%async_computation.5 | async-start | bytes 5242880 | tf_op jit(solution)/shard_map/reduce_scatter | solution.py:388
  278.9 24.1 %collective-permute-start.11 = (f32[128,2048]{1,0:T(8,128)S(1)}, f32[128,2048]{1,0:T(8,128)S(1)}, u32[]{:S(2)}, u32[]{:S(2)}) collective-permute-start(f32[128,2048]{1,0:T(8,128)S(1)} %copy-done.8), channel_id=1, source_target_pairs={{0,2},{1,3},{2,4},{3,5},{4,6},{5,7},{6,0},{7,1},{8,10},{9,11},{10,... | collective-permute-start | bytes 3145736 | tf_op jit(solution)/shard_map/ppermute | solution.py:349
  278.9 84.4 %collective-permute-start.12 = (f32[128,2048]{1,0:T(8,128)S(1)}, f32[128,2048]{1,0:T(8,128)S(1)}, u32[]{:S(2)}, u32[]{:S(2)}) collective-permute-start(f32[128,2048]{1,0:T(8,128)S(1)} %copy-done.8), channel_id=1, source_target_pairs={{0,4},{1,5},{2,6},{3,7},{4,0},{5,1},{6,2},{7,3},{8,12},{9,13},{10,... | collective-permute-start | bytes 3145736 | tf_op jit(solution)/shard_map/ppermute | solution.py:349
  280.9 82.5 %collective-permute-start.13 = (f32[128,2048]{1,0:T(8,128)S(1)}, f32[128,2048]{1,0:T(8,128)}, u32[]{:S(2)}, u32[]{:S(2)}) collective-permute-start(f32[128,2048]{1,0:T(8,128)S(1)} %copy-done.8), channel_id=1, source_target_pairs={{0,6},{1,7},{2,0},{3,1},{4,2},{5,3},{6,4},{7,5},{8,14},{9,15},{10,... | collective-permute-start | bytes 3145736 | tf_op jit(solution)/shard_map/ppermute | solution.py:349
  281.0 91.7 %collective-permute-start.21 = (f32[128,2048]{1,0:T(8,128)S(1)}, f32[128,2048]{1,0:T(8,128)}, u32[]{:S(2)}, u32[]{:S(2)}) collective-permute-start(f32[128,2048]{1,0:T(8,128)S(1)} %copy-done.8), channel_id=1, source_target_pairs={{0,1},{1,0},{2,3},{3,2},{4,5},{5,4},{6,7},{7,6},{8,9},{9,8},{10,11... | collective-permute-start | bytes 3145736 | tf_op jit(solution)/shard_map/ppermute | solution.py:345
  363.4 11.1 %collective-permute-start.22 = (f32[128,2048]{1,0:T(8,128)S(1)}, f32[128,2048]{1,0:T(8,128)S(1)}, u32[]{:S(2)}, u32[]{:S(2)}) collective-permute-start(f32[128,2048]{1,0:T(8,128)S(1)} %collective-permute-done.11.refs_1_), channel_id=1, source_target_pairs={{0,1},{1,0},{2,3},{3,2},{4,5},{5,4},{6,7},{7,6},{8,9},{9,8},{10,11... | collective-permute-start | bytes 3145736 | tf_op jit(solution)/shard_map/ppermute | solution.py:345
  372.2 5.3 collective-permute-start.23
  372.2 5.5 collective-permute-start.24
  403.1 2.1 copy-start.2
  406.4 25.4 %collective-permute-start.18 = (f32[128,2048]{1,0:T(8,128)S(1)}, f32[128,2048]{1,0:T(8,128)S(1)}, u32[]{:S(2)}, u32[]{:S(2)}) collective-permute-start(f32[128,2048]{1,0:T(8,128)S(1)} %copy-done.7), channel_id=1, source_target_pairs={{0,2},{1,3},{2,4},{3,5},{4,6},{5,7},{6,0},{7,1},{8,10},{9,11},{10,... | collective-permute-start | bytes 3145736 | tf_op jit(solution)/shard_map/ppermute | solution.py:349
  406.4 88.4 %collective-permute-start.19 = (f32[128,2048]{1,0:T(8,128)S(1)}, f32[128,2048]{1,0:T(8,128)S(1)}, u32[]{:S(2)}, u32[]{:S(2)}) collective-permute-start(f32[128,2048]{1,0:T(8,128)S(1)} %copy-done.7), channel_id=1, source_target_pairs={{0,4},{1,5},{2,6},{3,7},{4,0},{5,1},{6,2},{7,3},{8,12},{9,13},{10,... | collective-permute-start | bytes 3145736 | tf_op jit(solution)/shard_map/ppermute | solution.py:349
  411.1 83.7 %collective-permute-start.20 = (f32[128,2048]{1,0:T(8,128)S(1)}, f32[128,2048]{1,0:T(8,128)}, u32[]{:S(2)}, u32[]{:S(2)}) collective-permute-start(f32[128,2048]{1,0:T(8,128)S(1)} %copy-done.7), channel_id=1, source_target_pairs={{0,6},{1,7},{2,0},{3,1},{4,2},{5,3},{6,4},{7,5},{8,14},{9,15},{10,... | collective-permute-start | bytes 3145736 | tf_op jit(solution)/shard_map/ppermute | solution.py:349
  411.1 91.8 %collective-permute-start.25 = (f32[128,2048]{1,0:T(8,128)S(1)}, f32[128,2048]{1,0:T(8,128)}, u32[]{:S(2)}, u32[]{:S(2)}) collective-permute-start(f32[128,2048]{1,0:T(8,128)S(1)} %copy-done.7), channel_id=1, source_target_pairs={{0,1},{1,0},{2,3},{3,2},{4,5},{5,4},{6,7},{7,6},{8,9},{9,8},{10,11... | collective-permute-start | bytes 3145736 | tf_op jit(solution)/shard_map/ppermute | solution.py:345
  494.8 9.9 %collective-permute-start.26 = (f32[128,2048]{1,0:T(8,128)S(1)}, f32[128,2048]{1,0:T(8,128)S(1)}, u32[]{:S(2)}, u32[]{:S(2)}) collective-permute-start(f32[128,2048]{1,0:T(8,128)S(1)} %collective-permute-done.18.refs_1_), channel_id=1, source_target_pairs={{0,1},{1,0},{2,3},{3,2},{4,5},{5,4},{6,7},{7,6},{8,9},{9,8},{10,11... | collective-permute-start | bytes 3145736 | tf_op jit(solution)/shard_map/ppermute | solution.py:345
  502.3 5.3 collective-permute-start.27
  502.3 5.5 collective-permute-start.28
  530.9 20.7 %collective-permute-start.29 = (f32[2,128,512]{2,1,0:T(8,128)}, f32[2,128,512]{2,1,0:T(8,128)}, u32[]{:S(2)}, u32[]{:S(2)}) collective-permute-start(f32[2,128,512]{2,1,0:T(8,128)} %copy-done.18), channel_id=1, source_target_pairs={{0,8},{8,0},{16,24},{24,16},{1,9},{9,1},{17,25},{25,17},{2,10},{10... | collective-permute-start | bytes 1572872 | tf_op jit(solution)/shard_map/ppermute | solution.py:353
  532.4 19.2 %collective-permute-start.30 = (f32[2,128,512]{2,1,0:T(8,128)}, f32[2,128,512]{2,1,0:T(8,128)}, u32[]{:S(2)}, u32[]{:S(2)}) collective-permute-start(f32[2,128,512]{2,1,0:T(8,128)} %copy-done.17), channel_id=1, source_target_pairs={{0,16},{8,24},{16,0},{24,8},{1,17},{9,25},{17,1},{25,9},{2,18},{10... | collective-permute-start | bytes 1572872 | tf_op jit(solution)/shard_map/ppermute | solution.py:353
  551.7 17.1 %collective-permute-start.31 = (f32[2,128,512]{2,1,0:T(8,128)}, f32[2,128,512]{2,1,0:T(8,128)S(1)}, u32[]{:S(2)}, u32[]{:S(2)}) collective-permute-start(f32[2,128,512]{2,1,0:T(8,128)} %get-tuple-element.111), channel_id=1, source_target_pairs={{0,8},{8,0},{16,24},{24,16},{1,9},{9,1},{17,25},{25,17},{2,10},{10... | collective-permute-start | bytes 1572872 | tf_op jit(solution)/shard_map/ppermute | solution.py:353
  555.9 15.3 %collective-permute-start.32 = (f32[2,128,512]{2,1,0:T(8,128)}, f32[2,128,512]{2,1,0:T(8,128)S(1)}, u32[]{:S(2)}, u32[]{:S(2)}) collective-permute-start(f32[2,128,512]{2,1,0:T(8,128)} %get-tuple-element.112), channel_id=1, source_target_pairs={{0,16},{8,24},{16,0},{24,8},{1,17},{9,25},{17,1},{25,9},{2,18},{10... | collective-permute-start | bytes 1572872 | tf_op jit(solution)/shard_map/ppermute | solution.py:353
  567.2 10.4 %collective-permute-start.35 = (f32[128,512]{1,0:T(8,128)}, f32[128,512]{1,0:T(8,128)S(1)}, u32[]{:S(2)}, u32[]{:S(2)}) collective-permute-start(f32[128,512]{1,0:T(8,128)} %get-tuple-element.124), channel_id=1, source_target_pairs={{0,16},{8,24},{16,0},{24,8},{1,17},{9,25},{17,1},{25,9},{2,18},{10... | collective-permute-start | bytes 786440 | tf_op jit(solution)/shard_map/ppermute | solution.py:353
  567.2 10.4 %collective-permute-start.36 = (f32[128,512]{1,0:T(8,128)}, f32[128,512]{1,0:T(8,128)S(1)}, u32[]{:S(2)}, u32[]{:S(2)}) collective-permute-start(f32[128,512]{1,0:T(8,128)} %get-tuple-element.125), channel_id=1, source_target_pairs={{0,8},{8,0},{16,24},{24,16},{1,9},{9,1},{17,25},{25,17},{2,10},{10... | collective-permute-start | bytes 786440 | tf_op jit(solution)/shard_map/ppermute | solution.py:353
  568.8 2.3 copy-start.21
  574.0 8.4 %collective-permute-start.33 = (f32[128,512]{1,0:T(8,128)}, f32[128,512]{1,0:T(8,128)S(1)}, u32[]{:S(2)}, u32[]{:S(2)}) collective-permute-start(f32[128,512]{1,0:T(8,128)} %get-tuple-element.118), channel_id=1, source_target_pairs={{0,16},{8,24},{16,0},{24,8},{1,17},{9,25},{17,1},{25,9},{2,18},{10... | collective-permute-start | bytes 786440 | tf_op jit(solution)/shard_map/ppermute | solution.py:353
  575.6 6.8 %collective-permute-start.34 = (f32[128,512]{1,0:T(8,128)}, f32[128,512]{1,0:T(8,128)S(1)}, u32[]{:S(2)}, u32[]{:S(2)}) collective-permute-start(f32[128,512]{1,0:T(8,128)} %get-tuple-element.119), channel_id=1, source_target_pairs={{0,8},{8,0},{16,24},{24,16},{1,9},{9,1},{17,25},{25,17},{2,10},{10... | collective-permute-start | bytes 786440 | tf_op jit(solution)/shard_map/ppermute | solution.py:353
  (20 other events, 18.7 us)
Sparse Core Ops, SparseCore 0:
  148.6 61.9 reduce-scatter.3
  277.9 60.6 reduce-scatter.5
  405.3 62.1 reduce-scatter.7

commit v4 on v0

--- a/solution.py
+++ b/solution.py
@@ -1,10 +1,21 @@
+import functools
+
 import jax
 import jax.numpy as jnp
 from jax import lax
+from jax.experimental import pallas as pl
+from jax.experimental.pallas import tpu as pltpu
 from jax.sharding import PartitionSpec as P
 
 TILE = 1024
 TILE_ROWS = 128
+CORES = 2
+VMEM_BYTES = 58 * 1024 * 1024
+COLUMNS = 256
+ROUNDS = 4
+FIRST, AWAY, STAY, WHOSE = 0, 2, 4, 6
+CHAINS = 2
+RANKS = (((0, 2), (1, 3)), ((0, 1), (2, 3)))
 
 
 def spread_tiles(tile_flags, row_span, col_span):
@@ -15,7 +26,7 @@
     ).reshape(tile_rows * row_span, tile_cols * col_span)
 
 
-def on_device(amplitudes, amp_tiles, integrals, int_tiles, owner_tiles, other_terms, denominators):
+def plain(amplitudes, amp_tiles, integrals, int_tiles, owner_tiles, other_terms, denominators):
     masked_ints = integrals * spread_tiles(int_tiles, TILE, TILE)
     masked_amps = amplitudes * spread_tiles(amp_tiles, TILE_ROWS, TILE)
     tile_count = owner_tiles.shape[0]
@@ -31,7 +42,333 @@
     return (owned + other_terms) / denominators
 
 
+def plan_kernel(devices, half, owner_ref, here_ref, take_ref, source_ref, slot_ref, *scratch):
+    inverse_ref, color_ref, pair_ref, device_ref, late_ref = scratch
+    rank, spot = here_ref[0], here_ref[1]
+    ranks = devices * 2 // ROUNDS
+    for q in range(2 * devices):
+        inverse_ref[owner_ref[q]] = q
+        color_ref[q] = -1
+    for d in range(devices):
+        late_ref[d] = -1
+
+    def walk(first, colors_ref, after):
+        def step(state):
+            at, _ = state
+            colors_ref[at] = 0
+            colors_ref[at ^ 1] = 1
+            following = after(at ^ 1)
+            return following, colors_ref[following]
+
+        lax.while_loop(lambda state: state[1] < 0, step, (jnp.int32(first), colors_ref[first]))
+
+    for t in range(0, 2 * devices, 2):
+        walk(t, color_ref, lambda u: owner_ref[inverse_ref[u] ^ 1])
+    for c in range(ranks):
+        for p in range(2):
+            q = ROUNDS * c + 2 * p
+            second = color_ref[owner_ref[q]]
+            source_ref[p * ranks + (c ^ rank)] = owner_ref[q + second] >> 1
+            group = 2 * c + p
+            device = owner_ref[q + 1 - second] >> 1
+            device_ref[group] = device
+            pair_ref[device] = group
+
+            @pl.when(rank == c)
+            def _():
+                slot_ref[p] = 2 * p + second
+                slot_ref[2 + p] = 2 * p + 1 - second
+
+    for d in range(0, devices, 2):
+        walk(d, late_ref, lambda u: device_ref[pair_ref[u] ^ 1])
+    for c in range(ranks):
+        swap = late_ref[device_ref[2 * c]]
+        for p in range(2):
+            r = 2 + (swap ^ p)
+            source_ref[r * ranks + (c ^ rank)] = device_ref[2 * c + p] >> 1
+
+        @pl.when(jnp.logical_and(rank == c, swap != 0))
+        def _():
+            kept = slot_ref[2]
+            slot_ref[2] = slot_ref[3]
+            slot_ref[3] = kept
+
+    early = color_ref[2 * spot]
+    core = spot % CORES
+    take_ref[FIRST] = early
+    take_ref[FIRST + 1] = 0
+    take_ref[AWAY] = 1 - early
+    take_ref[AWAY + 1] = (1 - core) * half
+    take_ref[STAY] = 1 - early
+    take_ref[STAY + 1] = core * half
+    take_ref[WHOSE] = late_ref[spot]
+
+
+def plan(owner_tiles, here, devices, half):
+    tiles = 2 * devices
+    smem = pl.BlockSpec(memory_space=pltpu.SMEM)
+    ints = jnp.int32
+    return pl.pallas_call(
+        functools.partial(plan_kernel, devices, half),
+        out_shape=(
+            jax.ShapeDtypeStruct((WHOSE + 1,), ints),
+            jax.ShapeDtypeStruct((tiles,), ints),
+            jax.ShapeDtypeStruct((ROUNDS,), ints),
+        ),
+        in_specs=[smem, smem],
+        out_specs=(smem, smem, smem),
+        scratch_shapes=[pltpu.SMEM((tiles,), ints)] * 2 + [pltpu.SMEM((devices,), ints)] * 3,
+    )(owner_tiles, here)
+
+
+def take_kernel(at, take_ref, flag_ref, amp_ref, out_ref):
+    flag = flag_ref[take_ref[at], take_ref[at + 1] + pl.program_id(0)]
+    out_ref[...] = amp_ref[...] * flag.astype(jnp.float32)
+
+
+def take(at, tiles, where, amp_tiles, amplitudes):
+    return pl.pallas_call(
+        functools.partial(take_kernel, at),
+        out_shape=jax.ShapeDtypeStruct((TILE_ROWS, tiles * TILE), jnp.float32),
+        grid_spec=pltpu.PrefetchScalarGridSpec(
+            num_scalar_prefetch=2,
+            grid=(tiles,),
+            in_specs=[
+                pl.BlockSpec((TILE_ROWS, TILE), lambda j, where, flags: (where[at], where[at + 1] + j))
+            ],
+            out_specs=pl.BlockSpec((TILE_ROWS, TILE), lambda j, where, flags: (0, j)),
+        ),
+    )(where, amp_tiles, amplitudes)
+
+
+def split_kernel(value_ref, high_ref, low_ref):
+    value = value_ref[...]
+    high = value.astype(jnp.bfloat16)
+    high_ref[...] = high
+    low_ref[...] = (value - high.astype(jnp.float32)).astype(jnp.bfloat16)
+
+
+def split(integrals):
+    depth, width = integrals.shape
+    rows = TILE // 2
+    block = pl.BlockSpec((rows, width), lambda i: (i, 0))
+    half = jax.ShapeDtypeStruct((depth, width), jnp.bfloat16)
+    return pl.pallas_call(
+        split_kernel,
+        out_shape=(half, half),
+        grid=(depth // rows,),
+        in_specs=[block],
+        out_specs=(block, block),
+        compiler_params=pltpu.CompilerParams(vmem_limit_bytes=VMEM_BYTES),
+        cost_estimate=pl.CostEstimate(flops=0, bytes_accessed=8 * depth * width, transcendentals=0),
+    )(integrals)
+
+
+def product_kernel(first, ranks, source_ref, flag_ref, *refs):
+    amp_refs, (high_ref, low_ref), refs = refs[:ranks], refs[ranks : ranks + 2], refs[ranks + 2 :]
+    out_refs, (pair_ref, total_ref) = refs[: 2 * CHAINS], refs[2 * CHAINS :]
+    rows = ranks * TILE_ROWS
+    width = high_ref.shape[1]
+    step = pl.program_id(0)
+
+    @pl.when(step == 0)
+    def _():
+        for i, amp_ref in enumerate(amp_refs):
+            shards, _, wide = amp_ref.shape
+            for shard in range(shards):
+                value = amp_ref[shard]
+                high = value.astype(jnp.bfloat16)
+                columns = pl.ds(shard * wide, wide)
+                pair_ref[pl.ds(i * TILE_ROWS, TILE_ROWS), columns] = high
+                pair_ref[pl.ds(rows + i * TILE_ROWS, TILE_ROWS), columns] = (
+                    value - high.astype(jnp.float32)
+                ).astype(jnp.bfloat16)
+
+    total_ref[...] = jnp.zeros_like(total_ref)
+    for k in range(high_ref.shape[0] // TILE):
+        @pl.when(flag_ref[k, (first + step) * width // TILE] != 0)
+        def _():
+            deep = pl.ds(k * TILE, TILE)
+            both = jnp.dot(pair_ref[:, deep], high_ref[deep, :], preferred_element_type=jnp.float32)
+            cross = jnp.dot(pair_ref[:rows, deep], low_ref[deep, :], preferred_element_type=jnp.float32)
+            total_ref[...] += both[:rows] + (both[rows:] + cross)
+    share = width // CHAINS
+    for chain, (kept, sent) in enumerate(RANKS):
+        columns = pl.ds(chain * share, share)
+        for ref, peers in ((out_refs[2 * chain], kept), (out_refs[2 * chain + 1], sent)):
+            for i, peer in enumerate(peers):
+                ref[i] = total_ref[pl.ds(peer * TILE_ROWS, TILE_ROWS), columns]
+
+
+def product(r, piece, pieces, ranks, source, int_tiles, gathered, high, low):
+    depth, width = high.shape
+    shards = depth // gathered.shape[2]
+    rows = ranks * TILE_ROWS
+    share = COLUMNS // CHAINS
+    steps = width // COLUMNS // pieces
+
+    def amp(peer):
+        return pl.BlockSpec(
+            (shards, TILE_ROWS, depth // shards),
+            lambda i, source, flags: (source[r * ranks + peer], 0, 0),
+            pipeline_mode=pl.Buffered(1),
+        )
+
+    integral = pl.BlockSpec((depth, COLUMNS), lambda i, *_: (0, piece * steps + i))
+    return pl.pallas_call(
+        functools.partial(product_kernel, piece * steps, ranks),
+        out_shape=[jax.ShapeDtypeStruct((2, TILE_ROWS, share * steps), jnp.float32)] * (2 * CHAINS),
+        grid_spec=pltpu.PrefetchScalarGridSpec(
+            num_scalar_prefetch=2,
+            grid=(steps,),
+            in_specs=[amp(peer) for peer in range(ranks)] + [integral, integral],
+            out_specs=[pl.BlockSpec((2, TILE_ROWS, share), lambda i, *_: (0, 0, i))] * (2 * CHAINS),
+            scratch_shapes=[
+                pltpu.VMEM((2 * rows, depth), jnp.bfloat16),
+                pltpu.VMEM((rows, COLUMNS), jnp.float32),
+            ],
+        ),
+        compiler_params=pltpu.CompilerParams(vmem_limit_bytes=VMEM_BYTES),
+        cost_estimate=pl.CostEstimate(
+            flops=6 * rows * depth * width // pieces, bytes_accessed=4 * depth * width // pieces, transcendentals=0
+        ),
+    )(source, int_tiles, *[gathered] * ranks, high, low)
+
+
+def relay_kernel(*refs):
+    for chain in range(CHAINS):
+        refs[2 * CHAINS + chain][...] = refs[2 * chain][0] + refs[2 * chain + 1][0]
+
+
+def relay(kept, heard):
+    _, rows, width = kept[0].shape
+    passed = pl.BlockSpec((1, rows, width), lambda i: (1, 0, 0))
+    out = jax.ShapeDtypeStruct((rows, width), jnp.float32)
+    return pl.pallas_call(
+        relay_kernel,
+        out_shape=[out] * CHAINS,
+        grid=(1,),
+        in_specs=[passed] * (2 * CHAINS),
+        out_specs=[pl.BlockSpec((rows, width), lambda i: (0, 0))] * CHAINS,
+    )(*[array for pair in zip(kept, heard) for array in pair])
+
+
+def finish_kernel(columns, *refs):
+    refs = refs[1:]
+    parts, (term_ref, denominator_ref), out_ref = refs[: 3 * CHAINS], refs[3 * CHAINS : 3 * CHAINS + 2], refs[-1]
+    share = columns // CHAINS
+    for block in range(term_ref.shape[1] // columns):
+        for chain in range(CHAINS):
+            kept, heard, relayed = parts[3 * chain : 3 * chain + 3]
+            source = pl.ds(block * share, share)
+            target = pl.ds(block * columns + chain * share, share)
+            total = kept[0, :, source] + heard[0, :, source] + relayed[:, source]
+            out_ref[:, target] = (total + term_ref[:, target]) / denominator_ref[:, target]
+
+
+def finish(r, piece, slot, kept, heard, relayed, other_terms, denominators, update):
+    share = kept[0].shape[2]
+    width = share * CHAINS
+    first = pl.BlockSpec((1, TILE_ROWS, share), lambda i, slot: (0, 0, 0))
+    whole = pl.BlockSpec((TILE_ROWS, share), lambda i, slot: (0, 0))
+    owned = pl.BlockSpec((TILE_ROWS, width), lambda i, slot: (slot[r], piece))
+    before = [] if update is None else [update]
+    return pl.pallas_call(
+        functools.partial(finish_kernel, COLUMNS),
+        out_shape=jax.ShapeDtypeStruct(other_terms.shape, jnp.float32),
+        grid_spec=pltpu.PrefetchScalarGridSpec(
+            num_scalar_prefetch=1,
+            grid=(1,),
+            in_specs=[first, first, whole] * CHAINS
+            + [owned, owned]
+            + [pl.BlockSpec(memory_space=pl.ANY)] * len(before),
+            out_specs=owned,
+        ),
+        input_output_aliases={3 * CHAINS + 3: 0} if before else {},
+        cost_estimate=pl.CostEstimate(flops=0, bytes_accessed=24 * TILE_ROWS * width, transcendentals=0),
+    )(
+        slot,
+        *[array for chain in zip(kept, heard, relayed) for array in chain],
+        other_terms,
+        denominators,
+        *before,
+    )
+
+
+def in_rounds(devices, ranks, amplitudes, amp_tiles, integrals, int_tiles, owner_tiles, other_terms, denominators):
+    rank = lax.axis_index("cd").astype(jnp.int32)
+    spot = lax.axis_index("ab").astype(jnp.int32)
+    tiles = amp_tiles.shape[1]
+    half = tiles // CORES
+
+    def gather(array):
+        return lax.all_gather(array, "ab", axis=0)
+
+    def swap(sent, peers):
+        return [lax.ppermute(array, "cd", [(c, c ^ peer) for c in range(ranks)]) for array, peer in zip(sent, peers)]
+
+    where, source, slot = plan(owner_tiles, jnp.stack([rank, spot]), devices, half)
+    whole = take(FIRST, tiles, where, amp_tiles, amplitudes)
+    high, low = split(integrals)
+    away = take(AWAY, half, where, amp_tiles, amplitudes)
+    stay = take(STAY, half, where, amp_tiles, amplitudes)
+    came = lax.ppermute(away, "ab", [(i, i ^ 1) for i in range(devices)])
+    mine = where[WHOSE] == 0
+    shards = [whole, jnp.where(mine, stay, came), jnp.where(mine, came, stay)]
+    gathered = [gather(shard) for shard in shards]
+    groups = [[(0, 0, 1), (1, 0, 1)], [(2, 0, 1)], [(3, 0, 2), (3, 1, 2)]]
+    terms = (other_terms, denominators)
+    update, waiting = None, []
+    for index, group in enumerate(groups):
+        final = index == len(groups) - 1
+        if index == 0:
+            rows, high, low, *_ = lax.optimization_barrier((gathered[0], high, low, *shards[1:]))
+        else:
+            rows, onward, update = lax.optimization_barrier((gathered[index], onward, update))
+        sums = []
+        for r, piece, pieces in group:
+            parts = product(r, piece, pieces, ranks, source, int_tiles, rows, high, low)
+            if sums:
+                parts, heard = lax.optimization_barrier((parts, sums[-1][1]))
+                sums[-1] = (sums[-1][0], heard)
+            elif waiting:
+                parts, relayed = lax.optimization_barrier((parts, [entry[-1] for entry in waiting]))
+                waiting = [(*entry[:-1], heard) for entry, heard in zip(waiting, relayed)]
+            sums.append((parts[0::2], swap(parts[1::2], (1, 2))))
+            if not final:
+                for entry in waiting:
+                    update = finish(*entry, *terms, update)
+                waiting = []
+        entries = []
+        for (r, piece, _), (kept, heard) in zip(group, sums):
+            if final and waiting:
+                if entries:
+                    for entry in waiting:
+                        update = finish(*entry, *terms, update)
+                    waiting = []
+                    heard, update = lax.optimization_barrier((heard, update))
+            onward = relay(kept, heard)
+            if final and waiting:
+                onward, slot = lax.optimization_barrier((onward, slot))
+                waiting = [(*entry[:2], slot, *entry[3:]) for entry in waiting]
+            entries.append((r, piece, slot, kept, heard, swap(onward, (2, 1))))
+        waiting = entries
+    for entry in waiting:
+        update = finish(*entry, *terms, update)
+    return update
+
+
 def solution(mesh):
+    ranks, places = mesh.shape["cd"], mesh.shape["ab"]
+
+    def on_device(amplitudes, amp_tiles, integrals, int_tiles, owner_tiles, other_terms, denominators):
+        args = (amplitudes, amp_tiles, integrals, int_tiles, owner_tiles, other_terms, denominators)
+        tiles = owner_tiles.shape[0]
+        whole = places % CORES == 0 and amplitudes.shape[1] % (CORES * TILE) == 0
+        if whole and ranks == 4 and tiles == 2 * places == ROUNDS * ranks:
+            return in_rounds(places, ranks, *args)
+        return plain(*args)
+
     return jax.shard_map(
         on_device,
         mesh=mesh,

time: 716 us -> 418 us (0.58)
  waiting for transfers between devices: 399 us -> 151 us
  matrix products: 226 us -> 0 us
  Pallas kernels: 0 us -> 205 us
  local copies, waits for them, and re-layouts: 63.4 us -> 7.66 us
  starting transfers between devices: 0.04 us -> 33 us
  other arithmetic: 13.9 us -> 3.43 us
    dot_general x1 -> x0, matrix products: 226 us -> none  [on_device(): jnp.dot(gathered, masked_ints, precision=lax.Precision.HIGHEST, preferred...]
    pallas_call x0 -> x20, Pallas kernels: none -> 205 us  [the longest x5 138 us: product(): pl.pallas_call(functools.partial(product_kernel, piece * steps, ranks), o...]
    reduce_scatter x1 -> x0, waiting for transfers between devices: 152 us -> none  [on_device(): lax.psum_scatter(partial_value, 'cd', scatter_dimension=0, tiled=True)]
    all_gather x1 -> x3, waiting for transfers between devices: 247 us -> 119 us  [gather(): return lax.all_gather(array, 'ab', axis=0)]
    ppermute x0 -> x21, starting transfers between devices: none -> 32.9 us  [the longest x20 32.5 us: swap(): lax.ppermute(array, 'cd', [(c, c ^ peer) for c in range(ranks)])]
    ppermute x0 -> x21, waiting for transfers between devices: none -> 32 us  [the longest x20 32 us: swap(): lax.ppermute(array, 'cd', [(c, c ^ peer) for c in range(ranks)])]
    unnamed x6 -> x43, local copies, waits for them, and re-layouts: 35.1 us -> 7 us
    broadcast_in_dim x2 -> x0, local copies, waits for them, and re-layouts: 14.3 us -> none  [spread_tiles(): jnp.broadcast_to(values[:, None, :, None], (tile_rows, row_span, tile_col...]
  transfers between devices with their start and end apart: 2 -> 24, of which waited for: 2 -> 7; matrix products, arithmetic and copies ran while one was open for 6% -> 1% of each run, Pallas kernels for 0% -> 47%
where the time goes in v4:
time: 418 us; the launch traced here: 415 us
  Pallas kernels  205 us (49%)
  waiting for transfers between devices  151 us (36%)
  starting transfers between devices  33 us (8%)
  between operations  14.1 us (3%)
  local copies, waits for them, and re-layouts  7.66 us (2%)
    pallas_call x5, Pallas kernels, product(): pl.pallas_call(functools.partial(product_kernel, piece * steps, ranks), o...  138 us
    all_gather x3, waiting for transfers between devices, gather(): return lax.all_gather(array, 'ab', axis=0)  119 us
    ppermute x20, starting transfers between devices, swap(): lax.ppermute(array, 'cd', [(c, c ^ peer) for c in range(ranks)])  32.5 us
    ppermute x20, waiting for transfers between devices, swap(): lax.ppermute(array, 'cd', [(c, c ^ peer) for c in range(ranks)])  32 us
    pallas_call x1, Pallas kernels, split(): pl.pallas_call(split_kernel, out_shape=(half, half), grid=(depth // rows,...  23.7 us
    pallas_call x5, Pallas kernels, finish(): pl.pallas_call(functools.partial(finish_kernel, COLUMNS), out_shape=jax.S...  20.4 us
    pallas_call x5, Pallas kernels, relay(): pl.pallas_call(relay_kernel, out_shape=[out] * CHAINS, grid=(1,), in_spec...  11.7 us
    pallas_call x3, Pallas kernels, take(): pl.pallas_call(functools.partial(take_kernel, at), out_shape=jax.ShapeDty...  10.1 us
  transfers between devices with their start and end apart: 24, of which 7 were waited for; matrix products, arithmetic and copies ran while one was open for 1% of the time, Pallas kernels for 47%

profile of v4, /device:TPU:0, one launch (start us, length us, event | category | flops | bytes accessed | tf_op | source)
XLA Modules:
  0.0 414.6 jit_solution(1744680120480879932)
XLA Ops:
  7.2 1.6 shard_map.73
  8.8 4.5 %shard_map.76 = f32[128,4096]{1,0:T(8,128)} custom-call(s32[7]{0:T(128)} %get-tuple-element.79.take_ref, s32[2,4]{1,0:T(2,128)} %flag_ref.10, f32[256,4096]{1,0:T(8,128)} %amp_ref.5), custom_call_target="tpu_custom_call" | custom-call | tf_op jit(solution)/shard_map/pallas_call | solution.py:130
  13.4 2.8 shard_map.74
  16.6 2.8 shard_map.75
  20.8 2.8 broadcast_select_fusion
  23.6 0.7 all-gather.7.cloned.1.call-update
  24.3 23.7 %shard_map.77 = (bf16[4096,2048]{1,0:T(8,128)(2,1)}, bf16[4096,2048]{1,0:T(8,128)(2,1)}) custom-call(f32[4096,2048]{1,0:T(8,128)} %value_ref.1), custom_call_target="tpu_custom_call" | custom-call | bytes 67108864 | tf_op jit(solution)/shard_map/pallas_call | solution.py:156
  48.7 118.6 %all-gather.11.cloned.1.call-done = f32[1024,4096]{1,0:T(8,128)} async-done(((f32[128,4096]{1,0:T(8,128)}), f32[1024,4096]{1,0:T(8,128)}) %all-gather.11.cloned.1.call-update) | async-done | bytes 16777232 | tf_op jit(solution)/shard_map/all_gather | solution.py:305
  167.3 32.9 %shard_map.79 = (f32[2,128,1024]{2,1,0:T(8,128)}, f32[2,128,1024]{2,1,0:T(8,128)}, f32[2,128,1024]{2,1,0:T(8,128)}, f32[2,128,1024]{2,1,0:T(8,128)}) custom-call(s32[16]{0:T(128)} %get-tuple-element.78.source_ref, s32[4,2]{1,0:T(4,128)} %copy.15.flag_ref, f32[8,128,4096]{2,1,0:T(8,128)} %bitcast.6, f32[8,128,4096]{2,1,0:T(8,128)} %bitcast.7, ...), custom_call_target="tpu_custom_call" | custom-call | flops 25769803776 | bytes 33554432 | tf_op jit(solution)/shard_map/pallas_call | solution.py:218
  200.2 4.3 %collective-permute-start.2 = (f32[2,128,1024]{2,1,0:T(8,128)}, f32[2,128,1024]{2,1,0:T(8,128)S(1)}, u32[]{:S(2)}, u32[]{:S(2)}) collective-permute-start(f32[2,128,1024]{2,1,0:T(8,128)} %get-tuple-element.90), channel_id=1, source_target_pairs={{0,16},{8,24},{16,0},{24,8},{1,17},{9,25},{17,1},{25,9},{2,18},{10... | collective-permute-start | bytes 3145736 | tf_op jit(solution)/shard_map/ppermute | solution.py:308
  204.4 32.4 %shard_map.78 = (f32[2,128,1024]{2,1,0:T(8,128)}, f32[2,128,1024]{2,1,0:T(8,128)}, f32[2,128,1024]{2,1,0:T(8,128)}, f32[2,128,1024]{2,1,0:T(8,128)}) custom-call(s32[16]{0:T(128)} %get-tuple-element.78.source_ref, s32[4,2]{1,0:T(4,128)} %copy.15.flag_ref, f32[8,128,4096]{2,1,0:T(8,128)} %bitcast.10, f32[8,128,4096]{2,1,0:T(8,128)} %bitcast.11, ...), custom_call_target="tpu_custom_call" | custom-call | flops 25769803776 | bytes 33554432 | tf_op jit(solution)/shard_map/pallas_call | solution.py:218
  237.0 3.3 collective-permute-start.4
  240.3 2.5 shard_map.82
  242.8 1.2 collective-permute-start.5
  244.0 0.8 collective-permute-start.6
  244.8 18.0 %collective-permute-done.3.refs_1_.refs_2_ = f32[2,128,1024]{2,1,0:T(8,128)S(1)} collective-permute-done((f32[2,128,1024]{2,1,0:T(8,128)}, f32[2,128,1024]{2,1,0:T(8,128)S(1)}, u32[]{:S(2)}, u32[]{:S(2)}) %collective-permute-start.3) | collective-permute-done | bytes 1048608 | tf_op jit(solution)/shard_map/ppermute | solution.py:308
  262.8 1.9 collective-permute-done.4.refs_3_.refs_5_
  264.7 2.6 shard_map.80
  267.3 2.8 collective-permute-start.7
  270.0 1.2 collective-permute-start.8
  271.2 32.8 %shard_map.81 = (f32[2,128,1024]{2,1,0:T(8,128)}, f32[2,128,1024]{2,1,0:T(8,128)}, f32[2,128,1024]{2,1,0:T(8,128)}, f32[2,128,1024]{2,1,0:T(8,128)}) custom-call(s32[16]{0:T(128)} %get-tuple-element.78.source_ref, s32[4,2]{1,0:T(4,128)} %copy.15.flag_ref, f32[8,128,2048]{2,1,0:T(8,128)} %bitcast.22, f32[8,128,2048]{2,1,0:T(8,128)} %bitcast.23, ...), custom_call_target="tpu_custom_call" | custom-call | flops 25769803776 | bytes 33554432 | tf_op jit(solution)/shard_map/pallas_call | solution.py:218
  304.1 0.7 copy-done.11
  305.0 3.0 collective-permute-start.10
  308.0 4.6 %shard_map.84.refs_9_ = f32[512,2048]{1,0:T(8,128)} custom-call(s32[4]{0:T(128)} %get-tuple-element.136.refs_0_, f32[2,128,1024]{2,1,0:T(8,128)} %get-tuple-element.102.refs_0_.refs_1_, f32[2,128,1024]{2,1,0:T(8,128)} %copy-done.2, f32[128,1024]{1,0:T(8,128)} %copy-done.11, f32[2,128,1024]{2,1,0:T(8,128)} %get-tuple-element.104.refs_2_.refs_4_, ...), custom_call_target="tpu_custom_call" | custom-call | bytes 6291456 | tf_op jit(solution)/shard_map/pallas_call | solution.py:276
  312.6 4.6 %shard_map.85.refs_9_ = f32[512,2048]{1,0:T(8,128)} custom-call(s32[4]{0:T(128)} %get-tuple-element.136.refs_0_, f32[2,128,1024]{2,1,0:T(8,128)} %get-tuple-element.91.refs_0_.refs_1_, f32[2,128,1024]{2,1,0:T(8,128)} %copy-done.4, f32[128,1024]{1,0:T(8,128)} %copy-done.13, ...), custom_call_target="tpu_custom_call", output_to_operand_aliasing={{}: (9, {})} | custom-call | bytes 6291456 | tf_op jit(solution)/shard_map/pallas_call | solution.py:276
  317.2 9.4 %collective-permute-done.10.refs_3_.refs_5_ = f32[2,128,1024]{2,1,0:T(8,128)S(1)} collective-permute-done((f32[2,128,1024]{2,1,0:T(8,128)}, f32[2,128,1024]{2,1,0:T(8,128)S(1)}, u32[]{:S(2)}, u32[]{:S(2)}) %collective-permute-start.10) | collective-permute-done | bytes 1048608 | tf_op jit(solution)/shard_map/ppermute | solution.py:308
  326.6 1.0 collective-permute-done.9.refs_1_.refs_2_
  327.6 1.0 copy-done.1
  328.6 2.5 shard_map.83
  331.2 0.7 collective-permute-start.11
  332.2 16.1 %shard_map.86 = (f32[2,128,512]{2,1,0:T(8,128)}, f32[2,128,512]{2,1,0:T(8,128)}, f32[2,128,512]{2,1,0:T(8,128)}, f32[2,128,512]{2,1,0:T(8,128)}) custom-call(s32[16]{0:T(128)} %get-tuple-element.78.source_ref, s32[4,2]{1,0:T(4,128)} %copy.15.flag_ref, f32[8,128,2048]{2,1,0:T(8,128)} %bitcast.14, f32[8,128,2048]{2,1,0:T(8,128)} %bitcast.15, ...), custom_call_target="tpu_custom_call" | custom-call | flops 12884901888 | bytes 16777216 | tf_op jit(solution)/shard_map/pallas_call | solution.py:218
  348.3 1.7 collective-permute-start.13
  350.0 7.8 %collective-permute-start.14 = (f32[2,128,512]{2,1,0:T(8,128)}, f32[2,128,512]{2,1,0:T(8,128)S(1)}, u32[]{:S(2)}, u32[]{:S(2)}) collective-permute-start(f32[2,128,512]{2,1,0:T(8,128)} %get-tuple-element.130), channel_id=1, source_target_pairs={{0,16},{8,24},{16,0},{24,8},{1,17},{9,25},{17,1},{25,9},{2,18},{10... | collective-permute-start | bytes 1572872 | tf_op jit(solution)/shard_map/ppermute | solution.py:308
  357.8 23.6 %shard_map.87 = (f32[2,128,512]{2,1,0:T(8,128)}, f32[2,128,512]{2,1,0:T(8,128)}, f32[2,128,512]{2,1,0:T(8,128)}, f32[2,128,512]{2,1,0:T(8,128)}) custom-call(s32[16]{0:T(128)} %get-tuple-element.78.source_ref, s32[4,2]{1,0:T(4,128)} %copy.15.flag_ref, f32[8,128,2048]{2,1,0:T(8,128)} %bitcast.18, f32[8,128,2048]{2,1,0:T(8,128)} %bitcast.19, ...), custom_call_target="tpu_custom_call" | custom-call | flops 12884901888 | bytes 16777216 | tf_op jit(solution)/shard_map/pallas_call | solution.py:218
  382.5 2.0 shard_map.88
  384.5 1.2 collective-permute-start.19
  385.7 1.9 collective-permute-start.20
  387.6 4.5 %shard_map.89.refs_9_ = f32[512,2048]{1,0:T(8,128)} custom-call(s32[4]{0:T(128)} %get-tuple-element.136.refs_0_, f32[2,128,1024]{2,1,0:T(8,128)} %get-tuple-element.108.refs_0_.refs_1_, f32[2,128,1024]{2,1,0:T(8,128)} %copy-done.1, f32[128,1024]{1,0:T(8,128)} %copy-done.9, ...), custom_call_target="tpu_custom_call", output_to_operand_aliasing={{}: (9, {})} | custom-call | bytes 6291456 | tf_op jit(solution)/shard_map/pallas_call | solution.py:276
  392.8 1.0 collective-permute-done.16.refs_3_.refs_5_
  393.8 0.8 copy-done.8
  394.6 2.0 shard_map.90
  396.6 2.0 collective-permute-start.18
  398.6 0.7 copy-done.15
  399.3 0.7 copy-done.16
  400.0 3.3 shard_map.91.refs_9_
  403.4 0.7 copy-done.17
  404.1 0.7 copy-done.18
  404.8 3.3 shard_map.92
  (69 shorter events, 4.9 us)
Async XLA Ops:
  6.5 160.7 %all-gather.11.cloned.1.call-start = ((), (), s32[]{:S(2)}) async-start(), calls=%async_computation.2 | async-start | bytes 18874368 | tf_op jit(solution)/shard_map/all_gather | solution.py:305
  13.3 6.1 %copy-start.19 = (s32[7]{0:T(128)S(1)}, s32[7]{0:T(128)}, u32[]{:S(2)}) copy-start(s32[7]{0:T(128)} %get-tuple-element.79.take_ref) | copy-start | bytes 88
  13.3 257.9 %all-gather.9.cloned.1.call-start = ((), (), s32[]{:S(2)}) async-start(), calls=%async_computation.1 | async-start | bytes 9437184 | tf_op jit(solution)/shard_map/all_gather | solution.py:305
  16.1 4.6 %collective-permute-start = (f32[128,2048]{1,0:T(8,128)}, f32[128,2048]{1,0:T(8,128)S(1)}, u32[]{:S(2)}, u32[]{:S(2)}) collective-permute-start(f32[128,2048]{1,0:T(8,128)} %shard_map.74), channel_id=1, source_target_pairs={{0,1},{1,0},{2,3},{3,2},{4,5},{5,4},{6,7},{7,6},{8,9},{9,8},{10,11... | collective-permute-start | bytes 3145736 | tf_op jit(solution)/shard_map/ppermute | solution.py:315
  23.6 308.6 %all-gather.7.cloned.1.call-start = ((), (), s32[]{:S(2)}) async-start(), calls=%async_computation | async-start | bytes 9437184 | tf_op jit(solution)/shard_map/all_gather | solution.py:305
  24.3 23.8 %copy-start.20 = (s32[4,2]{0,1:T(2,128)S(1)}, s32[4,2]{0,1:T(2,128)}, u32[]{:S(2)}) copy-start(s32[4,2]{0,1:T(2,128)} %param.10) | copy-start | bytes 100
  200.1 36.8 %collective-permute-start.1 = (f32[2,128,1024]{2,1,0:T(8,128)}, f32[2,128,1024]{2,1,0:T(8,128)S(1)}, u32[]{:S(2)}, u32[]{:S(2)}) collective-permute-start(f32[2,128,1024]{2,1,0:T(8,128)} %get-tuple-element.89), channel_id=1, source_target_pairs={{0,8},{8,0},{16,24},{24,16},{1,9},{9,1},{17,25},{25,17},{2,10},{10... | collective-permute-start | bytes 3145736 | tf_op jit(solution)/shard_map/ppermute | solution.py:308
  200.2 36.7 %collective-permute-start.2 = (f32[2,128,1024]{2,1,0:T(8,128)}, f32[2,128,1024]{2,1,0:T(8,128)S(1)}, u32[]{:S(2)}, u32[]{:S(2)}) collective-permute-start(f32[2,128,1024]{2,1,0:T(8,128)} %get-tuple-element.90), channel_id=1, source_target_pairs={{0,16},{8,24},{16,0},{24,8},{1,17},{9,25},{17,1},{25,9},{2,18},{10... | collective-permute-start | bytes 3145736 | tf_op jit(solution)/shard_map/ppermute | solution.py:308
  236.9 3.4 copy-start.2
  236.9 3.4 copy-start.3
  236.9 25.9 %collective-permute-start.3 = (f32[2,128,1024]{2,1,0:T(8,128)}, f32[2,128,1024]{2,1,0:T(8,128)S(1)}, u32[]{:S(2)}, u32[]{:S(2)}) collective-permute-start(f32[2,128,1024]{2,1,0:T(8,128)} %get-tuple-element.92), channel_id=1, source_target_pairs={{0,8},{8,0},{16,24},{24,16},{1,9},{9,1},{17,25},{25,17},{2,10},{10... | collective-permute-start | bytes 3145736 | tf_op jit(solution)/shard_map/ppermute | solution.py:308
  237.0 27.7 %collective-permute-start.4 = (f32[2,128,1024]{2,1,0:T(8,128)}, f32[2,128,1024]{2,1,0:T(8,128)}, u32[]{:S(2)}, u32[]{:S(2)}) collective-permute-start(f32[2,128,1024]{2,1,0:T(8,128)} %get-tuple-element.94), channel_id=1, source_target_pairs={{0,16},{8,24},{16,0},{24,8},{1,17},{9,25},{17,1},{25,9},{2,18},{10... | collective-permute-start | bytes 3145736 | tf_op jit(solution)/shard_map/ppermute | solution.py:308
  242.8 61.1 %collective-permute-start.5 = (f32[128,1024]{1,0:T(8,128)}, f32[128,1024]{1,0:T(8,128)S(1)}, u32[]{:S(2)}, u32[]{:S(2)}) collective-permute-start(f32[128,1024]{1,0:T(8,128)} %get-tuple-element.106), channel_id=1, source_target_pairs={{0,16},{8,24},{16,0},{24,8},{1,17},{9,25},{17,1},{25,9},{2,18},{10... | collective-permute-start | bytes 1572872 | tf_op jit(solution)/shard_map/ppermute | solution.py:308
  244.0 60.0 %collective-permute-start.6 = (f32[128,1024]{1,0:T(8,128)}, f32[128,1024]{1,0:T(8,128)S(1)}, u32[]{:S(2)}, u32[]{:S(2)}) collective-permute-start(f32[128,1024]{1,0:T(8,128)} %get-tuple-element.107), channel_id=1, source_target_pairs={{0,8},{8,0},{16,24},{24,16},{1,9},{9,1},{17,25},{25,17},{2,10},{10... | collective-permute-start | bytes 1572872 | tf_op jit(solution)/shard_map/ppermute | solution.py:308
  262.8 1.9 copy-start.4
  267.3 36.8 %collective-permute-start.7 = (f32[128,1024]{1,0:T(8,128)}, f32[128,1024]{1,0:T(8,128)S(1)}, u32[]{:S(2)}, u32[]{:S(2)}) collective-permute-start(f32[128,1024]{1,0:T(8,128)} %get-tuple-element.95), channel_id=1, source_target_pairs={{0,16},{8,24},{16,0},{24,8},{1,17},{9,25},{17,1},{25,9},{2,18},{10... | collective-permute-start | bytes 1572872 | tf_op jit(solution)/shard_map/ppermute | solution.py:308
  270.0 34.0 %collective-permute-start.8 = (f32[128,1024]{1,0:T(8,128)}, f32[128,1024]{1,0:T(8,128)S(1)}, u32[]{:S(2)}, u32[]{:S(2)}) collective-permute-start(f32[128,1024]{1,0:T(8,128)} %get-tuple-element.96), channel_id=1, source_target_pairs={{0,8},{8,0},{16,24},{24,16},{1,9},{9,1},{17,25},{25,17},{2,10},{10... | collective-permute-start | bytes 1572872 | tf_op jit(solution)/shard_map/ppermute | solution.py:308
  304.0 0.8 copy-start.11
  304.0 1.0 copy-start.12
  304.0 8.6 %copy-start.13 = (f32[128,1024]{1,0:T(8,128)}, f32[128,1024]{1,0:T(8,128)S(1)}, u32[]{:S(2)}) copy-start(f32[128,1024]{1,0:T(8,128)S(1)} %collective-permute-done.7.refs_3_) | copy-start | bytes 1572868
  304.1 8.6 %copy-start.14 = (f32[128,1024]{1,0:T(8,128)}, f32[128,1024]{1,0:T(8,128)S(1)}, u32[]{:S(2)}) copy-start(f32[128,1024]{1,0:T(8,128)S(1)} %collective-permute-done.8.refs_6_) | copy-start | bytes 1572868
  305.0 21.6 %collective-permute-start.10 = (f32[2,128,1024]{2,1,0:T(8,128)}, f32[2,128,1024]{2,1,0:T(8,128)S(1)}, u32[]{:S(2)}, u32[]{:S(2)}) collective-permute-start(f32[2,128,1024]{2,1,0:T(8,128)} %get-tuple-element.111), channel_id=1, source_target_pairs={{0,16},{8,24},{16,0},{24,8},{1,17},{9,25},{17,1},{25,9},{2,18},{10... | collective-permute-start | bytes 3145736 | tf_op jit(solution)/shard_map/ppermute | solution.py:308
  308.0 19.6 %collective-permute-start.9 = (f32[2,128,1024]{2,1,0:T(8,128)}, f32[2,128,1024]{2,1,0:T(8,128)S(1)}, u32[]{:S(2)}, u32[]{:S(2)}) collective-permute-start(f32[2,128,1024]{2,1,0:T(8,128)} %get-tuple-element.109), channel_id=1, source_target_pairs={{0,8},{8,0},{16,24},{24,16},{1,9},{9,1},{17,25},{25,17},{2,10},{10... | collective-permute-start | bytes 3145736 | tf_op jit(solution)/shard_map/ppermute | solution.py:308
  326.6 1.0 copy-start
  327.6 1.0 copy-start.1
  331.2 17.1 %collective-permute-start.11 = (f32[128,1024]{1,0:T(8,128)}, f32[128,1024]{1,0:T(8,128)S(1)}, u32[]{:S(2)}, u32[]{:S(2)}) collective-permute-start(f32[128,1024]{1,0:T(8,128)} %get-tuple-element.112), channel_id=1, source_target_pairs={{0,16},{8,24},{16,0},{24,8},{1,17},{9,25},{17,1},{25,9},{2,18},{10... | collective-permute-start | bytes 1572872 | tf_op jit(solution)/shard_map/ppermute | solution.py:308
  331.9 16.4 %collective-permute-start.12 = (f32[128,1024]{1,0:T(8,128)}, f32[128,1024]{1,0:T(8,128)S(1)}, u32[]{:S(2)}, u32[]{:S(2)}) collective-permute-start(f32[128,1024]{1,0:T(8,128)} %get-tuple-element.113), channel_id=1, source_target_pairs={{0,8},{8,0},{16,24},{24,16},{1,9},{9,1},{17,25},{25,17},{2,10},{10... | collective-permute-start | bytes 1572872 | tf_op jit(solution)/shard_map/ppermute | solution.py:308
  348.3 33.2 %copy-start.9 = (f32[128,1024]{1,0:T(8,128)}, f32[128,1024]{1,0:T(8,128)S(1)}, u32[]{:S(2)}) copy-start(f32[128,1024]{1,0:T(8,128)S(1)} %collective-permute-done.11.refs_3_) | copy-start | bytes 1572868
  348.3 33.2 %copy-start.10 = (f32[128,1024]{1,0:T(8,128)}, f32[128,1024]{1,0:T(8,128)S(1)}, u32[]{:S(2)}) copy-start(f32[128,1024]{1,0:T(8,128)S(1)} %collective-permute-done.12.refs_6_) | copy-start | bytes 1572868
  348.3 33.2 %collective-permute-start.13 = (f32[2,128,512]{2,1,0:T(8,128)}, f32[2,128,512]{2,1,0:T(8,128)S(1)}, u32[]{:S(2)}, u32[]{:S(2)}) collective-permute-start(f32[2,128,512]{2,1,0:T(8,128)} %get-tuple-element.129), channel_id=1, source_target_pairs={{0,8},{8,0},{16,24},{24,16},{1,9},{9,1},{17,25},{25,17},{2,10},{10... | collective-permute-start | bytes 1572872 | tf_op jit(solution)/shard_map/ppermute | solution.py:308
  350.0 31.4 %collective-permute-start.14 = (f32[2,128,512]{2,1,0:T(8,128)}, f32[2,128,512]{2,1,0:T(8,128)S(1)}, u32[]{:S(2)}, u32[]{:S(2)}) collective-permute-start(f32[2,128,512]{2,1,0:T(8,128)} %get-tuple-element.130), channel_id=1, source_target_pairs={{0,16},{8,24},{16,0},{24,8},{1,17},{9,25},{17,1},{25,9},{2,18},{10... | collective-permute-start | bytes 1572872 | tf_op jit(solution)/shard_map/ppermute | solution.py:308
  381.5 0.8 copy-start.5
  381.5 1.0 copy-start.6
  381.5 11.3 %collective-permute-start.15 = (f32[2,128,512]{2,1,0:T(8,128)}, f32[2,128,512]{2,1,0:T(8,128)S(1)}, u32[]{:S(2)}, u32[]{:S(2)}) collective-permute-start(f32[2,128,512]{2,1,0:T(8,128)} %get-tuple-element.138), channel_id=1, source_target_pairs={{0,8},{8,0},{16,24},{24,16},{1,9},{9,1},{17,25},{25,17},{2,10},{10... | collective-permute-start | bytes 1572872 | tf_op jit(solution)/shard_map/ppermute | solution.py:308
  381.6 12.2 %collective-permute-start.16 = (f32[2,128,512]{2,1,0:T(8,128)}, f32[2,128,512]{2,1,0:T(8,128)S(1)}, u32[]{:S(2)}, u32[]{:S(2)}) collective-permute-start(f32[2,128,512]{2,1,0:T(8,128)} %get-tuple-element.139), channel_id=1, source_target_pairs={{0,16},{8,24},{16,0},{24,8},{1,17},{9,25},{17,1},{25,9},{2,18},{10... | collective-permute-start | bytes 1572872 | tf_op jit(solution)/shard_map/ppermute | solution.py:308
  384.5 14.1 %collective-permute-start.19 = (f32[128,512]{1,0:T(8,128)}, f32[128,512]{1,0:T(8,128)S(1)}, u32[]{:S(2)}, u32[]{:S(2)}) collective-permute-start(f32[128,512]{1,0:T(8,128)} %get-tuple-element.148), channel_id=1, source_target_pairs={{0,16},{8,24},{16,0},{24,8},{1,17},{9,25},{17,1},{25,9},{2,18},{10... | collective-permute-start | bytes 786440 | tf_op jit(solution)/shard_map/ppermute | solution.py:308
  385.7 12.9 %collective-permute-start.20 = (f32[128,512]{1,0:T(8,128)}, f32[128,512]{1,0:T(8,128)S(1)}, u32[]{:S(2)}, u32[]{:S(2)}) collective-permute-start(f32[128,512]{1,0:T(8,128)} %get-tuple-element.149), channel_id=1, source_target_pairs={{0,8},{8,0},{16,24},{24,16},{1,9},{9,1},{17,25},{25,17},{2,10},{10... | collective-permute-start | bytes 786440 | tf_op jit(solution)/shard_map/ppermute | solution.py:308
  392.8 1.0 copy-start.7
  393.8 0.8 copy-start.8
  396.6 6.7 %collective-permute-start.17 = (f32[128,512]{1,0:T(8,128)}, f32[128,512]{1,0:T(8,128)S(1)}, u32[]{:S(2)}, u32[]{:S(2)}) collective-permute-start(f32[128,512]{1,0:T(8,128)} %get-tuple-element.146), channel_id=1, source_target_pairs={{0,16},{8,24},{16,0},{24,8},{1,17},{9,25},{17,1},{25,9},{2,18},{10... | collective-permute-start | bytes 786440 | tf_op jit(solution)/shard_map/ppermute | solution.py:308
  396.6 6.7 %collective-permute-start.18 = (f32[128,512]{1,0:T(8,128)}, f32[128,512]{1,0:T(8,128)S(1)}, u32[]{:S(2)}, u32[]{:S(2)}) collective-permute-start(f32[128,512]{1,0:T(8,128)} %get-tuple-element.147), channel_id=1, source_target_pairs={{0,8},{8,0},{16,24},{24,16},{1,9},{9,1},{17,25},{25,17},{2,10},{10... | collective-permute-start | bytes 786440 | tf_op jit(solution)/shard_map/ppermute | solution.py:308
  398.6 0.7 copy-start.15
  399.3 0.7 copy-start.16
  403.4 0.7 copy-start.17
  404.1 0.7 copy-start.18
Sparse Core Ops, SparseCore 0:
  13.4 153.7 all-gather.10
  168.9 80.2 all-gather.8
  250.8 80.5 all-gather.6

commit v5 on v4

--- a/solution.py
+++ b/solution.py
@@ -141,57 +141,60 @@
     )(where, amp_tiles, amplitudes)
 
 
-def split_kernel(value_ref, high_ref, low_ref):
+def split_kernel(value_ref, halves_ref):
     value = value_ref[...]
     high = value.astype(jnp.bfloat16)
-    high_ref[...] = high
-    low_ref[...] = (value - high.astype(jnp.float32)).astype(jnp.bfloat16)
+    halves_ref[:TILE, :] = high
+    halves_ref[TILE:, :] = (value - high.astype(jnp.float32)).astype(jnp.bfloat16)
 
 
 def split(integrals):
     depth, width = integrals.shape
-    rows = TILE // 2
-    block = pl.BlockSpec((rows, width), lambda i: (i, 0))
-    half = jax.ShapeDtypeStruct((depth, width), jnp.bfloat16)
     return pl.pallas_call(
         split_kernel,
-        out_shape=(half, half),
-        grid=(depth // rows,),
-        in_specs=[block],
-        out_specs=(block, block),
+        out_shape=jax.ShapeDtypeStruct((2 * depth, width), jnp.bfloat16),
+        grid=(depth // TILE, width // TILE),
+        in_specs=[pl.BlockSpec((TILE, TILE), lambda i, j: (i, j))],
+        out_specs=pl.BlockSpec((2 * TILE, TILE), lambda i, j: (i, j)),
         compiler_params=pltpu.CompilerParams(vmem_limit_bytes=VMEM_BYTES),
         cost_estimate=pl.CostEstimate(flops=0, bytes_accessed=8 * depth * width, transcendentals=0),
     )(integrals)
 
 
 def product_kernel(first, ranks, source_ref, flag_ref, *refs):
-    amp_refs, (high_ref, low_ref), refs = refs[:ranks], refs[ranks : ranks + 2], refs[ranks + 2 :]
-    out_refs, (pair_ref, total_ref) = refs[: 2 * CHAINS], refs[2 * CHAINS :]
-    rows = ranks * TILE_ROWS
-    width = high_ref.shape[1]
+    amp_refs, halves_ref, refs = refs[:ranks], refs[ranks], refs[ranks + 1 :]
+    out_refs, (twice_ref, low_ref, total_ref) = refs[: 2 * CHAINS], refs[2 * CHAINS :]
+    width = halves_ref.shape[1]
     step = pl.program_id(0)
 
     @pl.when(step == 0)
     def _():
         for i, amp_ref in enumerate(amp_refs):
+            rows = pl.ds(i * TILE_ROWS, TILE_ROWS)
             shards, _, wide = amp_ref.shape
             for shard in range(shards):
-                value = amp_ref[shard]
-                high = value.astype(jnp.bfloat16)
-                columns = pl.ds(shard * wide, wide)
-                pair_ref[pl.ds(i * TILE_ROWS, TILE_ROWS), columns] = high
-                pair_ref[pl.ds(rows + i * TILE_ROWS, TILE_ROWS), columns] = (
-                    value - high.astype(jnp.float32)
-                ).astype(jnp.bfloat16)
+                for tile in range(wide // TILE):
+                    k = shard * (wide // TILE) + tile
+                    value = amp_ref[shard, :, pl.ds(tile * TILE, TILE)]
+                    high = value.astype(jnp.bfloat16)
+                    twice_ref[rows, pl.ds(2 * k * TILE, TILE)] = high
+                    twice_ref[rows, pl.ds((2 * k + 1) * TILE, TILE)] = high
+                    low_ref[rows, pl.ds(k * TILE, TILE)] = (value - high.astype(jnp.float32)).astype(jnp.bfloat16)
 
     total_ref[...] = jnp.zeros_like(total_ref)
-    for k in range(high_ref.shape[0] // TILE):
+    for k in range(low_ref.shape[1] // TILE):
         @pl.when(flag_ref[k, (first + step) * width // TILE] != 0)
         def _():
-            deep = pl.ds(k * TILE, TILE)
-            both = jnp.dot(pair_ref[:, deep], high_ref[deep, :], preferred_element_type=jnp.float32)
-            cross = jnp.dot(pair_ref[:rows, deep], low_ref[deep, :], preferred_element_type=jnp.float32)
-            total_ref[...] += both[:rows] + (both[rows:] + cross)
+            total = total_ref[...]
+            total = total + jnp.dot(
+                low_ref[:, pl.ds(k * TILE, TILE)],
+                halves_ref[pl.ds(2 * k * TILE, TILE), :],
+                preferred_element_type=jnp.float32,
+            )
+            deep = pl.ds(2 * k * TILE, 2 * TILE)
+            total_ref[...] = total + jnp.dot(
+                twice_ref[:, deep], halves_ref[deep, :], preferred_element_type=jnp.float32
+            )
     share = width // CHAINS
     for chain, (kept, sent) in enumerate(RANKS):
         columns = pl.ds(chain * share, share)
@@ -200,8 +203,8 @@
                 ref[i] = total_ref[pl.ds(peer * TILE_ROWS, TILE_ROWS), columns]
 
 
-def product(r, piece, pieces, ranks, source, int_tiles, gathered, high, low):
-    depth, width = high.shape
+def product(r, piece, pieces, ranks, source, int_tiles, gathered, halves):
+    depth, width = halves.shape[0] // 2, halves.shape[1]
     shards = depth // gathered.shape[2]
     rows = ranks * TILE_ROWS
     share = COLUMNS // CHAINS
@@ -214,17 +217,18 @@
             pipeline_mode=pl.Buffered(1),
         )
 
-    integral = pl.BlockSpec((depth, COLUMNS), lambda i, *_: (0, piece * steps + i))
+    integral = pl.BlockSpec((2 * depth, COLUMNS), lambda i, *_: (0, piece * steps + i))
     return pl.pallas_call(
         functools.partial(product_kernel, piece * steps, ranks),
         out_shape=[jax.ShapeDtypeStruct((2, TILE_ROWS, share * steps), jnp.float32)] * (2 * CHAINS),
         grid_spec=pltpu.PrefetchScalarGridSpec(
             num_scalar_prefetch=2,
             grid=(steps,),
-            in_specs=[amp(peer) for peer in range(ranks)] + [integral, integral],
+            in_specs=[amp(peer) for peer in range(ranks)] + [integral],
             out_specs=[pl.BlockSpec((2, TILE_ROWS, share), lambda i, *_: (0, 0, i))] * (2 * CHAINS),
             scratch_shapes=[
-                pltpu.VMEM((2 * rows, depth), jnp.bfloat16),
+                pltpu.VMEM((rows, 2 * depth), jnp.bfloat16),
+                pltpu.VMEM((rows, depth), jnp.bfloat16),
                 pltpu.VMEM((rows, COLUMNS), jnp.float32),
             ],
         ),
@@ -232,7 +236,7 @@
         cost_estimate=pl.CostEstimate(
             flops=6 * rows * depth * width // pieces, bytes_accessed=4 * depth * width // pieces, transcendentals=0
         ),
-    )(source, int_tiles, *[gathered] * ranks, high, low)
+    )(source, int_tiles, *[gathered] * ranks, halves)
 
 
 def relay_kernel(*refs):
@@ -309,7 +313,7 @@
 
     where, source, slot = plan(owner_tiles, jnp.stack([rank, spot]), devices, half)
     whole = take(FIRST, tiles, where, amp_tiles, amplitudes)
-    high, low = split(integrals)
+    halves = split(integrals)
     away = take(AWAY, half, where, amp_tiles, amplitudes)
     stay = take(STAY, half, where, amp_tiles, amplitudes)
     came = lax.ppermute(away, "ab", [(i, i ^ 1) for i in range(devices)])
@@ -322,12 +326,16 @@
     for index, group in enumerate(groups):
         final = index == len(groups) - 1
         if index == 0:
-            rows, high, low, *_ = lax.optimization_barrier((gathered[0], high, low, *shards[1:]))
+            rows, halves, *_ = lax.optimization_barrier((gathered[0], halves, *shards[1:]))
         else:
+            if final:
+                for entry in waiting:
+                    update = finish(*entry, *terms, update)
+                waiting = []
             rows, onward, update = lax.optimization_barrier((gathered[index], onward, update))
         sums = []
         for r, piece, pieces in group:
-            parts = product(r, piece, pieces, ranks, source, int_tiles, rows, high, low)
+            parts = product(r, piece, pieces, ranks, source, int_tiles, rows, halves)
             if sums:
                 parts, heard = lax.optimization_barrier((parts, sums[-1][1]))
                 sums[-1] = (sums[-1][0], heard)
@@ -335,22 +343,12 @@
                 parts, relayed = lax.optimization_barrier((parts, [entry[-1] for entry in waiting]))
                 waiting = [(*entry[:-1], heard) for entry, heard in zip(waiting, relayed)]
             sums.append((parts[0::2], swap(parts[1::2], (1, 2))))
-            if not final:
-                for entry in waiting:
-                    update = finish(*entry, *terms, update)
-                waiting = []
+            for entry in waiting:
+                update = finish(*entry, *terms, update)
+            waiting = []
         entries = []
         for (r, piece, _), (kept, heard) in zip(group, sums):
-            if final and waiting:
-                if entries:
-                    for entry in waiting:
-                        update = finish(*entry, *terms, update)
-                    waiting = []
-                    heard, update = lax.optimization_barrier((heard, update))
             onward = relay(kept, heard)
-            if final and waiting:
-                onward, slot = lax.optimization_barrier((onward, slot))
-                waiting = [(*entry[:2], slot, *entry[3:]) for entry in waiting]
             entries.append((r, piece, slot, kept, heard, swap(onward, (2, 1))))
         waiting = entries
     for entry in waiting:

time: 418 us -> 435 us (1.041); the launches traced: 415 us -> 441 us
  waiting for transfers between devices: 151 us -> 176 us
    ppermute x20, waiting for transfers between devices: 32 us -> 57.5 us  [swap(): lax.ppermute(array, 'cd', [(c, c ^ peer) for c in range(ranks)])]
  transfers between devices with their start and end apart: 24 -> 24, of which waited for: 7 -> 10; matrix products, arithmetic and copies ran while one was open for 1% -> 1% of each run, Pallas kernels for 47% -> 40%
where the time goes in v5:
time: 435 us; the launch traced here: 441 us
  Pallas kernels  206 us (47%)
  waiting for transfers between devices  176 us (40%)
  starting transfers between devices  35.3 us (8%)
  between operations  14 us (3%)
  local copies, waits for them, and re-layouts  7.07 us (2%)
    pallas_call x5, Pallas kernels, product(): pl.pallas_call(functools.partial(product_kernel, piece * steps, ranks), o...  137 us
    all_gather x3, waiting for transfers between devices, gather(): return lax.all_gather(array, 'ab', axis=0)  117 us
    ppermute x20, waiting for transfers between devices, swap(): lax.ppermute(array, 'cd', [(c, c ^ peer) for c in range(ranks)])  57.5 us
    ppermute x20, starting transfers between devices, swap(): lax.ppermute(array, 'cd', [(c, c ^ peer) for c in range(ranks)])  34.8 us
    pallas_call x1, Pallas kernels, split(): pl.pallas_call(split_kernel, out_shape=jax.ShapeDtypeStruct((2 * depth, w...  25 us
    pallas_call x5, Pallas kernels, finish(): pl.pallas_call(functools.partial(finish_kernel, COLUMNS), out_shape=jax.S...  20.2 us
    pallas_call x5, Pallas kernels, relay(): pl.pallas_call(relay_kernel, out_shape=[out] * CHAINS, grid=(1,), in_spec...  11.8 us
    pallas_call x3, Pallas kernels, take(): pl.pallas_call(functools.partial(take_kernel, at), out_shape=jax.ShapeDty...  10.1 us
  transfers between devices with their start and end apart: 24, of which 10 were waited for; matrix products, arithmetic and copies ran while one was open for 1% of the time, Pallas kernels for 40%

profile of v5, /device:TPU:0, one launch (start us, length us, event | category | flops | bytes accessed | tf_op | source)
XLA Modules:
  0.0 441.0 jit_solution(7706194416888528690)
XLA Ops:
  7.2 1.6 shard_map.73
  8.8 4.5 %shard_map.76 = f32[128,4096]{1,0:T(8,128)} custom-call(s32[7]{0:T(128)} %get-tuple-element.65.take_ref, s32[2,4]{1,0:T(2,128)} %flag_ref.10, f32[256,4096]{1,0:T(8,128)} %amp_ref.5), custom_call_target="tpu_custom_call" | custom-call | tf_op jit(solution)/shard_map/pallas_call | solution.py:130
  13.3 2.8 shard_map.74
  16.6 2.8 shard_map.75
  20.7 2.8 broadcast_select_fusion
  24.2 25.0 %shard_map.77.refs_4_ = bf16[8192,2048]{1,0:T(8,128)(2,1)} custom-call(f32[4096,2048]{1,0:T(8,128)} %value_ref.1), custom_call_target="tpu_custom_call" | custom-call | bytes 67108864 | tf_op jit(solution)/shard_map/pallas_call | solution.py:153
  49.9 117.4 %all-gather.11.cloned.1.call-done = f32[1024,4096]{1,0:T(8,128)} async-done(((f32[128,4096]{1,0:T(8,128)}), f32[1024,4096]{1,0:T(8,128)}) %all-gather.11.cloned.1.call-update) | async-done | bytes 16777232 | tf_op jit(solution)/shard_map/all_gather | solution.py:309
  167.2 32.1 %shard_map.79 = (f32[2,128,1024]{2,1,0:T(8,128)}, f32[2,128,1024]{2,1,0:T(8,128)}, f32[2,128,1024]{2,1,0:T(8,128)}, f32[2,128,1024]{2,1,0:T(8,128)}) custom-call(s32[16]{0:T(128)} %get-tuple-element.64.source_ref, s32[4,2]{1,0:T(4,128)} %copy.15.flag_ref, f32[8,128,4096]{2,1,0:T(8,128)} %bitcast.6, f32[8,128,4096]{2,1,0:T(8,128)} %bitcast.7, ...), custom_call_target="tpu_custom_call" | custom-call | flops 25769803776 | bytes 33554432 | tf_op jit(solution)/shard_map/pallas_call | solution.py:221
  199.4 6.8 %collective-permute-start.2 = (f32[2,128,1024]{2,1,0:T(8,128)}, f32[2,128,1024]{2,1,0:T(8,128)S(1)}, u32[]{:S(2)}, u32[]{:S(2)}) collective-permute-start(f32[2,128,1024]{2,1,0:T(8,128)} %get-tuple-element.73), channel_id=1, source_target_pairs={{0,16},{8,24},{16,0},{24,8},{1,17},{9,25},{17,1},{25,9},{2,18},{10... | collective-permute-start | bytes 3145736 | tf_op jit(solution)/shard_map/ppermute | solution.py:312
  206.2 32.2 %shard_map.78 = (f32[2,128,1024]{2,1,0:T(8,128)}, f32[2,128,1024]{2,1,0:T(8,128)}, f32[2,128,1024]{2,1,0:T(8,128)}, f32[2,128,1024]{2,1,0:T(8,128)}) custom-call(s32[16]{0:T(128)} %get-tuple-element.64.source_ref, s32[4,2]{1,0:T(4,128)} %copy.15.flag_ref, f32[8,128,4096]{2,1,0:T(8,128)} %bitcast.10, f32[8,128,4096]{2,1,0:T(8,128)} %bitcast.11, ...), custom_call_target="tpu_custom_call" | custom-call | flops 25769803776 | bytes 33554432 | tf_op jit(solution)/shard_map/pallas_call | solution.py:221
  238.5 3.9 collective-permute-start.4
  242.4 2.6 shard_map.82
  245.0 1.2 collective-permute-start.6
  246.2 17.3 %collective-permute-done.3.refs_1_.refs_2_ = f32[2,128,1024]{2,1,0:T(8,128)S(1)} collective-permute-done((f32[2,128,1024]{2,1,0:T(8,128)}, f32[2,128,1024]{2,1,0:T(8,128)S(1)}, u32[]{:S(2)}, u32[]{:S(2)}) %collective-permute-start.3) | collective-permute-done | bytes 1048608 | tf_op jit(solution)/shard_map/ppermute | solution.py:312
  263.5 2.7 collective-permute-done.4.refs_3_.refs_5_
  266.3 2.6 shard_map.80
  268.8 2.5 collective-permute-start.7
  271.3 0.8 collective-permute-start.8
  272.1 32.4 %shard_map.81 = (f32[2,128,1024]{2,1,0:T(8,128)}, f32[2,128,1024]{2,1,0:T(8,128)}, f32[2,128,1024]{2,1,0:T(8,128)}, f32[2,128,1024]{2,1,0:T(8,128)}) custom-call(s32[16]{0:T(128)} %get-tuple-element.64.source_ref, s32[4,2]{1,0:T(4,128)} %copy.15.flag_ref, f32[8,128,2048]{2,1,0:T(8,128)} %bitcast.22, f32[8,128,2048]{2,1,0:T(8,128)} %bitcast.23, ...), custom_call_target="tpu_custom_call" | custom-call | flops 25769803776 | bytes 33554432 | tf_op jit(solution)/shard_map/pallas_call | solution.py:221
  304.6 0.7 copy-done.9
  305.5 5.0 %collective-permute-start.9 = (f32[2,128,1024]{2,1,0:T(8,128)}, f32[2,128,1024]{2,1,0:T(8,128)S(1)}, u32[]{:S(2)}, u32[]{:S(2)}) collective-permute-start(f32[2,128,1024]{2,1,0:T(8,128)} %get-tuple-element.92), channel_id=1, source_target_pairs={{0,8},{8,0},{16,24},{24,16},{1,9},{9,1},{17,25},{25,17},{2,10},{10... | collective-permute-start | bytes 3145736 | tf_op jit(solution)/shard_map/ppermute | solution.py:312
  310.5 14.6 %collective-permute-done.10.refs_3_.refs_5_ = f32[2,128,1024]{2,1,0:T(8,128)S(1)} collective-permute-done((f32[2,128,1024]{2,1,0:T(8,128)}, f32[2,128,1024]{2,1,0:T(8,128)S(1)}, u32[]{:S(2)}, u32[]{:S(2)}) %collective-permute-start.10) | collective-permute-done | bytes 1048608 | tf_op jit(solution)/shard_map/ppermute | solution.py:312
  325.2 9.2 %collective-permute-done.9.refs_1_.refs_2_ = f32[2,128,1024]{2,1,0:T(8,128)S(1)} collective-permute-done((f32[2,128,1024]{2,1,0:T(8,128)}, f32[2,128,1024]{2,1,0:T(8,128)S(1)}, u32[]{:S(2)}, u32[]{:S(2)}) %collective-permute-start.9) | collective-permute-done | bytes 1048608 | tf_op jit(solution)/shard_map/ppermute | solution.py:312
  334.3 1.0 copy-done.4
  335.4 2.5 shard_map.83
  338.2 2.7 collective-permute-start.12
  340.9 4.5 %shard_map.84.refs_9_ = f32[512,2048]{1,0:T(8,128)} custom-call(s32[4]{0:T(128)} %get-tuple-element.63.refs_0_, f32[2,128,1024]{2,1,0:T(8,128)} %get-tuple-element.85.refs_0_.refs_1_, f32[2,128,1024]{2,1,0:T(8,128)} %copy-done, f32[128,1024]{1,0:T(8,128)} %copy-done.9, f32[2,128,1024]{2,1,0:T(8,128)} %get-tuple-element.87.refs_2_.refs_4_, ...), custom_call_target="tpu_custom_call" | custom-call | bytes 6291456 | tf_op jit(solution)/shard_map/pallas_call | solution.py:280
  345.4 4.5 %shard_map.85.refs_9_ = f32[512,2048]{1,0:T(8,128)} custom-call(s32[4]{0:T(128)} %get-tuple-element.63.refs_0_, f32[2,128,1024]{2,1,0:T(8,128)} %get-tuple-element.74.refs_0_.refs_1_, f32[2,128,1024]{2,1,0:T(8,128)} %copy-done.2, f32[128,1024]{1,0:T(8,128)} %copy-done.11, ...), custom_call_target="tpu_custom_call", output_to_operand_aliasing={{}: (9, {})} | custom-call | bytes 6291456 | tf_op jit(solution)/shard_map/pallas_call | solution.py:280
  349.9 1.8 collective-permute-done.11.refs_3_
  351.7 1.0 collective-permute-done.12.refs_6_
  352.7 0.8 copy-done.14
  353.5 4.5 %shard_map.86.refs_9_ = f32[512,2048]{1,0:T(8,128)} custom-call(s32[4]{0:T(128)} %get-tuple-element.63.refs_0_, f32[2,128,1024]{2,1,0:T(8,128)} %get-tuple-element.91.refs_0_.refs_1_, f32[2,128,1024]{2,1,0:T(8,128)} %copy-done.4, f32[128,1024]{1,0:T(8,128)} %copy-done.13, ...), custom_call_target="tpu_custom_call", output_to_operand_aliasing={{}: (9, {})} | custom-call | bytes 6291456 | tf_op jit(solution)/shard_map/pallas_call | solution.py:280
  358.0 20.0 %shard_map.88 = (f32[2,128,512]{2,1,0:T(8,128)}, f32[2,128,512]{2,1,0:T(8,128)}, f32[2,128,512]{2,1,0:T(8,128)}, f32[2,128,512]{2,1,0:T(8,128)}) custom-call(s32[16]{0:T(128)} %get-tuple-element.64.source_ref, s32[4,2]{1,0:T(4,128)} %copy.15.flag_ref, f32[8,128,2048]{2,1,0:T(8,128)} %bitcast.14, f32[8,128,2048]{2,1,0:T(8,128)} %bitcast.15, ...), custom_call_target="tpu_custom_call" | custom-call | flops 12884901888 | bytes 16777216 | tf_op jit(solution)/shard_map/pallas_call | solution.py:221
  378.0 2.8 collective-permute-start.14
  380.8 20.3 %shard_map.87 = (f32[2,128,512]{2,1,0:T(8,128)}, f32[2,128,512]{2,1,0:T(8,128)}, f32[2,128,512]{2,1,0:T(8,128)}, f32[2,128,512]{2,1,0:T(8,128)}) custom-call(s32[16]{0:T(128)} %get-tuple-element.64.source_ref, s32[4,2]{1,0:T(4,128)} %copy.15.flag_ref, f32[8,128,2048]{2,1,0:T(8,128)} %bitcast.18, f32[8,128,2048]{2,1,0:T(8,128)} %bitcast.19, ...), custom_call_target="tpu_custom_call" | custom-call | flops 12884901888 | bytes 16777216 | tf_op jit(solution)/shard_map/pallas_call | solution.py:221
  401.2 5.1 %collective-permute-start.16 = (f32[2,128,512]{2,1,0:T(8,128)}, f32[2,128,512]{2,1,0:T(8,128)S(1)}, u32[]{:S(2)}, u32[]{:S(2)}) collective-permute-start(f32[2,128,512]{2,1,0:T(8,128)} %get-tuple-element.111), channel_id=1, source_target_pairs={{0,16},{8,24},{16,0},{24,8},{1,17},{9,25},{17,1},{25,9},{2,18},{10... | collective-permute-start | bytes 1572872 | tf_op jit(solution)/shard_map/ppermute | solution.py:312
  406.3 2.0 shard_map.90
  408.4 0.9 collective-permute-start.20
  409.2 7.0 %collective-permute-done.15.refs_1_.refs_2_ = f32[2,128,512]{2,1,0:T(8,128)S(1)} collective-permute-done((f32[2,128,512]{2,1,0:T(8,128)}, f32[2,128,512]{2,1,0:T(8,128)S(1)}, u32[]{:S(2)}, u32[]{:S(2)}) %collective-permute-start.15) | collective-permute-done | bytes 524320 | tf_op jit(solution)/shard_map/ppermute | solution.py:312
  416.2 3.1 collective-permute-done.16.refs_3_.refs_5_
  419.4 0.8 copy-done.8
  420.2 2.0 shard_map.89
  422.2 1.6 collective-permute-start.17
  423.8 1.1 collective-permute-start.18
  424.9 0.7 copy-done.15
  426.3 3.3 shard_map.91.refs_9_
  429.7 0.7 collective-permute-done.18.refs_6_
  431.1 3.3 shard_map.92
  (69 shorter events, 5.3 us)
Async XLA Ops:
  6.5 160.7 %all-gather.11.cloned.1.call-start = ((), (), s32[]{:S(2)}) async-start(), calls=%async_computation.2 | async-start | bytes 18874368 | tf_op jit(solution)/shard_map/all_gather | solution.py:309
  13.3 6.1 %copy-start.19 = (s32[7]{0:T(128)S(1)}, s32[7]{0:T(128)}, u32[]{:S(2)}) copy-start(s32[7]{0:T(128)} %get-tuple-element.65.take_ref) | copy-start | bytes 88
  13.3 258.8 %all-gather.9.cloned.1.call-start = ((), (), s32[]{:S(2)}) async-start(), calls=%async_computation.1 | async-start | bytes 9437184 | tf_op jit(solution)/shard_map/all_gather | solution.py:309
  16.2 4.5 %collective-permute-start = (f32[128,2048]{1,0:T(8,128)}, f32[128,2048]{1,0:T(8,128)S(1)}, u32[]{:S(2)}, u32[]{:S(2)}) collective-permute-start(f32[128,2048]{1,0:T(8,128)} %shard_map.74), channel_id=1, source_target_pairs={{0,1},{1,0},{2,3},{3,2},{4,5},{5,4},{6,7},{7,6},{8,9},{9,8},{10,11... | collective-permute-start | bytes 3145736 | tf_op jit(solution)/shard_map/ppermute | solution.py:319
  23.5 334.6 %all-gather.7.cloned.1.call-start = ((), (), s32[]{:S(2)}) async-start(), calls=%async_computation | async-start | bytes 9437184 | tf_op jit(solution)/shard_map/all_gather | solution.py:309
  24.2 25.0 %copy-start.20 = (s32[4,2]{0,1:T(2,128)S(1)}, s32[4,2]{0,1:T(2,128)}, u32[]{:S(2)}) copy-start(s32[4,2]{0,1:T(2,128)} %param.10) | copy-start | bytes 100
  199.3 39.1 %collective-permute-start.1 = (f32[2,128,1024]{2,1,0:T(8,128)}, f32[2,128,1024]{2,1,0:T(8,128)S(1)}, u32[]{:S(2)}, u32[]{:S(2)}) collective-permute-start(f32[2,128,1024]{2,1,0:T(8,128)} %get-tuple-element.72), channel_id=1, source_target_pairs={{0,8},{8,0},{16,24},{24,16},{1,9},{9,1},{17,25},{25,17},{2,10},{10... | collective-permute-start | bytes 3145736 | tf_op jit(solution)/shard_map/ppermute | solution.py:312
  199.4 39.1 %collective-permute-start.2 = (f32[2,128,1024]{2,1,0:T(8,128)}, f32[2,128,1024]{2,1,0:T(8,128)S(1)}, u32[]{:S(2)}, u32[]{:S(2)}) collective-permute-start(f32[2,128,1024]{2,1,0:T(8,128)} %get-tuple-element.73), channel_id=1, source_target_pairs={{0,16},{8,24},{16,0},{24,8},{1,17},{9,25},{17,1},{25,9},{2,18},{10... | collective-permute-start | bytes 3145736 | tf_op jit(solution)/shard_map/ppermute | solution.py:312
  238.4 4.0 copy-start
  238.4 4.0 copy-start.1
  238.4 25.1 %collective-permute-start.3 = (f32[2,128,1024]{2,1,0:T(8,128)}, f32[2,128,1024]{2,1,0:T(8,128)S(1)}, u32[]{:S(2)}, u32[]{:S(2)}) collective-permute-start(f32[2,128,1024]{2,1,0:T(8,128)} %get-tuple-element.75), channel_id=1, source_target_pairs={{0,8},{8,0},{16,24},{24,16},{1,9},{9,1},{17,25},{25,17},{2,10},{10... | collective-permute-start | bytes 3145736 | tf_op jit(solution)/shard_map/ppermute | solution.py:312
  238.5 27.7 %collective-permute-start.4 = (f32[2,128,1024]{2,1,0:T(8,128)}, f32[2,128,1024]{2,1,0:T(8,128)}, u32[]{:S(2)}, u32[]{:S(2)}) collective-permute-start(f32[2,128,1024]{2,1,0:T(8,128)} %get-tuple-element.77), channel_id=1, source_target_pairs={{0,16},{8,24},{16,0},{24,8},{1,17},{9,25},{17,1},{25,9},{2,18},{10... | collective-permute-start | bytes 3145736 | tf_op jit(solution)/shard_map/ppermute | solution.py:312
  245.0 59.5 %collective-permute-start.5 = (f32[128,1024]{1,0:T(8,128)}, f32[128,1024]{1,0:T(8,128)S(1)}, u32[]{:S(2)}, u32[]{:S(2)}) collective-permute-start(f32[128,1024]{1,0:T(8,128)} %get-tuple-element.89), channel_id=1, source_target_pairs={{0,16},{8,24},{16,0},{24,8},{1,17},{9,25},{17,1},{25,9},{2,18},{10... | collective-permute-start | bytes 1572872 | tf_op jit(solution)/shard_map/ppermute | solution.py:312
  245.0 59.5 %collective-permute-start.6 = (f32[128,1024]{1,0:T(8,128)}, f32[128,1024]{1,0:T(8,128)S(1)}, u32[]{:S(2)}, u32[]{:S(2)}) collective-permute-start(f32[128,1024]{1,0:T(8,128)} %get-tuple-element.90), channel_id=1, source_target_pairs={{0,8},{8,0},{16,24},{24,16},{1,9},{9,1},{17,25},{25,17},{2,10},{10... | collective-permute-start | bytes 1572872 | tf_op jit(solution)/shard_map/ppermute | solution.py:312
  263.5 2.8 copy-start.2
  268.8 35.7 %collective-permute-start.7 = (f32[128,1024]{1,0:T(8,128)}, f32[128,1024]{1,0:T(8,128)S(1)}, u32[]{:S(2)}, u32[]{:S(2)}) collective-permute-start(f32[128,1024]{1,0:T(8,128)} %get-tuple-element.78), channel_id=1, source_target_pairs={{0,16},{8,24},{16,0},{24,8},{1,17},{9,25},{17,1},{25,9},{2,18},{10... | collective-permute-start | bytes 1572872 | tf_op jit(solution)/shard_map/ppermute | solution.py:312
  271.3 33.3 %collective-permute-start.8 = (f32[128,1024]{1,0:T(8,128)}, f32[128,1024]{1,0:T(8,128)S(1)}, u32[]{:S(2)}, u32[]{:S(2)}) collective-permute-start(f32[128,1024]{1,0:T(8,128)} %get-tuple-element.79), channel_id=1, source_target_pairs={{0,8},{8,0},{16,24},{24,16},{1,9},{9,1},{17,25},{25,17},{2,10},{10... | collective-permute-start | bytes 1572872 | tf_op jit(solution)/shard_map/ppermute | solution.py:312
  304.5 0.8 copy-start.9
  304.6 1.0 copy-start.10
  304.6 40.8 %copy-start.11 = (f32[128,1024]{1,0:T(8,128)}, f32[128,1024]{1,0:T(8,128)S(1)}, u32[]{:S(2)}) copy-start(f32[128,1024]{1,0:T(8,128)S(1)} %collective-permute-done.7.refs_3_) | copy-start | bytes 1572868
  304.6 40.8 %copy-start.12 = (f32[128,1024]{1,0:T(8,128)}, f32[128,1024]{1,0:T(8,128)S(1)}, u32[]{:S(2)}) copy-start(f32[128,1024]{1,0:T(8,128)S(1)} %collective-permute-done.8.refs_6_) | copy-start | bytes 1572868
  305.5 19.6 %collective-permute-start.10 = (f32[2,128,1024]{2,1,0:T(8,128)}, f32[2,128,1024]{2,1,0:T(8,128)S(1)}, u32[]{:S(2)}, u32[]{:S(2)}) collective-permute-start(f32[2,128,1024]{2,1,0:T(8,128)} %get-tuple-element.94), channel_id=1, source_target_pairs={{0,16},{8,24},{16,0},{24,8},{1,17},{9,25},{17,1},{25,9},{2,18},{10... | collective-permute-start | bytes 3145736 | tf_op jit(solution)/shard_map/ppermute | solution.py:312
  305.5 28.8 %collective-permute-start.9 = (f32[2,128,1024]{2,1,0:T(8,128)}, f32[2,128,1024]{2,1,0:T(8,128)S(1)}, u32[]{:S(2)}, u32[]{:S(2)}) collective-permute-start(f32[2,128,1024]{2,1,0:T(8,128)} %get-tuple-element.92), channel_id=1, source_target_pairs={{0,8},{8,0},{16,24},{24,16},{1,9},{9,1},{17,25},{25,17},{2,10},{10... | collective-permute-start | bytes 3145736 | tf_op jit(solution)/shard_map/ppermute | solution.py:312
  325.2 9.2 %copy-start.3 = (f32[2,128,1024]{2,1,0:T(8,128)}, f32[2,128,1024]{2,1,0:T(8,128)S(1)}, u32[]{:S(2)}) copy-start(f32[2,128,1024]{2,1,0:T(8,128)S(1)} %collective-permute-done.10.refs_3_.refs_5_) | copy-start | bytes 3145732
  334.3 1.0 copy-start.4
  337.9 13.8 %collective-permute-start.11 = (f32[128,1024]{1,0:T(8,128)}, f32[128,1024]{1,0:T(8,128)S(1)}, u32[]{:S(2)}, u32[]{:S(2)}) collective-permute-start(f32[128,1024]{1,0:T(8,128)} %get-tuple-element.95), channel_id=1, source_target_pairs={{0,16},{8,24},{16,0},{24,8},{1,17},{9,25},{17,1},{25,9},{2,18},{10... | collective-permute-start | bytes 1572872 | tf_op jit(solution)/shard_map/ppermute | solution.py:312
  338.2 14.5 %collective-permute-start.12 = (f32[128,1024]{1,0:T(8,128)}, f32[128,1024]{1,0:T(8,128)S(1)}, u32[]{:S(2)}, u32[]{:S(2)}) collective-permute-start(f32[128,1024]{1,0:T(8,128)} %get-tuple-element.96), channel_id=1, source_target_pairs={{0,8},{8,0},{16,24},{24,16},{1,9},{9,1},{17,25},{25,17},{2,10},{10... | collective-permute-start | bytes 1572872 | tf_op jit(solution)/shard_map/ppermute | solution.py:312
  351.7 1.0 copy-start.13
  352.7 0.8 copy-start.14
  378.0 23.1 %collective-permute-start.13 = (f32[2,128,512]{2,1,0:T(8,128)}, f32[2,128,512]{2,1,0:T(8,128)S(1)}, u32[]{:S(2)}, u32[]{:S(2)}) collective-permute-start(f32[2,128,512]{2,1,0:T(8,128)} %get-tuple-element.106), channel_id=1, source_target_pairs={{0,8},{8,0},{16,24},{24,16},{1,9},{9,1},{17,25},{25,17},{2,10},{10... | collective-permute-start | bytes 1572872 | tf_op jit(solution)/shard_map/ppermute | solution.py:312
  378.0 23.1 %collective-permute-start.14 = (f32[2,128,512]{2,1,0:T(8,128)}, f32[2,128,512]{2,1,0:T(8,128)S(1)}, u32[]{:S(2)}, u32[]{:S(2)}) collective-permute-start(f32[2,128,512]{2,1,0:T(8,128)} %get-tuple-element.107), channel_id=1, source_target_pairs={{0,16},{8,24},{16,0},{24,8},{1,17},{9,25},{17,1},{25,9},{2,18},{10... | collective-permute-start | bytes 1572872 | tf_op jit(solution)/shard_map/ppermute | solution.py:312
  401.1 5.2 %copy-start.5 = (f32[2,128,512]{2,1,0:T(8,128)}, f32[2,128,512]{2,1,0:T(8,128)S(1)}, u32[]{:S(2)}) copy-start(f32[2,128,512]{2,1,0:T(8,128)S(1)} %collective-permute-done.13.refs_1_.refs_2_) | copy-start | bytes 1572868
  401.1 5.2 %copy-start.6 = (f32[2,128,512]{2,1,0:T(8,128)}, f32[2,128,512]{2,1,0:T(8,128)S(1)}, u32[]{:S(2)}) copy-start(f32[2,128,512]{2,1,0:T(8,128)S(1)} %collective-permute-done.14.refs_3_.refs_5_) | copy-start | bytes 1572868
  401.1 15.1 %collective-permute-start.15 = (f32[2,128,512]{2,1,0:T(8,128)}, f32[2,128,512]{2,1,0:T(8,128)S(1)}, u32[]{:S(2)}, u32[]{:S(2)}) collective-permute-start(f32[2,128,512]{2,1,0:T(8,128)} %get-tuple-element.109), channel_id=1, source_target_pairs={{0,8},{8,0},{16,24},{24,16},{1,9},{9,1},{17,25},{25,17},{2,10},{10... | collective-permute-start | bytes 1572872 | tf_op jit(solution)/shard_map/ppermute | solution.py:312
  401.2 18.1 %collective-permute-start.16 = (f32[2,128,512]{2,1,0:T(8,128)}, f32[2,128,512]{2,1,0:T(8,128)S(1)}, u32[]{:S(2)}, u32[]{:S(2)}) collective-permute-start(f32[2,128,512]{2,1,0:T(8,128)} %get-tuple-element.111), channel_id=1, source_target_pairs={{0,16},{8,24},{16,0},{24,8},{1,17},{9,25},{17,1},{25,9},{2,18},{10... | collective-permute-start | bytes 1572872 | tf_op jit(solution)/shard_map/ppermute | solution.py:312
  408.3 16.6 %collective-permute-start.19 = (f32[128,512]{1,0:T(8,128)}, f32[128,512]{1,0:T(8,128)S(1)}, u32[]{:S(2)}, u32[]{:S(2)}) collective-permute-start(f32[128,512]{1,0:T(8,128)} %get-tuple-element.118), channel_id=1, source_target_pairs={{0,16},{8,24},{16,0},{24,8},{1,17},{9,25},{17,1},{25,9},{2,18},{10... | collective-permute-start | bytes 786440 | tf_op jit(solution)/shard_map/ppermute | solution.py:312
  408.4 16.6 %collective-permute-start.20 = (f32[128,512]{1,0:T(8,128)}, f32[128,512]{1,0:T(8,128)S(1)}, u32[]{:S(2)}, u32[]{:S(2)}) collective-permute-start(f32[128,512]{1,0:T(8,128)} %get-tuple-element.119), channel_id=1, source_target_pairs={{0,8},{8,0},{16,24},{24,16},{1,9},{9,1},{17,25},{25,17},{2,10},{10... | collective-permute-start | bytes 786440 | tf_op jit(solution)/shard_map/ppermute | solution.py:312
  416.2 3.1 copy-start.7
  419.4 0.8 copy-start.8
  422.2 7.5 %collective-permute-start.17 = (f32[128,512]{1,0:T(8,128)}, f32[128,512]{1,0:T(8,128)S(1)}, u32[]{:S(2)}, u32[]{:S(2)}) collective-permute-start(f32[128,512]{1,0:T(8,128)} %get-tuple-element.112), channel_id=1, source_target_pairs={{0,16},{8,24},{16,0},{24,8},{1,17},{9,25},{17,1},{25,9},{2,18},{10... | collective-permute-start | bytes 786440 | tf_op jit(solution)/shard_map/ppermute | solution.py:312
  423.8 6.6 %collective-permute-start.18 = (f32[128,512]{1,0:T(8,128)}, f32[128,512]{1,0:T(8,128)S(1)}, u32[]{:S(2)}, u32[]{:S(2)}) collective-permute-start(f32[128,512]{1,0:T(8,128)} %get-tuple-element.113), channel_id=1, source_target_pairs={{0,8},{8,0},{16,24},{24,16},{1,9},{9,1},{17,25},{25,17},{2,10},{10... | collective-permute-start | bytes 786440 | tf_op jit(solution)/shard_map/ppermute | solution.py:312
  424.9 0.7 copy-start.15
  425.6 0.7 copy-start.16
  429.7 0.7 copy-start.17
  430.4 0.7 copy-start.18
Sparse Core Ops, SparseCore 0:
  13.4 153.7 all-gather.10
  168.8 80.2 all-gather.8
  250.8 80.5 all-gather.6

commit v6 on v5

--- a/solution.py
+++ b/solution.py
@@ -203,12 +203,11 @@
                 ref[i] = total_ref[pl.ds(peer * TILE_ROWS, TILE_ROWS), columns]
 
 
-def product(r, piece, pieces, ranks, source, int_tiles, gathered, halves):
+def product(r, first, steps, ranks, source, int_tiles, gathered, halves):
     depth, width = halves.shape[0] // 2, halves.shape[1]
     shards = depth // gathered.shape[2]
     rows = ranks * TILE_ROWS
     share = COLUMNS // CHAINS
-    steps = width // COLUMNS // pieces
 
     def amp(peer):
         return pl.BlockSpec(
@@ -217,9 +216,9 @@
             pipeline_mode=pl.Buffered(1),
         )
 
-    integral = pl.BlockSpec((2 * depth, COLUMNS), lambda i, *_: (0, piece * steps + i))
-    return pl.pallas_call(
-        functools.partial(product_kernel, piece * steps, ranks),
+    integral = pl.BlockSpec((2 * depth, COLUMNS), lambda i, *_: (0, first + i))
+    return pl.pallas_call(
+        functools.partial(product_kernel, first, ranks),
         out_shape=[jax.ShapeDtypeStruct((2, TILE_ROWS, share * steps), jnp.float32)] * (2 * CHAINS),
         grid_spec=pltpu.PrefetchScalarGridSpec(
             num_scalar_prefetch=2,
@@ -234,7 +233,7 @@
         ),
         compiler_params=pltpu.CompilerParams(vmem_limit_bytes=VMEM_BYTES),
         cost_estimate=pl.CostEstimate(
-            flops=6 * rows * depth * width // pieces, bytes_accessed=4 * depth * width // pieces, transcendentals=0
+            flops=6 * rows * depth * steps * COLUMNS, bytes_accessed=4 * depth * steps * COLUMNS, transcendentals=0
         ),
     )(source, int_tiles, *[gathered] * ranks, halves)
 
@@ -270,12 +269,12 @@
             out_ref[:, target] = (total + term_ref[:, target]) / denominator_ref[:, target]
 
 
-def finish(r, piece, slot, kept, heard, relayed, other_terms, denominators, update):
+def finish(r, start, slot, kept, heard, relayed, other_terms, denominators, update):
     share = kept[0].shape[2]
     width = share * CHAINS
     first = pl.BlockSpec((1, TILE_ROWS, share), lambda i, slot: (0, 0, 0))
     whole = pl.BlockSpec((TILE_ROWS, share), lambda i, slot: (0, 0))
-    owned = pl.BlockSpec((TILE_ROWS, width), lambda i, slot: (slot[r], piece))
+    owned = pl.BlockSpec((TILE_ROWS, width), lambda i, slot: (slot[r], start * COLUMNS // width))
     before = [] if update is None else [update]
     return pl.pallas_call(
         functools.partial(finish_kernel, COLUMNS),
@@ -320,40 +319,50 @@
     mine = where[WHOSE] == 0
     shards = [whole, jnp.where(mine, stay, came), jnp.where(mine, came, stay)]
     gathered = [gather(shard) for shard in shards]
-    groups = [[(0, 0, 1), (1, 0, 1)], [(2, 0, 1)], [(3, 0, 2), (3, 1, 2)]]
     terms = (other_terms, denominators)
-    update, waiting = None, []
-    for index, group in enumerate(groups):
-        final = index == len(groups) - 1
-        if index == 0:
-            rows, halves, *_ = lax.optimization_barrier((gathered[0], halves, *shards[1:]))
-        else:
-            if final:
-                for entry in waiting:
-                    update = finish(*entry, *terms, update)
-                waiting = []
-            rows, onward, update = lax.optimization_barrier((gathered[index], onward, update))
-        sums = []
-        for r, piece, pieces in group:
-            parts = product(r, piece, pieces, ranks, source, int_tiles, rows, halves)
-            if sums:
-                parts, heard = lax.optimization_barrier((parts, sums[-1][1]))
-                sums[-1] = (sums[-1][0], heard)
-            elif waiting:
-                parts, relayed = lax.optimization_barrier((parts, [entry[-1] for entry in waiting]))
-                waiting = [(*entry[:-1], heard) for entry, heard in zip(waiting, relayed)]
-            sums.append((parts[0::2], swap(parts[1::2], (1, 2))))
-            for entry in waiting:
-                update = finish(*entry, *terms, update)
-            waiting = []
-        entries = []
-        for (r, piece, _), (kept, heard) in zip(group, sums):
-            onward = relay(kept, heard)
-            entries.append((r, piece, slot, kept, heard, swap(onward, (2, 1))))
-        waiting = entries
-    for entry in waiting:
-        update = finish(*entry, *terms, update)
-    return update
+    tie = lax.optimization_barrier
+    steps = halves.shape[1] // COLUMNS
+    most = steps * 3 // 4
+
+    def begin(r, rows, first=0, count=steps):
+        return product(r, first, count, ranks, source, int_tiles, rows, halves)
+
+    def send(parts):
+        return swap(parts[1::2], (1, 2))
+
+    def pass_on(parts, heard):
+        onward = relay(parts[0::2], heard)
+        return onward, swap(onward, (2, 1))
+
+    rows, halves, *_ = tie((gathered[0], halves, *shards[1:]))
+    parts0 = begin(0, rows)
+    heard0 = send(parts0)
+    parts1, heard0 = tie((begin(1, rows), heard0))
+    heard1 = send(parts1)
+    onward, relayed0 = pass_on(parts0, heard0)
+
+    rows, onward = tie((gathered[1], onward))
+    parts2, relayed0, heard1 = tie((begin(2, rows), relayed0, heard1))
+    heard2 = send(parts2)
+    onward, relayed1 = pass_on(parts1, heard1)
+    slot, onward = tie((slot, onward))
+    update = finish(0, 0, slot, parts0[0::2], heard0, relayed0, *terms, None)
+    heard2, update = tie((heard2, update))
+    onward, relayed2 = pass_on(parts2, heard2)
+    update = finish(1, 0, slot, parts1[0::2], heard1, relayed1, *terms, update)
+
+    rows, onward, update = tie((gathered[2], onward, update))
+    parts3, relayed2 = tie((begin(3, rows, 0, most), relayed2))
+    heard3 = send(parts3)
+    parts4, heard3 = tie((begin(3, rows, most, steps - most), heard3))
+    heard4 = send(parts4)
+    onward, relayed3 = pass_on(parts3, heard3)
+    slot, onward = tie((slot, onward))
+    update = finish(2, 0, slot, parts2[0::2], heard2, relayed2, *terms, update)
+    heard4, update = tie((heard4, update))
+    _, relayed4 = pass_on(parts4, heard4)
+    update = finish(3, 0, slot, parts3[0::2], heard3, relayed3, *terms, update)
+    return finish(3, most, slot, parts4[0::2], heard4, relayed4, *terms, update)
 
 
 def solution(mesh):

time: 435 us -> 414 us (0.952); the launches traced: 441 us -> 410 us
  waiting for transfers between devices: 176 us -> 148 us
  starting transfers between devices: 35.3 us -> 23.3 us
  local copies, waits for them, and re-layouts: 7.07 us -> 11.8 us
    ppermute x20, waiting for transfers between devices: 57.5 us -> 19.6 us  [swap(): lax.ppermute(array, 'cd', [(c, c ^ peer) for c in range(ranks)])]
    ppermute x20, starting transfers between devices: 34.8 us -> 22.7 us  [swap(): lax.ppermute(array, 'cd', [(c, c ^ peer) for c in range(ranks)])]
    all_gather x3, waiting for transfers between devices: 117 us -> 128 us  [gather(): return lax.all_gather(array, 'ab', axis=0)]
    unnamed x43 -> x47, local copies, waits for them, and re-layouts: 6.47 us -> 11.2 us
  transfers between devices with their start and end apart: 24 -> 24, of which waited for: 10 -> 8; matrix products, arithmetic and copies ran while one was open for 1% -> 1% of each run, Pallas kernels for 40% -> 49%
where the time goes in v6:
time: 414 us; the launch traced here: 410 us
  Pallas kernels  210 us (51%)
  waiting for transfers between devices  148 us (36%)
  starting transfers between devices  23.3 us (6%)
  between operations  13.9 us (3%)
  local copies, waits for them, and re-layouts  11.8 us (3%)
    pallas_call x5, Pallas kernels, product(): pl.pallas_call(functools.partial(product_kernel, first, ranks), out_shape...  140 us
    all_gather x3, waiting for transfers between devices, gather(): return lax.all_gather(array, 'ab', axis=0)  128 us
    pallas_call x1, Pallas kernels, split(): pl.pallas_call(split_kernel, out_shape=jax.ShapeDtypeStruct((2 * depth, w...  26.4 us
    ppermute x20, starting transfers between devices, swap(): lax.ppermute(array, 'cd', [(c, c ^ peer) for c in range(ranks)])  22.7 us
    pallas_call x5, Pallas kernels, finish(): pl.pallas_call(functools.partial(finish_kernel, COLUMNS), out_shape=jax.S...  20.3 us
    ppermute x20, waiting for transfers between devices, swap(): lax.ppermute(array, 'cd', [(c, c ^ peer) for c in range(ranks)])  19.6 us
    pallas_call x5, Pallas kernels, relay(): pl.pallas_call(relay_kernel, out_shape=[out] * CHAINS, grid=(1,), in_spec...  11.9 us
    unnamed x47, local copies, waits for them, and re-layouts  11.2 us
  transfers between devices with their start and end apart: 24, of which 8 were waited for; matrix products, arithmetic and copies ran while one was open for 1% of the time, Pallas kernels for 49%

profile of v6, /device:TPU:0, one launch (start us, length us, event | category | flops | bytes accessed | tf_op | source)
XLA Modules:
  0.0 410.4 jit_solution(14578572961834710122)
XLA Ops:
  7.1 1.6 shard_map.73
  8.7 4.5 %shard_map.74 = f32[128,4096]{1,0:T(8,128)} custom-call(s32[7]{0:T(128)} %get-tuple-element.79.take_ref, s32[2,4]{1,0:T(2,128)} %flag_ref.10, f32[256,4096]{1,0:T(8,128)} %amp_ref.5), custom_call_target="tpu_custom_call" | custom-call | tf_op jit(solution)/shard_map/pallas_call | solution.py:130
  13.3 2.9 shard_map.77
  16.6 2.8 shard_map.76
  20.5 2.7 broadcast_select_fusion
  24.6 26.4 %shard_map.75.refs_4_ = bf16[8192,2048]{1,0:T(8,128)(2,1)} custom-call(f32[4096,2048]{1,0:T(8,128)} %value_ref.1), custom_call_target="tpu_custom_call" | custom-call | bytes 67108864 | tf_op jit(solution)/shard_map/pallas_call | solution.py:153
  51.1 116.1 %all-gather.7.cloned.1.call-done = f32[1024,4096]{1,0:T(8,128)} async-done(((f32[128,4096]{1,0:T(8,128)}), f32[1024,4096]{1,0:T(8,128)}) %all-gather.7.cloned.1.call-update) | async-done | bytes 16777232 | tf_op jit(solution)/shard_map/all_gather | solution.py:308
  167.2 32.8 %shard_map.79 = (f32[2,128,1024]{2,1,0:T(8,128)}, f32[2,128,1024]{2,1,0:T(8,128)}, f32[2,128,1024]{2,1,0:T(8,128)}, f32[2,128,1024]{2,1,0:T(8,128)}) custom-call(s32[16]{0:T(128)} %get-tuple-element.78.source_ref, s32[4,2]{1,0:T(4,128)} %copy.12.flag_ref, f32[8,128,4096]{2,1,0:T(8,128)} %bitcast.6, f32[8,128,4096]{2,1,0:T(8,128)} %bitcast.7, ...), custom_call_target="tpu_custom_call" | custom-call | flops 25769803776 | bytes 33554432 | tf_op jit(solution)/shard_map/pallas_call | solution.py:220
  200.0 2.2 collective-permute-start.2
  202.2 32.8 %shard_map.78 = (f32[2,128,1024]{2,1,0:T(8,128)}, f32[2,128,1024]{2,1,0:T(8,128)}, f32[2,128,1024]{2,1,0:T(8,128)}, f32[2,128,1024]{2,1,0:T(8,128)}) custom-call(s32[16]{0:T(128)} %get-tuple-element.78.source_ref, s32[4,2]{1,0:T(4,128)} %copy.12.flag_ref, f32[8,128,4096]{2,1,0:T(8,128)} %bitcast.10, f32[8,128,4096]{2,1,0:T(8,128)} %bitcast.11, ...), custom_call_target="tpu_custom_call" | custom-call | flops 25769803776 | bytes 33554432 | tf_op jit(solution)/shard_map/pallas_call | solution.py:220
  235.1 1.0 copy-done.2
  236.4 2.6 shard_map.80
  239.0 1.2 collective-permute-start.4
  240.2 8.9 %all-gather.9.cloned.1.call-done = f32[1024,2048]{1,0:T(8,128)} async-done(((f32[128,2048]{1,0:T(8,128)}), f32[1024,2048]{1,0:T(8,128)}) %all-gather.9.cloned.1.call-update) | async-done | bytes 8388624 | tf_op jit(solution)/shard_map/all_gather | solution.py:308
  249.1 1.5 collective-permute-start.5
  250.6 1.5 collective-permute-start.6
  252.1 33.5 %shard_map.81 = (f32[2,128,1024]{2,1,0:T(8,128)}, f32[2,128,1024]{2,1,0:T(8,128)}, f32[2,128,1024]{2,1,0:T(8,128)}, f32[2,128,1024]{2,1,0:T(8,128)}) custom-call(s32[16]{0:T(128)} %get-tuple-element.78.source_ref, s32[4,2]{1,0:T(4,128)} %copy.12.flag_ref, f32[8,128,2048]{2,1,0:T(8,128)} %bitcast.22, f32[8,128,2048]{2,1,0:T(8,128)} %bitcast.23, ...), custom_call_target="tpu_custom_call" | custom-call | flops 25769803776 | bytes 33554432 | tf_op jit(solution)/shard_map/pallas_call | solution.py:220
  285.7 1.1 copy-done.12
  287.3 2.6 shard_map.82
  289.9 1.6 collective-permute-start.9
  291.5 2.0 collective-permute-start.10
  293.6 4.5 %shard_map.83.refs_9_ = f32[512,2048]{1,0:T(8,128)} custom-call(s32[4]{0:T(128)} %get-tuple-element.136.refs_0_, f32[2,128,1024]{2,1,0:T(8,128)} %get-tuple-element.89.refs_0_.refs_1_, f32[2,128,1024]{2,1,0:T(8,128)} %copy-done.2, f32[128,1024]{1,0:T(8,128)} %copy-done.12, f32[2,128,1024]{2,1,0:T(8,128)} %get-tuple-element.91.refs_2_.refs_4_, ...), custom_call_target="tpu_custom_call" | custom-call | bytes 6291456 | tf_op jit(solution)/shard_map/pallas_call | solution.py:279
  298.1 13.2 %collective-permute-done.7.refs_1_.refs_2_ = f32[2,128,1024]{2,1,0:T(8,128)S(1)} collective-permute-done((f32[2,128,1024]{2,1,0:T(8,128)}, f32[2,128,1024]{2,1,0:T(8,128)S(1)}, u32[]{:S(2)}, u32[]{:S(2)}) %collective-permute-start.7) | collective-permute-done | bytes 1048608 | tf_op jit(solution)/shard_map/ppermute | solution.py:311
  311.3 1.0 copy-done
  312.3 1.0 copy-done.1
  313.3 2.6 shard_map.84
  315.9 1.8 collective-permute-start.12
  317.7 4.8 %collective-permute-done.9.refs_3_ = f32[128,1024]{1,0:T(8,128)S(1)} collective-permute-done((f32[128,1024]{1,0:T(8,128)}, f32[128,1024]{1,0:T(8,128)S(1)}, u32[]{:S(2)}, u32[]{:S(2)}) %collective-permute-start.9) | collective-permute-done | bytes 524320 | tf_op jit(solution)/shard_map/ppermute | solution.py:311
  322.5 0.8 copy-done.14
  323.3 0.8 copy-done.15
  324.2 4.6 %shard_map.85.refs_9_ = f32[512,2048]{1,0:T(8,128)} custom-call(s32[4]{0:T(128)} %get-tuple-element.136.refs_0_, f32[2,128,1024]{2,1,0:T(8,128)} %get-tuple-element.88.refs_0_.refs_1_, f32[2,128,1024]{2,1,0:T(8,128)} %copy-done.4, f32[128,1024]{1,0:T(8,128)} %copy-done.14, ...), custom_call_target="tpu_custom_call", output_to_operand_aliasing={{}: (9, {})} | custom-call | bytes 6291456 | tf_op jit(solution)/shard_map/pallas_call | solution.py:279
  328.7 2.6 all-gather.11.cloned.1.call-done
  331.3 24.6 %shard_map.86 = (f32[2,128,768]{2,1,0:T(8,128)}, f32[2,128,768]{2,1,0:T(8,128)}, f32[2,128,768]{2,1,0:T(8,128)}, f32[2,128,768]{2,1,0:T(8,128)}) custom-call(s32[16]{0:T(128)} %get-tuple-element.78.source_ref, s32[4,2]{1,0:T(4,128)} %copy.12.flag_ref, f32[8,128,2048]{2,1,0:T(8,128)} %bitcast.14, f32[8,128,2048]{2,1,0:T(8,128)} %bitcast.15, ...), custom_call_target="tpu_custom_call" | custom-call | flops 19327352832 | bytes 25165824 | tf_op jit(solution)/shard_map/pallas_call | solution.py:220
  356.1 4.4 %collective-permute-start.14 = (f32[2,128,768]{2,1,0:T(8,128)}, f32[2,128,768]{2,1,0:T(8,128)S(1)}, u32[]{:S(2)}, u32[]{:S(2)}) collective-permute-start(f32[2,128,768]{2,1,0:T(8,128)} %get-tuple-element.130), channel_id=1, source_target_pairs={{0,16},{8,24},{16,0},{24,8},{1,17},{9,25},{17,1},{25,9},{2,18},{10... | collective-permute-start | bytes 2359304 | tf_op jit(solution)/shard_map/ppermute | solution.py:311
  360.5 16.1 %shard_map.87 = (f32[2,128,256]{2,1,0:T(8,128)}, f32[2,128,256]{2,1,0:T(8,128)}, f32[2,128,256]{2,1,0:T(8,128)}, f32[2,128,256]{2,1,0:T(8,128)}) custom-call(s32[16]{0:T(128)} %get-tuple-element.78.source_ref, s32[4,2]{1,0:T(4,128)} %copy.12.flag_ref, f32[8,128,2048]{2,1,0:T(8,128)} %bitcast.18, f32[8,128,2048]{2,1,0:T(8,128)} %bitcast.19, ...), custom_call_target="tpu_custom_call" | custom-call | flops 6442450944 | bytes 8388608 | tf_op jit(solution)/shard_map/pallas_call | solution.py:220
  377.0 2.4 collective-permute-start.16
  379.4 2.3 shard_map.88
  381.6 0.8 collective-permute-start.19
  382.5 1.2 collective-permute-start.20
  383.7 4.5 %shard_map.89.refs_9_ = f32[512,2048]{1,0:T(8,128)} custom-call(s32[4]{0:T(128)} %get-tuple-element.136.refs_0_, f32[2,128,1024]{2,1,0:T(8,128)} %get-tuple-element.108.refs_0_.refs_1_, f32[2,128,1024]{2,1,0:T(8,128)} %copy-done, f32[128,1024]{1,0:T(8,128)} %copy-done.10, ...), custom_call_target="tpu_custom_call", output_to_operand_aliasing={{}: (9, {})} | custom-call | bytes 6291456 | tf_op jit(solution)/shard_map/pallas_call | solution.py:279
  388.2 0.7 copy-done.8
  388.9 0.7 copy-done.9
  389.6 1.8 shard_map.90
  391.4 2.0 collective-permute-start.17
  393.4 0.9 collective-permute-done.19.refs_3_
  395.1 0.8 copy-done.17
  395.8 3.8 shard_map.91.refs_9_
  401.0 2.8 shard_map.92
  (73 shorter events, 6.5 us)
Async XLA Ops:
  6.5 160.7 %all-gather.7.cloned.1.call-start = ((), (), s32[]{:S(2)}) async-start(), calls=%async_computation | async-start | bytes 18874368 | tf_op jit(solution)/shard_map/all_gather | solution.py:308
  13.2 6.2 %copy-start.20 = (s32[7]{0:T(128)S(1)}, s32[7]{0:T(128)}, u32[]{:S(2)}) copy-start(s32[7]{0:T(128)} %get-tuple-element.79.take_ref) | copy-start | bytes 88
  13.2 235.9 %all-gather.9.cloned.1.call-start = ((), (), s32[]{:S(2)}) async-start(), calls=%async_computation.1 | async-start | bytes 9437184 | tf_op jit(solution)/shard_map/all_gather | solution.py:308
  16.1 4.4 %collective-permute-start = (f32[128,2048]{1,0:T(8,128)}, f32[128,2048]{1,0:T(8,128)S(1)}, u32[]{:S(2)}, u32[]{:S(2)}) collective-permute-start(f32[128,2048]{1,0:T(8,128)} %shard_map.77), channel_id=1, source_target_pairs={{0,1},{1,0},{2,3},{3,2},{4,5},{5,4},{6,7},{7,6},{8,9},{9,8},{10,11... | collective-permute-start | bytes 3145736 | tf_op jit(solution)/shard_map/ppermute | solution.py:318
  19.4 4.6 %copy-start.21 = (s32[4,2]{0,1:T(2,128)S(1)}, s32[4,2]{0,1:T(2,128)}, u32[]{:S(2)}) copy-start(s32[4,2]{0,1:T(2,128)} %param.10) | copy-start | bytes 100
  23.3 308.1 %all-gather.11.cloned.1.call-start = ((), (), s32[]{:S(2)}) async-start(), calls=%async_computation.2 | async-start | bytes 9437184 | tf_op jit(solution)/shard_map/all_gather | solution.py:308
  200.0 35.0 %collective-permute-start.1 = (f32[2,128,1024]{2,1,0:T(8,128)}, f32[2,128,1024]{2,1,0:T(8,128)S(1)}, u32[]{:S(2)}, u32[]{:S(2)}) collective-permute-start(f32[2,128,1024]{2,1,0:T(8,128)} %get-tuple-element.86), channel_id=1, source_target_pairs={{0,8},{8,0},{16,24},{24,16},{1,9},{9,1},{17,25},{25,17},{2,10},{10... | collective-permute-start | bytes 3145736 | tf_op jit(solution)/shard_map/ppermute | solution.py:311
  200.0 35.0 %collective-permute-start.2 = (f32[2,128,1024]{2,1,0:T(8,128)}, f32[2,128,1024]{2,1,0:T(8,128)S(1)}, u32[]{:S(2)}, u32[]{:S(2)}) collective-permute-start(f32[2,128,1024]{2,1,0:T(8,128)} %get-tuple-element.87), channel_id=1, source_target_pairs={{0,16},{8,24},{16,0},{24,8},{1,17},{9,25},{17,1},{25,9},{2,18},{10... | collective-permute-start | bytes 3145736 | tf_op jit(solution)/shard_map/ppermute | solution.py:311
  235.1 15.6 %copy-start.22 = (f32[2,128,1024]{2,1,0:T(8,128)S(1)}, f32[2,128,1024]{2,1,0:T(8,128)}, u32[]{:S(2)}) copy-start(f32[2,128,1024]{2,1,0:T(8,128)} %get-tuple-element.101) | copy-start | bytes 3145732
  235.1 1.0 copy-start.2
  235.1 1.3 copy-start.3
  239.0 46.6 %collective-permute-start.3 = (f32[128,1024]{1,0:T(8,128)}, f32[128,1024]{1,0:T(8,128)S(1)}, u32[]{:S(2)}, u32[]{:S(2)}) collective-permute-start(f32[128,1024]{1,0:T(8,128)} %get-tuple-element.93), channel_id=1, source_target_pairs={{0,16},{8,24},{16,0},{24,8},{1,17},{9,25},{17,1},{25,9},{2,18},{10... | collective-permute-start | bytes 1572872 | tf_op jit(solution)/shard_map/ppermute | solution.py:311
  239.0 46.6 %collective-permute-start.4 = (f32[128,1024]{1,0:T(8,128)}, f32[128,1024]{1,0:T(8,128)S(1)}, u32[]{:S(2)}, u32[]{:S(2)}) collective-permute-start(f32[128,1024]{1,0:T(8,128)} %get-tuple-element.94), channel_id=1, source_target_pairs={{0,8},{8,0},{16,24},{24,16},{1,9},{9,1},{17,25},{25,17},{2,10},{10... | collective-permute-start | bytes 1572872 | tf_op jit(solution)/shard_map/ppermute | solution.py:311
  249.1 36.5 %collective-permute-start.5 = (f32[2,128,1024]{2,1,0:T(8,128)}, f32[2,128,1024]{2,1,0:T(8,128)S(1)}, u32[]{:S(2)}, u32[]{:S(2)}) collective-permute-start(f32[2,128,1024]{2,1,0:T(8,128)} %get-tuple-element.100), channel_id=1, source_target_pairs={{0,8},{8,0},{16,24},{24,16},{1,9},{9,1},{17,25},{25,17},{2,10},{10... | collective-permute-start | bytes 3145736 | tf_op jit(solution)/shard_map/ppermute | solution.py:311
  250.6 35.0 %collective-permute-start.6 = (f32[2,128,1024]{2,1,0:T(8,128)S(1)}, f32[2,128,1024]{2,1,0:T(8,128)S(1)}, u32[]{:S(2)}, u32[]{:S(2)}) collective-permute-start(f32[2,128,1024]{2,1,0:T(8,128)S(1)} %copy-done.22), channel_id=1, source_target_pairs={{0,16},{8,24},{16,0},{24,8},{1,17},{9,25},{17,1},{25,9},{2,18},{10... | collective-permute-start | bytes 3145736 | tf_op jit(solution)/shard_map/ppermute | solution.py:311
  285.6 1.2 copy-start.12
  285.6 1.3 copy-start.13
  285.6 1.7 copy-start.4
  285.7 1.3 copy-start.5
  286.9 24.4 %collective-permute-start.7 = (f32[2,128,1024]{2,1,0:T(8,128)}, f32[2,128,1024]{2,1,0:T(8,128)S(1)}, u32[]{:S(2)}, u32[]{:S(2)}) collective-permute-start(f32[2,128,1024]{2,1,0:T(8,128)} %get-tuple-element.109), channel_id=1, source_target_pairs={{0,8},{8,0},{16,24},{24,16},{1,9},{9,1},{17,25},{25,17},{2,10},{10... | collective-permute-start | bytes 3145736 | tf_op jit(solution)/shard_map/ppermute | solution.py:311
  286.9 24.4 %collective-permute-start.8 = (f32[2,128,1024]{2,1,0:T(8,128)}, f32[2,128,1024]{2,1,0:T(8,128)S(1)}, u32[]{:S(2)}, u32[]{:S(2)}) collective-permute-start(f32[2,128,1024]{2,1,0:T(8,128)} %get-tuple-element.110), channel_id=1, source_target_pairs={{0,16},{8,24},{16,0},{24,8},{1,17},{9,25},{17,1},{25,9},{2,18},{10... | collective-permute-start | bytes 3145736 | tf_op jit(solution)/shard_map/ppermute | solution.py:311
  289.9 32.6 %collective-permute-start.9 = (f32[128,1024]{1,0:T(8,128)}, f32[128,1024]{1,0:T(8,128)S(1)}, u32[]{:S(2)}, u32[]{:S(2)}) collective-permute-start(f32[128,1024]{1,0:T(8,128)} %get-tuple-element.105), channel_id=1, source_target_pairs={{0,16},{8,24},{16,0},{24,8},{1,17},{9,25},{17,1},{25,9},{2,18},{10... | collective-permute-start | bytes 1572872 | tf_op jit(solution)/shard_map/ppermute | solution.py:311
  291.5 31.0 %collective-permute-start.10 = (f32[128,1024]{1,0:T(8,128)}, f32[128,1024]{1,0:T(8,128)S(1)}, u32[]{:S(2)}, u32[]{:S(2)}) collective-permute-start(f32[128,1024]{1,0:T(8,128)} %get-tuple-element.106), channel_id=1, source_target_pairs={{0,8},{8,0},{16,24},{24,16},{1,9},{9,1},{17,25},{25,17},{2,10},{10... | collective-permute-start | bytes 1572872 | tf_op jit(solution)/shard_map/ppermute | solution.py:311
  311.3 1.0 copy-start
  312.3 1.0 copy-start.1
  315.9 40.0 %collective-permute-start.11 = (f32[128,1024]{1,0:T(8,128)}, f32[128,1024]{1,0:T(8,128)S(1)}, u32[]{:S(2)}, u32[]{:S(2)}) collective-permute-start(f32[128,1024]{1,0:T(8,128)} %get-tuple-element.116), channel_id=1, source_target_pairs={{0,16},{8,24},{16,0},{24,8},{1,17},{9,25},{17,1},{25,9},{2,18},{10... | collective-permute-start | bytes 1572872 | tf_op jit(solution)/shard_map/ppermute | solution.py:311
  315.9 40.0 %collective-permute-start.12 = (f32[128,1024]{1,0:T(8,128)}, f32[128,1024]{1,0:T(8,128)S(1)}, u32[]{:S(2)}, u32[]{:S(2)}) collective-permute-start(f32[128,1024]{1,0:T(8,128)} %get-tuple-element.117), channel_id=1, source_target_pairs={{0,8},{8,0},{16,24},{24,16},{1,9},{9,1},{17,25},{25,17},{2,10},{10... | collective-permute-start | bytes 1572872 | tf_op jit(solution)/shard_map/ppermute | solution.py:311
  322.5 0.8 copy-start.14
  323.3 0.8 copy-start.15
  356.0 20.6 %copy-start.10 = (f32[128,1024]{1,0:T(8,128)}, f32[128,1024]{1,0:T(8,128)S(1)}, u32[]{:S(2)}) copy-start(f32[128,1024]{1,0:T(8,128)S(1)} %collective-permute-done.11.refs_3_) | copy-start | bytes 1572868
  356.0 20.6 %copy-start.11 = (f32[128,1024]{1,0:T(8,128)}, f32[128,1024]{1,0:T(8,128)S(1)}, u32[]{:S(2)}) copy-start(f32[128,1024]{1,0:T(8,128)S(1)} %collective-permute-done.12.refs_6_) | copy-start | bytes 1572868
  356.0 20.6 %collective-permute-start.13 = (f32[2,128,768]{2,1,0:T(8,128)}, f32[2,128,768]{2,1,0:T(8,128)S(1)}, u32[]{:S(2)}, u32[]{:S(2)}) collective-permute-start(f32[2,128,768]{2,1,0:T(8,128)} %get-tuple-element.129), channel_id=1, source_target_pairs={{0,8},{8,0},{16,24},{24,16},{1,9},{9,1},{17,25},{25,17},{2,10},{10... | collective-permute-start | bytes 2359304 | tf_op jit(solution)/shard_map/ppermute | solution.py:311
  356.1 20.9 %collective-permute-start.14 = (f32[2,128,768]{2,1,0:T(8,128)}, f32[2,128,768]{2,1,0:T(8,128)S(1)}, u32[]{:S(2)}, u32[]{:S(2)}) collective-permute-start(f32[2,128,768]{2,1,0:T(8,128)} %get-tuple-element.130), channel_id=1, source_target_pairs={{0,16},{8,24},{16,0},{24,8},{1,17},{9,25},{17,1},{25,9},{2,18},{10... | collective-permute-start | bytes 2359304 | tf_op jit(solution)/shard_map/ppermute | solution.py:311
  376.6 2.8 copy-start.6
  377.0 2.4 copy-start.7
  377.0 11.2 %collective-permute-start.15 = (f32[2,128,256]{2,1,0:T(8,128)}, f32[2,128,256]{2,1,0:T(8,128)S(1)}, u32[]{:S(2)}, u32[]{:S(2)}) collective-permute-start(f32[2,128,256]{2,1,0:T(8,128)} %get-tuple-element.138), channel_id=1, source_target_pairs={{0,8},{8,0},{16,24},{24,16},{1,9},{9,1},{17,25},{25,17},{2,10},{10... | collective-permute-start | bytes 786440 | tf_op jit(solution)/shard_map/ppermute | solution.py:311
  377.0 11.2 %collective-permute-start.16 = (f32[2,128,256]{2,1,0:T(8,128)}, f32[2,128,256]{2,1,0:T(8,128)S(1)}, u32[]{:S(2)}, u32[]{:S(2)}) collective-permute-start(f32[2,128,256]{2,1,0:T(8,128)} %get-tuple-element.139), channel_id=1, source_target_pairs={{0,16},{8,24},{16,0},{24,8},{1,17},{9,25},{17,1},{25,9},{2,18},{10... | collective-permute-start | bytes 786440 | tf_op jit(solution)/shard_map/ppermute | solution.py:311
  381.6 12.7 %collective-permute-start.19 = (f32[128,768]{1,0:T(8,128)}, f32[128,768]{1,0:T(8,128)S(1)}, u32[]{:S(2)}, u32[]{:S(2)}) collective-permute-start(f32[128,768]{1,0:T(8,128)} %get-tuple-element.134), channel_id=1, source_target_pairs={{0,16},{8,24},{16,0},{24,8},{1,17},{9,25},{17,1},{25,9},{2,18},{10... | collective-permute-start | bytes 1179656 | tf_op jit(solution)/shard_map/ppermute | solution.py:311
  382.5 12.1 %collective-permute-start.20 = (f32[128,768]{1,0:T(8,128)}, f32[128,768]{1,0:T(8,128)S(1)}, u32[]{:S(2)}, u32[]{:S(2)}) collective-permute-start(f32[128,768]{1,0:T(8,128)} %get-tuple-element.135), channel_id=1, source_target_pairs={{0,8},{8,0},{16,24},{24,16},{1,9},{9,1},{17,25},{25,17},{2,10},{10... | collective-permute-start | bytes 1179656 | tf_op jit(solution)/shard_map/ppermute | solution.py:311
  388.2 0.7 copy-start.8
  388.9 0.7 copy-start.9
  391.4 8.3 %collective-permute-start.17 = (f32[128,256]{1,0:T(8,128)}, f32[128,256]{1,0:T(8,128)S(1)}, u32[]{:S(2)}, u32[]{:S(2)}) collective-permute-start(f32[128,256]{1,0:T(8,128)} %get-tuple-element.146), channel_id=1, source_target_pairs={{0,16},{8,24},{16,0},{24,8},{1,17},{9,25},{17,1},{25,9},{2,18},{10... | collective-permute-start | bytes 393224 | tf_op jit(solution)/shard_map/ppermute | solution.py:311
  393.4 6.3 %collective-permute-start.18 = (f32[128,256]{1,0:T(8,128)}, f32[128,256]{1,0:T(8,128)S(1)}, u32[]{:S(2)}, u32[]{:S(2)}) collective-permute-start(f32[128,256]{1,0:T(8,128)} %get-tuple-element.147), channel_id=1, source_target_pairs={{0,8},{8,0},{16,24},{24,16},{1,9},{9,1},{17,25},{25,17},{2,10},{10... | collective-permute-start | bytes 393224 | tf_op jit(solution)/shard_map/ppermute | solution.py:311
  394.3 0.8 copy-start.16
  395.1 0.8 copy-start.17
  399.7 0.6 copy-start.18
  400.3 0.7 copy-start.19
Sparse Core Ops, SparseCore 0:
  13.3 153.7 all-gather.6
  168.8 80.2 all-gather.8
  250.7 80.5 all-gather.10

commit v7 on v6

--- a/solution.py
+++ b/solution.py
@@ -161,21 +161,27 @@
     )(integrals)
 
 
-def product_kernel(first, ranks, source_ref, flag_ref, *refs):
-    amp_refs, halves_ref, refs = refs[:ranks], refs[ranks], refs[ranks + 1 :]
-    out_refs, (twice_ref, low_ref, total_ref) = refs[: 2 * CHAINS], refs[2 * CHAINS :]
+def product_kernel(r, first, ranks, source_ref, flag_ref, *refs):
+    amp_ref, halves_ref, refs = refs[0], refs[1], refs[2:]
+    out_refs, (tiles_ref, twice_ref, low_ref, total_ref, ready) = refs[: 2 * CHAINS], refs[2 * CHAINS :]
     width = halves_ref.shape[1]
     step = pl.program_id(0)
 
     @pl.when(step == 0)
     def _():
-        for i, amp_ref in enumerate(amp_refs):
+        shards, _, wide = tiles_ref.shape[1:]
+        copies = []
+        for i in range(ranks):
+            shard = pl.ds(source_ref[r * ranks + i] * shards, shards)
+            copies.append(pltpu.make_async_copy(amp_ref.at[shard], tiles_ref.at[i], ready.at[i]))
+            copies[i].start()
+        for i in range(ranks):
+            copies[i].wait()
             rows = pl.ds(i * TILE_ROWS, TILE_ROWS)
-            shards, _, wide = amp_ref.shape
             for shard in range(shards):
                 for tile in range(wide // TILE):
                     k = shard * (wide // TILE) + tile
-                    value = amp_ref[shard, :, pl.ds(tile * TILE, TILE)]
+                    value = tiles_ref[i, shard, :, pl.ds(tile * TILE, TILE)]
                     high = value.astype(jnp.bfloat16)
                     twice_ref[rows, pl.ds(2 * k * TILE, TILE)] = high
                     twice_ref[rows, pl.ds((2 * k + 1) * TILE, TILE)] = high
@@ -209,33 +215,28 @@
     rows = ranks * TILE_ROWS
     share = COLUMNS // CHAINS
 
-    def amp(peer):
-        return pl.BlockSpec(
-            (shards, TILE_ROWS, depth // shards),
-            lambda i, source, flags: (source[r * ranks + peer], 0, 0),
-            pipeline_mode=pl.Buffered(1),
-        )
-
     integral = pl.BlockSpec((2 * depth, COLUMNS), lambda i, *_: (0, first + i))
     return pl.pallas_call(
-        functools.partial(product_kernel, first, ranks),
+        functools.partial(product_kernel, r, first, ranks),
         out_shape=[jax.ShapeDtypeStruct((2, TILE_ROWS, share * steps), jnp.float32)] * (2 * CHAINS),
         grid_spec=pltpu.PrefetchScalarGridSpec(
             num_scalar_prefetch=2,
             grid=(steps,),
-            in_specs=[amp(peer) for peer in range(ranks)] + [integral],
+            in_specs=[pl.BlockSpec(memory_space=pl.ANY), integral],
             out_specs=[pl.BlockSpec((2, TILE_ROWS, share), lambda i, *_: (0, 0, i))] * (2 * CHAINS),
             scratch_shapes=[
+                pltpu.VMEM((ranks, shards, TILE_ROWS, depth // shards), jnp.float32),
                 pltpu.VMEM((rows, 2 * depth), jnp.bfloat16),
                 pltpu.VMEM((rows, depth), jnp.bfloat16),
                 pltpu.VMEM((rows, COLUMNS), jnp.float32),
+                pltpu.SemaphoreType.DMA((ranks,)),
             ],
         ),
         compiler_params=pltpu.CompilerParams(vmem_limit_bytes=VMEM_BYTES),
         cost_estimate=pl.CostEstimate(
             flops=6 * rows * depth * steps * COLUMNS, bytes_accessed=4 * depth * steps * COLUMNS, transcendentals=0
         ),
-    )(source, int_tiles, *[gathered] * ranks, halves)
+    )(source, int_tiles, gathered, halves)
 
 
 def relay_kernel(*refs):
@@ -270,18 +271,19 @@
 
 
 def finish(r, start, slot, kept, heard, relayed, other_terms, denominators, update):
-    share = kept[0].shape[2]
+    blocks = 2 if start == 0 else 1
+    share = kept[0].shape[2] // blocks
     width = share * CHAINS
-    first = pl.BlockSpec((1, TILE_ROWS, share), lambda i, slot: (0, 0, 0))
-    whole = pl.BlockSpec((TILE_ROWS, share), lambda i, slot: (0, 0))
-    owned = pl.BlockSpec((TILE_ROWS, width), lambda i, slot: (slot[r], start * COLUMNS // width))
+    first = pl.BlockSpec((1, TILE_ROWS, share), lambda i, slot: (0, 0, i))
+    whole = pl.BlockSpec((TILE_ROWS, share), lambda i, slot: (0, i))
+    owned = pl.BlockSpec((TILE_ROWS, width), lambda i, slot: (slot[r], start * COLUMNS // width + i))
     before = [] if update is None else [update]
     return pl.pallas_call(
         functools.partial(finish_kernel, COLUMNS),
         out_shape=jax.ShapeDtypeStruct(other_terms.shape, jnp.float32),
         grid_spec=pltpu.PrefetchScalarGridSpec(
             num_scalar_prefetch=1,
-            grid=(1,),
+            grid=(blocks,),
             in_specs=[first, first, whole] * CHAINS
             + [owned, owned]
             + [pl.BlockSpec(memory_space=pl.ANY)] * len(before),
@@ -343,13 +345,13 @@
 
     rows, onward = tie((gathered[1], onward))
     parts2, relayed0, heard1 = tie((begin(2, rows), relayed0, heard1))
+    onward, relayed1 = pass_on(parts1, heard1)
+    parts2, slot, onward = tie((parts2, slot, onward))
     heard2 = send(parts2)
-    onward, relayed1 = pass_on(parts1, heard1)
-    slot, onward = tie((slot, onward))
     update = finish(0, 0, slot, parts0[0::2], heard0, relayed0, *terms, None)
+    update = finish(1, 0, slot, parts1[0::2], heard1, relayed1, *terms, update)
     heard2, update = tie((heard2, update))
     onward, relayed2 = pass_on(parts2, heard2)
-    update = finish(1, 0, slot, parts1[0::2], heard1, relayed1, *terms, update)
 
     rows, onward, update = tie((gathered[2], onward, update))
     parts3, relayed2 = tie((begin(3, rows, 0, most), relayed2))

time: 414 us -> 422 us (1.019)
  Pallas kernels: 210 us -> 179 us
  starting transfers between devices: 23.3 us -> 48.1 us
  waiting for transfers between devices: 148 us -> 161 us
    pallas_call x5, Pallas kernels: 140 us -> 112 us  [product(): pl.pallas_call(functools.partial(product_kernel, r, first, ranks), out_sh...]
    ppermute x20, starting transfers between devices: 22.7 us -> 47.5 us  [swap(): lax.ppermute(array, 'cd', [(c, c ^ peer) for c in range(ranks)])]
    ppermute x20, waiting for transfers between devices: 19.6 us -> 30.6 us  [swap(): lax.ppermute(array, 'cd', [(c, c ^ peer) for c in range(ranks)])]
    unnamed x47 -> x41, local copies, waits for them, and re-layouts: 11.2 us -> 9.56 us
  transfers between devices with their start and end apart: 24 -> 24, of which waited for: 8 -> 6; matrix products, arithmetic and copies ran while one was open for 1% -> 1% of each run, Pallas kernels for 49% -> 41%
where the time goes in v7:
time: 422 us; the launch traced here: 416 us
  Pallas kernels  179 us (42%)
  waiting for transfers between devices  161 us (38%)
  starting transfers between devices  48.1 us (11%)
  between operations  14.1 us (3%)
  local copies, waits for them, and re-layouts  10.2 us (2%)
    all_gather x3, waiting for transfers between devices, gather(): return lax.all_gather(array, 'ab', axis=0)  129 us
    pallas_call x5, Pallas kernels, product(): pl.pallas_call(functools.partial(product_kernel, r, first, ranks), out_sh...  112 us
    ppermute x20, starting transfers between devices, swap(): lax.ppermute(array, 'cd', [(c, c ^ peer) for c in range(ranks)])  47.5 us
    ppermute x20, waiting for transfers between devices, swap(): lax.ppermute(array, 'cd', [(c, c ^ peer) for c in range(ranks)])  30.6 us
    pallas_call x1, Pallas kernels, split(): pl.pallas_call(split_kernel, out_shape=jax.ShapeDtypeStruct((2 * depth, w...  25.1 us
    pallas_call x5, Pallas kernels, finish(): pl.pallas_call(functools.partial(finish_kernel, COLUMNS), out_shape=jax.S...  19.1 us
    pallas_call x5, Pallas kernels, relay(): pl.pallas_call(relay_kernel, out_shape=[out] * CHAINS, grid=(1,), in_spec...  11.8 us
    pallas_call x3, Pallas kernels, take(): pl.pallas_call(functools.partial(take_kernel, at), out_shape=jax.ShapeDty...  10.1 us
  transfers between devices with their start and end apart: 24, of which 6 were waited for; matrix products, arithmetic and copies ran while one was open for 1% of the time, Pallas kernels for 41%

profile of v7, /device:TPU:0, one launch (start us, length us, event | category | flops | bytes accessed | tf_op | source)
XLA Modules:
  0.0 415.7 jit_solution(7298749739207290718)
XLA Ops:
  7.1 1.6 shard_map.73
  8.7 4.5 %shard_map.76 = f32[128,4096]{1,0:T(8,128)} custom-call(s32[7]{0:T(128)} %get-tuple-element.82.take_ref, s32[2,4]{1,0:T(2,128)} %flag_ref.10, f32[256,4096]{1,0:T(8,128)} %amp_ref.5), custom_call_target="tpu_custom_call" | custom-call | tf_op jit(solution)/shard_map/pallas_call | solution.py:130
  13.3 2.8 shard_map.75
  16.5 2.8 shard_map.74
  20.5 2.7 broadcast_select_fusion
  24.0 25.1 %shard_map.77.refs_1_ = bf16[8192,2048]{1,0:T(8,128)(2,1)} custom-call(f32[4096,2048]{1,0:T(8,128)} %value_ref.1), custom_call_target="tpu_custom_call" | custom-call | bytes 67108864 | tf_op jit(solution)/shard_map/pallas_call | solution.py:153
  49.8 117.4 %all-gather.9.cloned.1.call-done = f32[1024,4096]{1,0:T(8,128)} async-done(((f32[128,4096]{1,0:T(8,128)}), f32[1024,4096]{1,0:T(8,128)}) %all-gather.9.cloned.1.call-update) | async-done | bytes 16777232 | tf_op jit(solution)/shard_map/all_gather | solution.py:310
  167.2 25.7 %shard_map.78 = (f32[2,128,1024]{2,1,0:T(8,128)}, f32[2,128,1024]{2,1,0:T(8,128)}, f32[2,128,1024]{2,1,0:T(8,128)}, f32[2,128,1024]{2,1,0:T(8,128)}) custom-call(s32[16]{0:T(128)} %get-tuple-element.81.source_ref, s32[4,2]{1,0:T(4,128)} %copy.14.flag_ref, f32[8,128,4096]{2,1,0:T(8,128)} %bitcast.8, bf16[8192,2048]{1,0:T(8,128)(2,1)} %shard_map.77.refs_1_), custom_call_target="tpu_custom_call" | custom-call | flops 25769803776 | bytes 33554432 | tf_op jit(solution)/shard_map/pallas_call | solution.py:219
  192.9 4.8 %collective-permute-start.1 = (f32[2,128,1024]{2,1,0:T(8,128)}, f32[2,128,1024]{2,1,0:T(8,128)S(1)}, u32[]{:S(2)}, u32[]{:S(2)}) collective-permute-start(f32[2,128,1024]{2,1,0:T(8,128)} %get-tuple-element.90), channel_id=1, source_target_pairs={{0,8},{8,0},{16,24},{24,16},{1,9},{9,1},{17,25},{25,17},{2,10},{10... | collective-permute-start | bytes 3145736 | tf_op jit(solution)/shard_map/ppermute | solution.py:313
  197.7 3.2 collective-permute-start.2
  200.9 25.6 %shard_map.79 = (f32[2,128,1024]{2,1,0:T(8,128)}, f32[2,128,1024]{2,1,0:T(8,128)}, f32[2,128,1024]{2,1,0:T(8,128)}, f32[2,128,1024]{2,1,0:T(8,128)}) custom-call(s32[16]{0:T(128)} %get-tuple-element.81.source_ref, s32[4,2]{1,0:T(4,128)} %copy.14.flag_ref, f32[8,128,4096]{2,1,0:T(8,128)} %bitcast.9, bf16[8192,2048]{1,0:T(8,128)(2,1)} %shard_map.77.refs_1_), custom_call_target="tpu_custom_call" | custom-call | flops 25769803776 | bytes 33554432 | tf_op jit(solution)/shard_map/pallas_call | solution.py:219
  226.6 0.9 copy-done.2
  227.9 2.5 shard_map.80
  230.5 6.6 %collective-permute-start.3 = (f32[128,1024]{1,0:T(8,128)}, f32[128,1024]{1,0:T(8,128)S(1)}, u32[]{:S(2)}, u32[]{:S(2)}) collective-permute-start(f32[128,1024]{1,0:T(8,128)} %get-tuple-element.95), channel_id=1, source_target_pairs={{0,16},{8,24},{16,0},{24,8},{1,17},{9,25},{17,1},{25,9},{2,18},{10... | collective-permute-start | bytes 1572872 | tf_op jit(solution)/shard_map/ppermute | solution.py:313
  237.1 12.0 %all-gather.7.cloned.1.call-done = f32[1024,2048]{1,0:T(8,128)} async-done(((f32[128,2048]{1,0:T(8,128)}), f32[1024,2048]{1,0:T(8,128)}) %all-gather.7.cloned.1.call-update) | async-done | bytes 8388624 | tf_op jit(solution)/shard_map/all_gather | solution.py:310
  249.1 1.5 collective-permute-start.5
  250.6 1.5 collective-permute-start.6
  252.1 27.1 %shard_map.81 = (f32[2,128,1024]{2,1,0:T(8,128)}, f32[2,128,1024]{2,1,0:T(8,128)}, f32[2,128,1024]{2,1,0:T(8,128)}, f32[2,128,1024]{2,1,0:T(8,128)}) custom-call(s32[16]{0:T(128)} %get-tuple-element.81.source_ref, s32[4,2]{1,0:T(4,128)} %copy.14.flag_ref, f32[8,128,2048]{2,1,0:T(8,128)} %bitcast.10, bf16[8192,2048]{1,0:T(8,128)(2,1)} %shard_map.77.refs_1_), custom_call_target="tpu_custom_call" | custom-call | flops 25769803776 | bytes 33554432 | tf_op jit(solution)/shard_map/pallas_call | solution.py:219
  279.2 1.0 copy-done.4
  280.6 2.7 shard_map.82
  283.2 3.1 collective-permute-start.7
  286.3 3.3 collective-permute-start.8
  289.6 2.0 collective-permute-start.10
  291.7 4.2 %shard_map.83.refs_9_ = f32[512,2048]{1,0:T(8,128)} custom-call(s32[4]{0:T(128)} %get-tuple-element.144.refs_0_, f32[2,128,1024]{2,1,0:T(8,128)} %get-tuple-element.85.refs_0_.refs_1_, f32[2,128,1024]{2,1,0:T(8,128)} %copy-done.2, f32[128,1024]{1,0:T(8,128)} %copy-done.12, f32[2,128,1024]{2,1,0:T(8,128)} %get-tuple-element.93.refs_2_.refs_4_, ...), custom_call_target="tpu_custom_call" | custom-call | bytes 3145728 | tf_op jit(solution)/shard_map/pallas_call | solution.py:281
  295.9 20.1 %collective-permute-done.10.refs_6_ = f32[128,1024]{1,0:T(8,128)} collective-permute-done((f32[128,1024]{1,0:T(8,128)}, f32[128,1024]{1,0:T(8,128)}, u32[]{:S(2)}, u32[]{:S(2)}) %collective-permute-start.10) | collective-permute-done | bytes 524320 | tf_op jit(solution)/shard_map/ppermute | solution.py:313
  315.9 6.4 %collective-permute-done.9.refs_3_ = f32[128,1024]{1,0:T(8,128)} collective-permute-done((f32[128,1024]{1,0:T(8,128)}, f32[128,1024]{1,0:T(8,128)}, u32[]{:S(2)}, u32[]{:S(2)}) %collective-permute-start.9) | collective-permute-done | bytes 524320 | tf_op jit(solution)/shard_map/ppermute | solution.py:313
  322.3 4.2 shard_map.84.refs_9_
  326.5 1.0 copy-done
  327.5 1.0 copy-done.1
  328.4 2.5 shard_map.85
  331.0 2.7 collective-permute-start.11
  333.7 3.6 collective-permute-start.12
  337.4 21.0 %shard_map.86 = (f32[2,128,768]{2,1,0:T(8,128)}, f32[2,128,768]{2,1,0:T(8,128)}, f32[2,128,768]{2,1,0:T(8,128)}, f32[2,128,768]{2,1,0:T(8,128)}) custom-call(s32[16]{0:T(128)} %get-tuple-element.81.source_ref, s32[4,2]{1,0:T(4,128)} %copy.14.flag_ref, f32[8,128,2048]{2,1,0:T(8,128)} %bitcast.6, bf16[8192,2048]{1,0:T(8,128)(2,1)} %shard_map.77.refs_1_), custom_call_target="tpu_custom_call" | custom-call | flops 19327352832 | bytes 25165824 | tf_op jit(solution)/shard_map/pallas_call | solution.py:219
  358.4 3.5 collective-permute-start.13
  361.9 1.7 collective-permute-start.14
  363.6 12.3 %shard_map.87 = (f32[2,128,256]{2,1,0:T(8,128)}, f32[2,128,256]{2,1,0:T(8,128)}, f32[2,128,256]{2,1,0:T(8,128)}, f32[2,128,256]{2,1,0:T(8,128)}) custom-call(s32[16]{0:T(128)} %get-tuple-element.81.source_ref, s32[4,2]{1,0:T(4,128)} %copy.14.flag_ref, f32[8,128,2048]{2,1,0:T(8,128)} %bitcast.7, bf16[8192,2048]{1,0:T(8,128)(2,1)} %shard_map.77.refs_1_), custom_call_target="tpu_custom_call" | custom-call | flops 6442450944 | bytes 8388608 | tf_op jit(solution)/shard_map/pallas_call | solution.py:219
  376.0 2.6 collective-permute-done.14.refs_3_.refs_5_
  378.6 3.5 collective-permute-start.15
  382.1 2.4 collective-permute-start.16
  384.5 2.3 shard_map.88
  387.4 1.0 collective-permute-start.20
  388.3 4.2 shard_map.89.refs_9_
  393.9 1.8 shard_map.90
  395.7 2.0 collective-permute-start.17
  398.2 1.6 collective-permute-done.19.refs_3_
  399.8 0.8 copy-done.14
  401.3 3.7 shard_map.91.refs_9_
  406.3 2.8 shard_map.92
  (67 shorter events, 8.4 us)
Async XLA Ops:
  6.5 160.6 %all-gather.9.cloned.1.call-start = ((), (), s32[]{:S(2)}) async-start(), calls=%async_computation.1 | async-start | bytes 18874368 | tf_op jit(solution)/shard_map/all_gather | solution.py:310
  13.2 6.1 %copy-start.18 = (s32[7]{0:T(128)S(1)}, s32[7]{0:T(128)}, u32[]{:S(2)}) copy-start(s32[7]{0:T(128)} %get-tuple-element.82.take_ref) | copy-start | bytes 88
  13.2 235.9 %all-gather.7.cloned.1.call-start = ((), (), s32[]{:S(2)}) async-start(), calls=%async_computation | async-start | bytes 9437184 | tf_op jit(solution)/shard_map/all_gather | solution.py:310
  16.1 4.4 %collective-permute-start = (f32[128,2048]{1,0:T(8,128)}, f32[128,2048]{1,0:T(8,128)S(1)}, u32[]{:S(2)}, u32[]{:S(2)}) collective-permute-start(f32[128,2048]{1,0:T(8,128)} %shard_map.75), channel_id=1, source_target_pairs={{0,1},{1,0},{2,3},{3,2},{4,5},{5,4},{6,7},{7,6},{8,9},{9,8},{10,11... | collective-permute-start | bytes 3145736 | tf_op jit(solution)/shard_map/ppermute | solution.py:320
  23.3 314.1 %all-gather.11.cloned.1.call-start = ((), (), s32[]{:S(2)}) async-start(), calls=%async_computation.2 | async-start | bytes 9437184 | tf_op jit(solution)/shard_map/all_gather | solution.py:310
  24.0 25.1 %copy-start.19 = (s32[4,2]{0,1:T(2,128)S(1)}, s32[4,2]{0,1:T(2,128)}, u32[]{:S(2)}) copy-start(s32[4,2]{0,1:T(2,128)} %param.10) | copy-start | bytes 100
  192.9 33.7 %collective-permute-start.1 = (f32[2,128,1024]{2,1,0:T(8,128)}, f32[2,128,1024]{2,1,0:T(8,128)S(1)}, u32[]{:S(2)}, u32[]{:S(2)}) collective-permute-start(f32[2,128,1024]{2,1,0:T(8,128)} %get-tuple-element.90), channel_id=1, source_target_pairs={{0,8},{8,0},{16,24},{24,16},{1,9},{9,1},{17,25},{25,17},{2,10},{10... | collective-permute-start | bytes 3145736 | tf_op jit(solution)/shard_map/ppermute | solution.py:313
  197.7 28.9 %collective-permute-start.2 = (f32[2,128,1024]{2,1,0:T(8,128)}, f32[2,128,1024]{2,1,0:T(8,128)S(1)}, u32[]{:S(2)}, u32[]{:S(2)}) collective-permute-start(f32[2,128,1024]{2,1,0:T(8,128)} %get-tuple-element.91), channel_id=1, source_target_pairs={{0,16},{8,24},{16,0},{24,8},{1,17},{9,25},{17,1},{25,9},{2,18},{10... | collective-permute-start | bytes 3145736 | tf_op jit(solution)/shard_map/ppermute | solution.py:313
  226.6 1.0 copy-start.2
  226.6 1.3 copy-start.3
  230.5 48.7 %collective-permute-start.3 = (f32[128,1024]{1,0:T(8,128)}, f32[128,1024]{1,0:T(8,128)S(1)}, u32[]{:S(2)}, u32[]{:S(2)}) collective-permute-start(f32[128,1024]{1,0:T(8,128)} %get-tuple-element.95), channel_id=1, source_target_pairs={{0,16},{8,24},{16,0},{24,8},{1,17},{9,25},{17,1},{25,9},{2,18},{10... | collective-permute-start | bytes 1572872 | tf_op jit(solution)/shard_map/ppermute | solution.py:313
  237.1 42.1 %collective-permute-start.4 = (f32[128,1024]{1,0:T(8,128)}, f32[128,1024]{1,0:T(8,128)S(1)}, u32[]{:S(2)}, u32[]{:S(2)}) collective-permute-start(f32[128,1024]{1,0:T(8,128)} %get-tuple-element.96), channel_id=1, source_target_pairs={{0,8},{8,0},{16,24},{24,16},{1,9},{9,1},{17,25},{25,17},{2,10},{10... | collective-permute-start | bytes 1572872 | tf_op jit(solution)/shard_map/ppermute | solution.py:313
  249.1 30.1 %collective-permute-start.5 = (f32[2,128,1024]{2,1,0:T(8,128)}, f32[2,128,1024]{2,1,0:T(8,128)S(1)}, u32[]{:S(2)}, u32[]{:S(2)}) collective-permute-start(f32[2,128,1024]{2,1,0:T(8,128)} %get-tuple-element.102), channel_id=1, source_target_pairs={{0,8},{8,0},{16,24},{24,16},{1,9},{9,1},{17,25},{25,17},{2,10},{10... | collective-permute-start | bytes 3145736 | tf_op jit(solution)/shard_map/ppermute | solution.py:313
  250.6 28.6 %collective-permute-start.6 = (f32[2,128,1024]{2,1,0:T(8,128)}, f32[2,128,1024]{2,1,0:T(8,128)S(1)}, u32[]{:S(2)}, u32[]{:S(2)}) collective-permute-start(f32[2,128,1024]{2,1,0:T(8,128)} %get-tuple-element.103), channel_id=1, source_target_pairs={{0,16},{8,24},{16,0},{24,8},{1,17},{9,25},{17,1},{25,9},{2,18},{10... | collective-permute-start | bytes 3145736 | tf_op jit(solution)/shard_map/ppermute | solution.py:313
  279.2 12.5 %copy-start.12 = (f32[128,1024]{1,0:T(8,128)}, f32[128,1024]{1,0:T(8,128)S(1)}, u32[]{:S(2)}) copy-start(f32[128,1024]{1,0:T(8,128)S(1)} %collective-permute-done.3.refs_3_) | copy-start | bytes 1572868
  279.2 12.5 %copy-start.13 = (f32[128,1024]{1,0:T(8,128)}, f32[128,1024]{1,0:T(8,128)S(1)}, u32[]{:S(2)}) copy-start(f32[128,1024]{1,0:T(8,128)S(1)} %collective-permute-done.4.refs_6_) | copy-start | bytes 1572868
  279.2 1.1 copy-start.4
  279.2 1.4 copy-start.5
  283.2 43.2 %collective-permute-start.7 = (f32[2,128,1024]{2,1,0:T(8,128)}, f32[2,128,1024]{2,1,0:T(8,128)S(1)}, u32[]{:S(2)}, u32[]{:S(2)}) collective-permute-start(f32[2,128,1024]{2,1,0:T(8,128)} %get-tuple-element.117), channel_id=1, source_target_pairs={{0,8},{8,0},{16,24},{24,16},{1,9},{9,1},{17,25},{25,17},{2,10},{10... | collective-permute-start | bytes 3145736 | tf_op jit(solution)/shard_map/ppermute | solution.py:313
  286.3 40.1 %collective-permute-start.8 = (f32[2,128,1024]{2,1,0:T(8,128)}, f32[2,128,1024]{2,1,0:T(8,128)S(1)}, u32[]{:S(2)}, u32[]{:S(2)}) collective-permute-start(f32[2,128,1024]{2,1,0:T(8,128)} %get-tuple-element.118), channel_id=1, source_target_pairs={{0,16},{8,24},{16,0},{24,8},{1,17},{9,25},{17,1},{25,9},{2,18},{10... | collective-permute-start | bytes 3145736 | tf_op jit(solution)/shard_map/ppermute | solution.py:313
  289.6 26.3 %collective-permute-start.10 = (f32[128,1024]{1,0:T(8,128)}, f32[128,1024]{1,0:T(8,128)}, u32[]{:S(2)}, u32[]{:S(2)}) collective-permute-start(f32[128,1024]{1,0:T(8,128)} %get-tuple-element.114), channel_id=1, source_target_pairs={{0,8},{8,0},{16,24},{24,16},{1,9},{9,1},{17,25},{25,17},{2,10},{10... | collective-permute-start | bytes 1572872 | tf_op jit(solution)/shard_map/ppermute | solution.py:313
  291.6 30.6 %collective-permute-start.9 = (f32[128,1024]{1,0:T(8,128)}, f32[128,1024]{1,0:T(8,128)}, u32[]{:S(2)}, u32[]{:S(2)}) collective-permute-start(f32[128,1024]{1,0:T(8,128)} %get-tuple-element.113), channel_id=1, source_target_pairs={{0,16},{8,24},{16,0},{24,8},{1,17},{9,25},{17,1},{25,9},{2,18},{10... | collective-permute-start | bytes 1572872 | tf_op jit(solution)/shard_map/ppermute | solution.py:313
  326.4 1.0 copy-start
  327.5 1.0 copy-start.1
  331.0 27.4 %collective-permute-start.11 = (f32[128,1024]{1,0:T(8,128)}, f32[128,1024]{1,0:T(8,128)S(1)}, u32[]{:S(2)}, u32[]{:S(2)}) collective-permute-start(f32[128,1024]{1,0:T(8,128)} %get-tuple-element.124), channel_id=1, source_target_pairs={{0,16},{8,24},{16,0},{24,8},{1,17},{9,25},{17,1},{25,9},{2,18},{10... | collective-permute-start | bytes 1572872 | tf_op jit(solution)/shard_map/ppermute | solution.py:313
  333.7 24.7 %collective-permute-start.12 = (f32[128,1024]{1,0:T(8,128)}, f32[128,1024]{1,0:T(8,128)S(1)}, u32[]{:S(2)}, u32[]{:S(2)}) collective-permute-start(f32[128,1024]{1,0:T(8,128)} %get-tuple-element.125), channel_id=1, source_target_pairs={{0,8},{8,0},{16,24},{24,16},{1,9},{9,1},{17,25},{25,17},{2,10},{10... | collective-permute-start | bytes 1572872 | tf_op jit(solution)/shard_map/ppermute | solution.py:313
  358.4 17.6 %copy-start.10 = (f32[128,1024]{1,0:T(8,128)}, f32[128,1024]{1,0:T(8,128)S(1)}, u32[]{:S(2)}) copy-start(f32[128,1024]{1,0:T(8,128)S(1)} %collective-permute-done.11.refs_3_) | copy-start | bytes 1572868
  358.4 17.6 %copy-start.11 = (f32[128,1024]{1,0:T(8,128)}, f32[128,1024]{1,0:T(8,128)S(1)}, u32[]{:S(2)}) copy-start(f32[128,1024]{1,0:T(8,128)S(1)} %collective-permute-done.12.refs_6_) | copy-start | bytes 1572868
  358.4 17.6 %collective-permute-start.13 = (f32[2,128,768]{2,1,0:T(8,128)}, f32[2,128,768]{2,1,0:T(8,128)S(1)}, u32[]{:S(2)}, u32[]{:S(2)}) collective-permute-start(f32[2,128,768]{2,1,0:T(8,128)} %get-tuple-element.137), channel_id=1, source_target_pairs={{0,8},{8,0},{16,24},{24,16},{1,9},{9,1},{17,25},{25,17},{2,10},{10... | collective-permute-start | bytes 2359304 | tf_op jit(solution)/shard_map/ppermute | solution.py:313
  361.9 16.7 %collective-permute-start.14 = (f32[2,128,768]{2,1,0:T(8,128)}, f32[2,128,768]{2,1,0:T(8,128)S(1)}, u32[]{:S(2)}, u32[]{:S(2)}) collective-permute-start(f32[2,128,768]{2,1,0:T(8,128)} %get-tuple-element.138), channel_id=1, source_target_pairs={{0,16},{8,24},{16,0},{24,8},{1,17},{9,25},{17,1},{25,9},{2,18},{10... | collective-permute-start | bytes 2359304 | tf_op jit(solution)/shard_map/ppermute | solution.py:313
  376.0 8.5 %copy-start.6 = (f32[2,128,768]{2,1,0:T(8,128)}, f32[2,128,768]{2,1,0:T(8,128)S(1)}, u32[]{:S(2)}) copy-start(f32[2,128,768]{2,1,0:T(8,128)S(1)} %collective-permute-done.13.refs_1_.refs_2_) | copy-start | bytes 2359300
  378.6 5.9 %copy-start.7 = (f32[2,128,768]{2,1,0:T(8,128)}, f32[2,128,768]{2,1,0:T(8,128)S(1)}, u32[]{:S(2)}) copy-start(f32[2,128,768]{2,1,0:T(8,128)S(1)} %collective-permute-done.14.refs_3_.refs_5_) | copy-start | bytes 2359300
  378.6 13.9 %collective-permute-start.15 = (f32[2,128,256]{2,1,0:T(8,128)}, f32[2,128,256]{2,1,0:T(8,128)S(1)}, u32[]{:S(2)}, u32[]{:S(2)}) collective-permute-start(f32[2,128,256]{2,1,0:T(8,128)} %get-tuple-element.146), channel_id=1, source_target_pairs={{0,8},{8,0},{16,24},{24,16},{1,9},{9,1},{17,25},{25,17},{2,10},{10... | collective-permute-start | bytes 786440 | tf_op jit(solution)/shard_map/ppermute | solution.py:313
  382.1 10.4 %collective-permute-start.16 = (f32[2,128,256]{2,1,0:T(8,128)}, f32[2,128,256]{2,1,0:T(8,128)S(1)}, u32[]{:S(2)}, u32[]{:S(2)}) collective-permute-start(f32[2,128,256]{2,1,0:T(8,128)} %get-tuple-element.147), channel_id=1, source_target_pairs={{0,16},{8,24},{16,0},{24,8},{1,17},{9,25},{17,1},{25,9},{2,18},{10... | collective-permute-start | bytes 786440 | tf_op jit(solution)/shard_map/ppermute | solution.py:313
  386.8 13.0 %collective-permute-start.19 = (f32[128,768]{1,0:T(8,128)}, f32[128,768]{1,0:T(8,128)S(1)}, u32[]{:S(2)}, u32[]{:S(2)}) collective-permute-start(f32[128,768]{1,0:T(8,128)} %get-tuple-element.142), channel_id=1, source_target_pairs={{0,16},{8,24},{16,0},{24,8},{1,17},{9,25},{17,1},{25,9},{2,18},{10... | collective-permute-start | bytes 1179656 | tf_op jit(solution)/shard_map/ppermute | solution.py:313
  387.4 12.4 %collective-permute-start.20 = (f32[128,768]{1,0:T(8,128)}, f32[128,768]{1,0:T(8,128)S(1)}, u32[]{:S(2)}, u32[]{:S(2)}) collective-permute-start(f32[128,768]{1,0:T(8,128)} %get-tuple-element.143), channel_id=1, source_target_pairs={{0,8},{8,0},{16,24},{24,16},{1,9},{9,1},{17,25},{25,17},{2,10},{10... | collective-permute-start | bytes 1179656 | tf_op jit(solution)/shard_map/ppermute | solution.py:313
  392.5 0.7 copy-start.8
  393.2 0.7 copy-start.9
  395.7 9.3 %collective-permute-start.17 = (f32[128,256]{1,0:T(8,128)}, f32[128,256]{1,0:T(8,128)S(1)}, u32[]{:S(2)}, u32[]{:S(2)}) collective-permute-start(f32[128,256]{1,0:T(8,128)} %get-tuple-element.154), channel_id=1, source_target_pairs={{0,16},{8,24},{16,0},{24,8},{1,17},{9,25},{17,1},{25,9},{2,18},{10... | collective-permute-start | bytes 393224 | tf_op jit(solution)/shard_map/ppermute | solution.py:313
  397.7 7.3 %collective-permute-start.18 = (f32[128,256]{1,0:T(8,128)}, f32[128,256]{1,0:T(8,128)S(1)}, u32[]{:S(2)}, u32[]{:S(2)}) collective-permute-start(f32[128,256]{1,0:T(8,128)} %get-tuple-element.155), channel_id=1, source_target_pairs={{0,8},{8,0},{16,24},{24,16},{1,9},{9,1},{17,25},{25,17},{2,10},{10... | collective-permute-start | bytes 393224 | tf_op jit(solution)/shard_map/ppermute | solution.py:313
  399.8 0.8 copy-start.14
  400.5 0.7 copy-start.15
  405.0 0.6 copy-start.16
  405.6 0.7 copy-start.17
Sparse Core Ops, SparseCore 0:
  13.3 153.7 all-gather.8
  168.8 80.2 all-gather.6
  250.7 80.5 all-gather.10
